TPU v7x, 32 devices: a whole 2x2x4 slice. The times are simulated.
32 devices in a mesh: group: 2 (over x), expert: 8 (over z, y), tensor: 2 (over core).
Axes of the slice: x: 2, y: 2, z: 4, core: 2. Of those that a mesh axis runs over, the one named last changes fastest.
Arguments:
- residual: bfloat16 [4, 64, 2880], P(None, ('group', 'expert')), parts along dimension 1, may hold values from -6 to 6
- queries: bfloat16 [4, 64, 2048], P(None, ('group', 'expert'), 'tensor'), parts along dimension 1, may hold values from -40 to 40
- new_kv: bfloat16 [4, 64, 2, 256], P(None, ('group', 'expert'), None, 'tensor'), parts along dimension 1, may hold values from -6 to 6
- cache_kv: bfloat16 [64, 256, 2, 256], P(('group', 'expert'), None, None, 'tensor'), parts along dimension 0, may hold values from -40 to 40
- lengths: int32 [64], P(('group', 'expert')), parts along dimension 0, may hold values from 2 to 256, as said below
- routing: int32 [4, 64, 4], P(None, ('group', 'expert')), parts along dimension 1, may hold values from 0 to 7, all different within a row; in each aligned block of 4 rows (0 to 3, 4 to 7, ..., all dimensions but the last counted through in order) at most 4 rows name the same one
- router: bfloat16 [2880, 8], replicated, may hold values from -0.109375 to 0.109375
- out_proj: bfloat16 [2048, 2880], P('tensor'), may hold values from -0.5 to 0.5
- mantissa: bfloat16 [2, 5760, 3, 2880], P('tensor', 'expert'), may hold values from -6 to 6
- exponent: int32 [2, 5760, 3, 90], P('tensor', 'expert'), may hold values from -8 to -6
- placement: int32 [1920], P('group'), parts along dimension 0, may hold values from 0 to 959, as said below
Outputs:
- layer_out: bfloat16 [4, 64, 2880], P(None, ('group', 'expert')), parts along dimension 1
There are 2 independent parts, one for each index of `group`. A program takes and returns all parts, laid end to end along the dimension named above; an argument that names none is the same for every part. Nothing has to cross between parts.
Inputs may be any that keep to these rules, and one draw needn't show every extreme that they name: placement names each learner tile once; learner tile k lies on learner device k // 120; of one owner's slots j * 120 to (j + 1) * 120 - 1 at most 15 take tiles of one learner device, and some take exactly 15. `routing`: each row names 4 different experts; in each aligned block of 4 rows (one device's rows in one step) no expert is named more than 4 times. `lengths`: some row has length 256.
All inputs are finite; a program needn't handle non-finite values.
Results may differ from a plain program's by a relative error of at most 0.0059.
Values may be sent and summed in bfloat16 or wider, within the bound.
No kernel may reach another device: no remote copies, remote signals or barrier semaphores. Data moves between devices by JAX's collectives and lax.ppermute only.
A program may use at most 192 MiB of HBM per device.

v0:
```python
import math

import jax
import jax.numpy as jnp
from jax import lax
from jax.sharding import PartitionSpec as P

HD = 64
EXPERTS = 8
TOP = 4
BLOCK = 32
TILE_UNITS = 6
CAP = 4


def dequantize(mantissa, exponent):
    full_shape = mantissa.shape
    width = full_shape[-1]
    block_count = exponent.shape[-1]
    scale_power = jnp.exp2(exponent.astype(jnp.float32)).reshape(-1, block_count)
    expander = (jnp.arange(width)[None, :] // BLOCK == jnp.arange(block_count)[:, None]).astype(
        jnp.float32
    )
    scale_full = jnp.dot(scale_power, expander, precision=lax.Precision.HIGHEST).reshape(full_shape)
    return (mantissa.astype(jnp.float32) * scale_full).astype(jnp.bfloat16)


def per_device(
    residual,
    queries,
    new_kv,
    cache_kv,
    lengths,
    routing,
    router,
    out_proj,
    mantissa,
    exponent,
    placement,
):
    axis_count = lax.axis_size("expert")
    my_index = lax.axis_index("expert")
    tensor_count = lax.axis_size("tensor")
    model_width = residual.shape[2]
    tiles_dev = mantissa.shape[1] // TILE_UNITS
    most_tiles = max(2, (tiles_dev + axis_count - 1) // axis_count)
    group_size = axis_count // EXPERTS
    source_dev = (placement // tiles_dev).reshape(axis_count, tiles_dev)
    local_tile = (placement % tiles_dev).reshape(axis_count, tiles_dev)
    mine_mask = (source_dev == my_index).astype(jnp.int32)
    order_rank = jnp.cumsum(mine_mask, axis=1) - 1
    pick_table = mine_mask[:, :, None] * (
        order_rank[:, :, None] == jnp.arange(most_tiles)[None, None, :]
    ).astype(jnp.int32)
    send_index = jnp.sum(pick_table * local_tile[:, :, None], axis=1).reshape(-1)
    own_source = lax.dynamic_index_in_dim(source_dev, my_index, 0, keepdims=False)
    earlier = jnp.arange(tiles_dev)[None, :] < jnp.arange(tiles_dev)[:, None]
    same_source = own_source[None, :] == own_source[:, None]
    own_rank = jnp.sum((earlier & same_source).astype(jnp.int32), axis=1)
    recv_slot = own_source * most_tiles + own_rank
    mant_tiles = mantissa[0].reshape(tiles_dev, TILE_UNITS, 3, model_width)
    expo_tiles = exponent[0].reshape(tiles_dev, TILE_UNITS, 3, exponent.shape[3])
    sent_mant = mant_tiles[send_index].reshape(axis_count, most_tiles, TILE_UNITS, 3, model_width)
    sent_expo = expo_tiles[send_index].reshape(
        axis_count, most_tiles, TILE_UNITS, 3, exponent.shape[3]
    )
    got_mant, got_expo = (
        lax.all_to_all(sent_mant, "expert", split_axis=0, concat_axis=0, tiled=True),
        lax.all_to_all(sent_expo, "expert", split_axis=0, concat_axis=0, tiled=True),
    )
    got_mant = got_mant.reshape(axis_count * most_tiles, TILE_UNITS, 3, model_width)[recv_slot]
    got_expo = got_expo.reshape(axis_count * most_tiles, TILE_UNITS, 3, exponent.shape[3])[
        recv_slot
    ]
    weights = dequantize(got_mant, got_expo).reshape(-1, 3, model_width)
    weights = lax.all_gather(weights, "tensor", axis=0, tiled=True)
    slot_width = CAP // tensor_count
    slot_first = lax.axis_index("tensor") * slot_width
    row_count = residual.shape[1]
    cache_len = cache_kv.shape[1]
    kv_heads = new_kv.shape[3] // HD
    per_group = queries.shape[2] // HD // kv_heads
    scale_factor = 1.0 / math.sqrt(HD)
    cache_keys = cache_kv[:, :, 0].reshape(row_count, cache_len, kv_heads, HD)
    cache_values = cache_kv[:, :, 1].reshape(row_count, cache_len, kv_heads, HD)
    alive = jnp.arange(cache_len)[None, :] < lengths[:, None]
    pair_count = row_count * TOP
    slot_window = slot_first + jnp.arange(slot_width)
    outputs = []
    for step_index in range(residual.shape[0]):
        queries_now = queries[step_index].reshape(row_count, kv_heads, per_group, HD)
        fresh_keys = new_kv[: step_index + 1, :, 0].reshape(step_index + 1, row_count, kv_heads, HD)
        fresh_values = new_kv[: step_index + 1, :, 1].reshape(
            step_index + 1, row_count, kv_heads, HD
        )
        cache_scores = (
            jnp.einsum(
                "tgqd,tlgd->tgql", queries_now, cache_keys, preferred_element_type=jnp.float32
            )
            * scale_factor
        )
        cache_scores = jnp.where(alive[:, None, None, :], cache_scores, -1e30)
        fresh_scores = (
            jnp.einsum(
                "tgqd,stgd->tgqs", queries_now, fresh_keys, preferred_element_type=jnp.float32
            )
            * scale_factor
        )
        highest = jnp.maximum(
            jnp.max(cache_scores, axis=-1, keepdims=True),
            jnp.max(fresh_scores, axis=-1, keepdims=True),
        )
        cache_exp = jnp.exp(cache_scores - highest)
        fresh_exp = jnp.exp(fresh_scores - highest)
        denominator = jnp.sum(cache_exp, axis=-1, keepdims=True) + jnp.sum(
            fresh_exp, axis=-1, keepdims=True
        )
        cache_prob = (cache_exp / denominator).astype(jnp.bfloat16)
        fresh_prob = (fresh_exp / denominator).astype(jnp.bfloat16)
        heads_out = jnp.einsum(
            "tgql,tlgd->tgqd", cache_prob, cache_values, preferred_element_type=jnp.float32
        )
        heads_out = heads_out + jnp.einsum(
            "tgqs,stgd->tgqd", fresh_prob, fresh_values, preferred_element_type=jnp.float32
        )
        heads_out = heads_out.astype(jnp.bfloat16).reshape(row_count, -1)
        projected = jnp.dot(heads_out, out_proj, preferred_element_type=jnp.float32)
        mixed = residual[step_index].astype(jnp.float32) + lax.psum(projected, "tensor")
        normed = (
            mixed * lax.rsqrt(jnp.mean(mixed * mixed, axis=-1, keepdims=True) + 1e-05)
        ).astype(jnp.bfloat16)
        logits = jnp.dot(normed, router, preferred_element_type=jnp.float32)
        chosen = jnp.take_along_axis(logits, routing[step_index], axis=1)
        sigmoids = jax.nn.sigmoid(chosen)
        gate_values = sigmoids / jnp.sum(sigmoids, axis=-1, keepdims=True)
        pair_expert = routing[step_index].reshape(pair_count)
        member = (pair_expert[:, None] == jnp.arange(EXPERTS)[None, :]).astype(jnp.int32)
        position = jnp.sum((jnp.cumsum(member, axis=0) - 1) * member, axis=1)
        select = member.T[:, None, :] * (
            position[None, None, :] == slot_window[None, :, None]
        ).astype(jnp.int32)
        spread = jnp.repeat(normed, TOP, axis=0)
        packed = jnp.einsum(
            "ecp,pd->ecd", select.astype(jnp.bfloat16), spread, preferred_element_type=jnp.float32
        ).astype(jnp.bfloat16)
        outgoing = jnp.repeat(packed, group_size, axis=0)
        received = lax.all_to_all(outgoing, "expert", split_axis=0, concat_axis=0, tiled=True)
        flat_rows = received.reshape(-1, received.shape[2])
        gate_part = jnp.einsum(
            "rd,ud->ru", flat_rows, weights[:, 0, :], preferred_element_type=jnp.float32
        )
        up_part = jnp.einsum(
            "rd,ud->ru", flat_rows, weights[:, 1, :], preferred_element_type=jnp.float32
        )
        hidden = (jax.nn.silu(gate_part) * up_part).astype(jnp.bfloat16)
        partial_value = jnp.einsum(
            "ru,ud->rd", hidden, weights[:, 2, :], preferred_element_type=jnp.float32
        )
        returned = lax.all_to_all(
            partial_value.reshape(received.shape), "expert", split_axis=0, concat_axis=0, tiled=True
        )
        summed = returned.reshape(EXPERTS, group_size, slot_width, model_width).sum(axis=1)
        per_pair = jnp.einsum(
            "ecp,ecd->pd", select.astype(jnp.float32), summed, precision=lax.Precision.HIGHEST
        )
        moe_part = jnp.sum(
            per_pair.reshape(row_count, TOP, model_width) * gate_values[:, :, None], axis=1
        )
        mixed = mixed + lax.psum(moe_part, "tensor")
        outputs.append(mixed.astype(jnp.bfloat16))
    return jnp.stack(outputs)


def solution(mesh):
    placed = (
        P(None, ("group", "expert"), None),
        P(None, ("group", "expert"), "tensor"),
        P(None, ("group", "expert"), None, "tensor"),
        P(("group", "expert"), None, None, "tensor"),
        P(("group", "expert")),
        P(None, ("group", "expert"), None),
        P(),
        P("tensor", None),
        P("tensor", "expert", None, None),
        P("tensor", "expert", None, None),
        P("group"),
    )
    return jax.shard_map(
        per_device,
        mesh=mesh,
        in_specs=placed,
        out_specs=P(None, ("group", "expert"), None),
        check_vma=False,
    )
```

profile of v0, /device:TPU:0, one launch (start us, length us, event | category | flops | bytes accessed | tf_op | source)
XLA Modules:
  0.0 614.5 jit_solution(18245593761651264930)
XLA Ops:
  12.8 7.3 %all-to-all-start.2 = ((s32[8,15,6,3,90]{4,1,3,2,0:T(8,128)}), s32[8,15,6,3,90]{4,1,3,2,0:T(8,128)S(1)}, u32[]{:S(2)}, u32[]{:S(2)}) async-start(s32[8,15,6,3,90]{4,1,3,2,0:T(8,128)} %copy.114), calls=%async_computation.2 | async-start | bytes 2359296 | tf_op jit(solution)/shard_map/all_to_all | solution.py:69
  20.1 20.5 %reshape_squeeze.47 = bf16[120,6,3,2880]{3,1,0,2:T(8,128)(2,1)} reshape(bf16[1,720,3,2880]{3,1,2,0:T(8,128)(2,1)} %param.21) | data formatting | bytes 24883200 | tf_op jit(solution)/shard_map/reshape;squeeze | solution.py:61
  40.6 14.4 %gather_fusion = bf16[120,6,3,2880]{3,1,2,0:T(8,128)(2,1)} fusion(bf16[120,6,3,2880]{3,1,0,2:T(8,128)(2,1)} %reshape_squeeze.47, s32[1024]{0:T(1024)S(1)} %pad_clamp_fusion.1), kind=kCustom, calls=%fused_computation.4 | custom fusion | bytes 24883680 | tf_op jit(solution)/shard_map/gather | solution.py:63
  55.0 12.9 %copy.108 = bf16[8,15,6,3,2880]{4,1,3,2,0:T(8,128)(2,1)} copy(bf16[8,15,6,3,2880]{4,2,3,1,0:T(8,128)(2,1)} %bitcast.245) | data formatting | bytes 24883200 | tf_op jit(solution)/shard_map/reshape | solution.py:63
  67.9 6.1 all-to-all-start.1
  98.0 269.6 %all-to-all-done.1 = bf16[8,15,6,3,2880]{4,1,3,2,0:T(8,128)(2,1)} async-done(((bf16[8,15,6,3,2880]{4,1,3,2,0:T(8,128)(2,1)}), bf16[8,15,6,3,2880]{4,1,3,2,0:T(8,128)(2,1)}, u32[]{:S(2)}, u32[]{:S(2)}) %all-to-all-start.1) | async-done | bytes 12441632 | tf_op jit(solution)/shard_map/all_to_all | solution.py:68
  367.6 15.3 %copy.109 = bf16[8,15,6,3,2880]{4,2,3,1,0:T(8,128)(2,1)} copy(bf16[8,15,6,3,2880]{4,1,3,2,0:T(8,128)(2,1)} %all-to-all-done.1) | data formatting | bytes 24883200 | tf_op jit(solution)/shard_map/all_to_all | solution.py:68
  382.9 14.3 %gather_fusion.1 = bf16[120,6,3,2880]{3,1,2,0:T(8,128)(2,1)} fusion(bf16[120,6,3,2880]{3,1,2,0:T(8,128)(2,1)} %bitcast.246, s32[1024]{0:T(1024)S(1)} %pad_clamp_fusion), kind=kCustom, calls=%fused_computation.5 | custom fusion | bytes 24883680 | tf_op jit(solution)/shard_map/gather | solution.py:71
  397.3 15.6 %multiply_convert_fusion = bf16[120,6,3,2880]{3,0,2,1:T(8,128)(2,1)S(1)} fusion(bf16[120,6,3,2880]{3,1,2,0:T(8,128)(2,1)} %gather_fusion.1, s32[120,6,3,90]{0,3,2,1:T(8,128)S(1)} %copy.117, s32[2880]{0:T(1024)S(1)} %add_select_fusion), kind=kOutput, calls=%fused_computation.8 | convolution fusion | flops 6737774592 | bytes 25672320 | tf_op jit(solution)/shard_map/dot_general | solution.py:24
  412.8 6.8 %copy.118 = bf16[120,6,3,2880]{3,1,0,2:T(8,128)(2,1)} copy(bf16[120,6,3,2880]{3,0,2,1:T(8,128)(2,1)S(1)} %multiply_convert_fusion) | data formatting | bytes 24883200 | tf_op jit(solution)/shard_map/convert_element_type | solution.py:25
  419.6 21.0 %reshape.643 = bf16[720,3,2880]{2,0,1:T(8,128)(2,1)} reshape(bf16[120,6,3,2880]{3,1,0,2:T(8,128)(2,1)} %copy.118) | data formatting | bytes 24883200 | tf_op jit(solution)/shard_map/reshape | solution.py:75
  463.0 7.0 %all-to-all-done.6 = bf16[8,2,2880]{2,1,0:T(2,128)(2,1)S(1)} async-done(((bf16[8,2,2880]{2,1,0:T(2,128)(2,1)}), bf16[8,2,2880]{2,1,0:T(2,128)(2,1)S(1)}, u32[]{:S(2)}, u32[]{:S(2)}) %all-to-all-start.6) | async-done | bytes 92192 | tf_op jit(solution)/shard_map/all_to_all | solution.py:147
  473.4 7.0 %all-to-all-done.4 = bf16[8,2,2880]{2,1,0:T(2,128)(2,1)S(1)} async-done(((bf16[8,2,2880]{2,1,0:T(2,128)(2,1)}), bf16[8,2,2880]{2,1,0:T(2,128)(2,1)S(1)}, u32[]{:S(2)}, u32[]{:S(2)}) %all-to-all-start.4) | async-done | bytes 92192 | tf_op jit(solution)/shard_map/all_to_all | solution.py:147
  484.3 6.7 %all-to-all-done = bf16[8,2,2880]{2,1,0:T(2,128)(2,1)S(1)} async-done(((bf16[8,2,2880]{2,1,0:T(2,128)(2,1)}), bf16[8,2,2880]{2,1,0:T(2,128)(2,1)S(1)}, u32[]{:S(2)}, u32[]{:S(2)}) %all-to-all-start) | async-done | bytes 92192 | tf_op jit(solution)/shard_map/all_to_all | solution.py:147
  491.1 5.7 fusion
  496.8 5.7 fusion.20
  511.4 5.7 fusion.1
  517.1 5.7 fusion.21
  528.3 5.7 fusion.2
  534.0 5.7 fusion.22
  545.2 5.7 fusion.3
  550.9 6.2 %all-to-all-start.7 = ((f32[8,2,2880]{2,1,0:T(2,128)}), f32[8,2,2880]{2,1,0:T(2,128)S(1)}, u32[]{:S(2)}, u32[]{:S(2)}) async-start(f32[8,2,2880]{2,1,0:T(2,128)} %copy.132), calls=%async_computation.7 | async-start | bytes 376832 | tf_op jit(solution)/shard_map/all_to_all | solution.py:159
  557.2 5.8 fusion.23
  589.4 16.4 %all-reduce.5.cloned.1.call-done = (f32[4,2880]{1,0:T(4,128)}, f32[4,2880]{1,0:T(4,128)}, f32[4,2880]{1,0:T(4,128)}, f32[4,2880]{1,0:T(4,128)}) async-done(((f32[4,2880]{1,0:T(4,128)}, f32[4,2880]{1,0:T(4,128)}, f32[4,2880]{1,0:T(4,128)}, f32[4,2880]{1,0:T(4,128)}), (f32[4,2880]{1,0:T(4,128)}, f32[4,2880]{1,0:T(4,128)}, f32[4,2880]{1,0:T(4,128)}, f32[4,2880]{1,0:T(4,128)})) %all-reduce.5.cloned.1.call-update) | async-done | bytes 184336 | tf_op jit(solution)/shard_map/psum | solution.py:169
  (224 shorter events, 107.5 us)
Async XLA Ops:
  6.5 443.6 %copy-start = (bf16[2880,8]{0,1:T(8,128)(2,1)S(1)}, bf16[2880,8]{0,1:T(8,128)(2,1)}, u32[]{:S(2)}) copy-start(bf16[2880,8]{0,1:T(8,128)(2,1)} %param.19) | copy-start | bytes 138244
  12.8 55.2 %all-to-all-start.2 = ((s32[8,15,6,3,90]{4,1,3,2,0:T(8,128)}), s32[8,15,6,3,90]{4,1,3,2,0:T(8,128)S(1)}, u32[]{:S(2)}, u32[]{:S(2)}) async-start(s32[8,15,6,3,90]{4,1,3,2,0:T(8,128)} %copy.114), calls=%async_computation.2 | async-start | bytes 2359296 | tf_op jit(solution)/shard_map/all_to_all | solution.py:69
  67.9 6.2 %copy-start.1 = (bf16[4,256,2,128]{3,2,1,0:T(2,128)(2,1)S(1)}, bf16[4,256,2,128]{3,2,1,0:T(2,128)(2,1)}, u32[]{:S(2)}) copy-start(bf16[4,256,2,128]{3,2,1,0:T(2,128)(2,1)} %param.16) | copy-start | bytes 1572868
  67.9 7.3 %copy-start.9 = (bf16[4,4,1024]{2,1,0:T(4,128)(2,1)S(1)}, bf16[4,4,1024]{2,1,0:T(4,128)(2,1)}, u32[]{:S(2)}) copy-start(bf16[4,4,1024]{2,1,0:T(4,128)(2,1)} %param.14) | copy-start | bytes 98308
  67.9 7.8 %copy-start.7 = (bf16[4,4,2,128]{3,2,1,0:T(2,128)(2,1)S(1)}, bf16[4,4,2,128]{3,2,1,0:T(2,128)(2,1)}, u32[]{:S(2)}) copy-start(bf16[4,4,2,128]{3,2,1,0:T(2,128)(2,1)} %param.15) | copy-start | bytes 24580
  67.9 8.0 %copy-start.10 = (s32[4]{0:T(128)S(1)}, s32[4]{0:T(128)}, u32[]{:S(2)}) copy-start(s32[4]{0:T(128)} %param.17) | copy-start | bytes 52
  67.9 299.7 %all-to-all-start.1 = ((bf16[8,15,6,3,2880]{4,1,3,2,0:T(8,128)(2,1)}), bf16[8,15,6,3,2880]{4,1,3,2,0:T(8,128)(2,1)}, u32[]{:S(2)}, u32[]{:S(2)}) async-start(bf16[8,15,6,3,2880]{4,1,3,2,0:T(8,128)(2,1)} %copy.108), calls=%async_computation.1 | async-start | bytes 27131904 | tf_op jit(solution)/shard_map/all_to_all | solution.py:68
  74.1 369.4 %all-reduce.7.cloned.1.call-start = ((), (), s32[]{:S(2)}) async-start(), calls=%async_computation.12 | async-start | bytes 376832 | tf_op jit(solution)/shard_map/psum | solution.py:128
  76.1 15.2 %slice-start = ((s8[5898240]{0:T(1024)(128)(4,1)}), s8[1703936]{0:T(1024)(128)(4,1)S(1)}, s32[]{:S(2)}) async-start(s8[5898240]{0:T(1024)(128)(4,1)} %bitcast.243), calls=%async_computation.13 | async-start | bytes 3407872
  81.3 10.1 %slice-start.1 = ((s8[5898240]{0:T(1024)(128)(4,1)}), s8[4194304]{0:T(1024)(128)(4,1)S(1)}, s32[]{:S(2)}) async-start(s8[5898240]{0:T(1024)(128)(4,1)} %bitcast.243), calls=%async_computation.14 | async-start | bytes 8388608
  95.9 395.2 %all-gather.2.cloned.1.call-start = ((), (), s32[]{:S(2)}) async-start(), calls=%async_computation.10 | async-start | bytes 38154240 | tf_op jit(solution)/shard_map/all_gather | solution.py:76
  446.5 10.7 %all-to-all-start.8 = ((bf16[8,2,2880]{2,1,0:T(2,128)(2,1)}), bf16[8,2,2880]{2,1,0:T(2,128)(2,1)S(1)}, u32[]{:S(2)}, u32[]{:S(2)}) async-start(bf16[8,2,2880]{2,1,0:T(2,128)(2,1)} %copy.136), calls=%async_computation.8 | async-start | bytes 188416 | tf_op jit(solution)/shard_map/all_to_all | solution.py:147
  457.2 12.8 %all-to-all-start.6 = ((bf16[8,2,2880]{2,1,0:T(2,128)(2,1)}), bf16[8,2,2880]{2,1,0:T(2,128)(2,1)S(1)}, u32[]{:S(2)}, u32[]{:S(2)}) async-start(bf16[8,2,2880]{2,1,0:T(2,128)(2,1)} %copy.130), calls=%async_computation.6 | async-start | bytes 188416 | tf_op jit(solution)/shard_map/all_to_all | solution.py:147
  470.0 10.4 %all-to-all-start.4 = ((bf16[8,2,2880]{2,1,0:T(2,128)(2,1)}), bf16[8,2,2880]{2,1,0:T(2,128)(2,1)S(1)}, u32[]{:S(2)}, u32[]{:S(2)}) async-start(bf16[8,2,2880]{2,1,0:T(2,128)(2,1)} %copy.124), calls=%async_computation.4 | async-start | bytes 188416 | tf_op jit(solution)/shard_map/all_to_all | solution.py:147
  480.4 10.6 %all-to-all-start = ((bf16[8,2,2880]{2,1,0:T(2,128)(2,1)}), bf16[8,2,2880]{2,1,0:T(2,128)(2,1)S(1)}, u32[]{:S(2)}, u32[]{:S(2)}) async-start(bf16[8,2,2880]{2,1,0:T(2,128)(2,1)} %copy.106), calls=%async_computation | async-start | bytes 188416 | tf_op jit(solution)/shard_map/all_to_all | solution.py:147
  508.0 42.9 %all-to-all-start.9 = ((f32[8,2,2880]{2,1,0:T(2,128)}), f32[8,2,2880]{2,1,0:T(2,128)S(1)}, u32[]{:S(2)}, u32[]{:S(2)}) async-start(f32[8,2,2880]{2,1,0:T(2,128)} %copy.138), calls=%async_computation.9 | async-start | bytes 376832 | tf_op jit(solution)/shard_map/all_to_all | solution.py:159
  550.9 13.9 %all-to-all-start.7 = ((f32[8,2,2880]{2,1,0:T(2,128)}), f32[8,2,2880]{2,1,0:T(2,128)S(1)}, u32[]{:S(2)}, u32[]{:S(2)}) async-start(f32[8,2,2880]{2,1,0:T(2,128)} %copy.132), calls=%async_computation.7 | async-start | bytes 376832 | tf_op jit(solution)/shard_map/all_to_all | solution.py:159
  557.1 48.7 %copy-start.3 = (f32[4,2880]{1,0:T(4,128)S(1)}, f32[4,2880]{1,0:T(4,128)}, u32[]{:S(2)}) copy-start(f32[4,2880]{1,0:T(4,128)} %get-tuple-element.20) | copy-start | bytes 138244
  557.1 48.7 %copy-start.4 = (f32[4,2880]{1,0:T(4,128)S(1)}, f32[4,2880]{1,0:T(4,128)}, u32[]{:S(2)}) copy-start(f32[4,2880]{1,0:T(4,128)} %get-tuple-element.21) | copy-start | bytes 138244
  557.1 48.7 %copy-start.5 = (f32[4,2880]{1,0:T(4,128)S(1)}, f32[4,2880]{1,0:T(4,128)}, u32[]{:S(2)}) copy-start(f32[4,2880]{1,0:T(4,128)} %get-tuple-element.22) | copy-start | bytes 138244
  557.1 48.7 %copy-start.6 = (f32[4,2880]{1,0:T(4,128)S(1)}, f32[4,2880]{1,0:T(4,128)}, u32[]{:S(2)}) copy-start(f32[4,2880]{1,0:T(4,128)} %get-tuple-element.23) | copy-start | bytes 138244
  564.8 11.9 %all-to-all-start.5 = ((f32[8,2,2880]{2,1,0:T(2,128)}), f32[8,2,2880]{2,1,0:T(2,128)S(1)}, u32[]{:S(2)}, u32[]{:S(2)}) async-start(f32[8,2,2880]{2,1,0:T(2,128)} %copy.126), calls=%async_computation.5 | async-start | bytes 376832 | tf_op jit(solution)/shard_map/all_to_all | solution.py:159
  576.7 11.4 %all-to-all-start.3 = ((f32[8,2,2880]{2,1,0:T(2,128)}), f32[8,2,2880]{2,1,0:T(2,128)S(1)}, u32[]{:S(2)}, u32[]{:S(2)}) async-start(f32[8,2,2880]{2,1,0:T(2,128)} %copy.120), calls=%async_computation.3 | async-start | bytes 376832 | tf_op jit(solution)/shard_map/all_to_all | solution.py:159
  580.4 25.4 %all-reduce.5.cloned.1.call-start = ((), (), s32[]{:S(2)}) async-start(), calls=%async_computation.11 | async-start | bytes 376832 | tf_op jit(solution)/shard_map/psum | solution.py:169
  (2 other events, 3.6 us)
Sparse Core Ops, SparseCore 0:
  96.1 19.5 all-reduce.6
  440.7 43.7 all-gather.1
  589.6 16.2 all-reduce.4
where the time goes:
time: 625 us; the launch traced here: 614 us
  waiting for transfers between devices  315 us (50%)
  local copies, waits for them, and re-layouts  126 us (20%)
  matrix products  104 us (17%)
  starting transfers between devices  47.4 us (8%)
  between operations  14.1 us (2%)
  other arithmetic  7.84 us (1%)
    all_to_all x1, waiting for transfers between devices, per_device(): lax.all_to_all(sent_mant, 'expert', split_axis=0, concat_axis=0, tiled=True)  270 us
    dot_general x4, matrix products, per_device(): jnp.einsum('rd,ud->ru', flat_rows, weights[:, 1, :], preferred_element_ty...  23 us
    dot_general x4, matrix products, per_device(): jnp.einsum('rd,ud->ru', flat_rows, weights[:, 0, :], preferred_element_ty...  22.8 us
    all_to_all x4, waiting for transfers between devices, per_device(): lax.all_to_all(outgoing, 'expert', split_axis=0, concat_axis=0, tiled=True)  21 us
    reshape x1, local copies, waits for them, and re-layouts, per_device(): weights = dequantize(got_mant, got_expo).reshape(-1, 3, model_width)  21 us
    another operation x1, local copies, waits for them, and re-layouts, per_device(): mant_tiles = mantissa[0].reshape(tiles_dev, TILE_UNITS, 3, model_width)  20.5 us
    dot_general x4, matrix products, per_device(): jnp.einsum('ru,ud->rd', hidden, weights[:, 2, :], preferred_element_type=...  18.5 us
    all_to_all x4, starting transfers between devices, per_device(): lax.all_to_all(partial_value.reshape(received.shape), 'expert', split_axi...  17.5 us
  transfers between devices with their start and end apart: 13, of which 9 were waited for; matrix products, arithmetic and copies ran while one was open for 34% of the time, Pallas kernels for 0%

commit v1 on v0

v1 whole, which is shorter than its diff:
```python
import functools

import jax
import jax.numpy as jnp
from jax import lax
from jax.experimental import pallas as pl
from jax.experimental.pallas import tpu as pltpu
from jax.sharding import PartitionSpec as P

HD = 64
EXPERTS = 8
TOP = 4
BLOCK = 32
TILE_UNITS = 6
LANES = 128
F32 = jnp.float32
BF16 = jnp.bfloat16
VMEM_LIMIT = 56 * 1024 * 1024

NT = (((1,), (1,)), ((), ()))
TN = (((0,), (0,)), ((), ()))


def dot(a, b, dims=(((1,), (0,)), ((), ()))):
    return lax.dot_general(a, b, dims, preferred_element_type=F32)


def iota(shape, dim):
    return lax.broadcasted_iota(jnp.int32, shape, dim)


def attention_kernel(
    steps, rows, lengths_ref, queries_ref, fresh_ref, cache_ref, proj_hbm, out_ref, packed, mixed, proj, sem
):
    copy = pltpu.make_async_copy(proj_hbm, proj, sem)
    copy.start()
    count = steps * rows
    groups = queries_ref.shape[1] // LANES
    half = groups // 2
    lane = iota((count, LANES), 1)
    for group in range(groups):
        piece = queries_ref[:, group * LANES : (group + 1) * LANES].astype(F32) * (HD**-0.5)
        mine = (lane < HD) == (group < half)
        packed[group * count : (group + 1) * count, :] = jnp.where(mine, piece, 0.0)
        packed[(groups + group) * count : (groups + group + 1) * count, :] = jnp.where(
            mine, pltpu.roll(piece, HD, 1), 0.0
        )
    amount = 2 * groups * steps
    span = cache_ref.shape[1]
    fresh = fresh_ref[...]
    width = fresh.shape[0]
    spot = iota((amount, span), 1)
    step_of = iota((amount, width), 0) % steps
    fresh_spot = iota((amount, width), 1)
    fresh_step = fresh_spot // (2 * rows)
    for row in range(rows):
        now = packed[pl.ds(row, amount, stride=rows), :].astype(BF16)
        cache = cache_ref[row]
        scores = dot(now, cache, NT)
        live = (spot % 2 == 0) & (spot < 2 * lengths_ref[row])
        scores = jnp.where(live, scores, -1e30)
        late = dot(now, fresh, NT)
        seen = (fresh_spot % (2 * rows) == 2 * row) & (fresh_step <= step_of)
        late = jnp.where(seen, late, -1e30)
        highest = jnp.maximum(
            jnp.max(scores, axis=1, keepdims=True), jnp.max(late, axis=1, keepdims=True)
        )
        scores = jnp.exp(scores - highest)
        late = jnp.exp(late - highest)
        total = jnp.sum(scores, axis=1, keepdims=True) + jnp.sum(late, axis=1, keepdims=True)
        probs = pltpu.roll(scores / total, 1, 1).astype(BF16)
        late_probs = pltpu.roll(late / total, 1, 1).astype(BF16)
        mixed[pl.ds(row, amount, stride=rows), :] = dot(probs, cache) + dot(late_probs, fresh)
    heads = []
    for group in range(groups):
        straight = mixed[group * count : (group + 1) * count, :]
        turned = mixed[(groups + group) * count : (groups + group + 1) * count, :]
        mine = (lane < HD) == (group < half)
        heads.append(jnp.where(mine, straight, pltpu.roll(turned, HD, 1)).astype(BF16))
    copy.wait()
    out_ref[...] = dot(jnp.concatenate(heads, axis=1), proj[...], NT)


def attend(lengths, queries, new_kv, cache_kv, out_proj):
    steps, rows, width = queries.shape
    span = cache_kv.shape[1]
    proj = out_proj.T
    model_width = proj.shape[0]
    count = steps * rows
    groups = width // LANES
    fresh = new_kv.reshape(steps * rows * 2, LANES)
    fresh = jnp.pad(fresh, ((0, -fresh.shape[0] % LANES), (0, 0)))
    return pl.pallas_call(
        functools.partial(attention_kernel, steps, rows),
        out_shape=jax.ShapeDtypeStruct((count, model_width), F32),
        in_specs=[
            pl.BlockSpec(memory_space=pltpu.SMEM),
            pl.BlockSpec(memory_space=pltpu.VMEM),
            pl.BlockSpec(memory_space=pltpu.VMEM),
            pl.BlockSpec(memory_space=pltpu.VMEM),
            pl.BlockSpec(memory_space=pl.ANY),
        ],
        out_specs=pl.BlockSpec(memory_space=pltpu.VMEM),
        scratch_shapes=[
            pltpu.VMEM((2 * groups * count, LANES), F32),
            pltpu.VMEM((2 * groups * count, LANES), F32),
            pltpu.VMEM(proj.shape, BF16),
            pltpu.SemaphoreType.DMA,
        ],
        compiler_params=pltpu.CompilerParams(vmem_limit_bytes=VMEM_LIMIT),
        cost_estimate=pl.CostEstimate(flops=2 * count * width * model_width, bytes_accessed=7 << 20, transcendentals=0),
        name="attention",
    )(lengths, queries.reshape(count, width), fresh, cache_kv.reshape(rows, 2 * span, LANES), proj)


def norm_kernel(residual_ref, mine_ref, other_ref, routing_ref, router_ref, mixed_ref, packed_ref):
    width = residual_ref.shape[1]
    mixed = residual_ref[...].astype(F32) + (mine_ref[...] + other_ref[...])
    mixed_ref[...] = mixed
    scale = lax.rsqrt(jnp.mean(mixed * mixed, axis=1, keepdims=True) + 1e-05)
    normed = (mixed * scale).astype(BF16)
    logits = dot(normed, router_ref[...], NT)
    routing = routing_ref[...]
    expert = iota(logits.shape, 1)
    chosen = expert == routing[:, 0:1]
    for slot in range(1, TOP):
        chosen = chosen | (expert == routing[:, slot : slot + 1])
    sigmoids = jnp.where(chosen, jax.nn.sigmoid(logits), 0.0)
    gates = sigmoids / jnp.sum(sigmoids, axis=1, keepdims=True)
    high = gates.astype(BF16)
    low = (gates - high.astype(F32)).astype(BF16)
    first = width // LANES * LANES
    offset = width - first
    target = iota((EXPERTS, LANES), 1) - iota((EXPERTS, LANES), 0)
    tail = dot(high, (target == offset).astype(BF16)) + dot(low, (target == offset + EXPERTS).astype(BF16))
    packed_ref[:, :width] = normed
    packed_ref[:, width : width + LANES - offset] = tail[:, offset:].astype(BF16)


def normalize(residual, mine, other, routing, router):
    count, width = residual.shape
    padded = -(-(width + 2 * EXPERTS) // LANES) * LANES
    return pl.pallas_call(
        norm_kernel,
        out_shape=(
            jax.ShapeDtypeStruct((count, width), F32),
            jax.ShapeDtypeStruct((count, padded), BF16),
        ),
        compiler_params=pltpu.CompilerParams(vmem_limit_bytes=VMEM_LIMIT),
        name="normalize",
    )(residual, mine, other, routing, router.T)


def weights_kernel(mantissa_ref, exponent_ref, out_ref):
    blocks, units = exponent_ref.shape[1], exponent_ref.shape[2]
    width = mantissa_ref.shape[2]
    expander = (iota((blocks, width), 1) // BLOCK == iota((blocks, width), 0)).astype(BF16)
    power = jnp.exp2(exponent_ref[0].astype(F32)).astype(BF16)
    scale = dot(power, expander, TN)
    out_ref[0] = (mantissa_ref[0].astype(F32) * scale).astype(BF16)


def dequantize(mantissa, exponent):
    units, parts, width = mantissa.shape
    blocks = exponent.shape[2]
    step = units
    mantissa = mantissa.transpose(1, 0, 2)
    exponent = exponent.transpose(1, 2, 0)
    return pl.pallas_call(
        weights_kernel,
        grid=(parts,),
        out_shape=jax.ShapeDtypeStruct((parts, units, width), BF16),
        in_specs=[
            pl.BlockSpec((1, step, width), lambda part: (part, 0, 0)),
            pl.BlockSpec((1, blocks, step), lambda part: (part, 0, 0)),
        ],
        out_specs=pl.BlockSpec((1, step, width), lambda part: (part, 0, 0)),
        compiler_params=pltpu.CompilerParams(vmem_limit_bytes=VMEM_LIMIT),
        cost_estimate=pl.CostEstimate(flops=2 * parts * units * blocks * width, bytes_accessed=4 * parts * units * width, transcendentals=0),
        name="weights",
    )(mantissa, exponent)


def experts_kernel(count, width, gate_ref, up_ref, down_ref, member_ref, *refs):
    arrived, (mine_ref, other_ref, rows, gates, total) = refs[:-5], refs[-5:]
    step = pl.program_id(0)

    @pl.when(step == 0)
    def _():
        place = 0
        for ref in arrived:
            rows[place : place + ref.shape[0], :] = ref[...]
            place += ref.shape[0]
        total[...] = jnp.zeros_like(total)
        gates[...] = rows[:, width : width + 2 * EXPERTS]

    inputs = rows[:, :width]
    gate = dot(inputs, gate_ref[0], NT)
    up = dot(inputs, up_ref[0], NT)
    member = member_ref[0]
    share = dot(gates[:, :EXPERTS], member) + dot(gates[:, EXPERTS:], member)
    hidden = (gate * jax.nn.sigmoid(gate) * up * share).astype(BF16)
    total[...] += dot(hidden, down_ref[0])

    @pl.when(step == pl.num_programs(0) - 1)
    def _():
        half = total.shape[0] // 2
        mine_ref[...] = total[:half, :]
        other_ref[...] = total[half:, :].astype(BF16)


def unit_step(units):
    for step in range(240, 15, -16):
        if units % step == 0:
            return step
    return units


def run_experts(weights, member, arrived):
    parts, units, width = weights.shape
    count = sum(block.shape[0] for block in arrived)
    padded = arrived[0].shape[1]
    step = unit_step(units)
    member = member.reshape(EXPERTS, units // step, step).transpose(1, 0, 2)
    part = lambda which: pl.BlockSpec((1, step, width), lambda place: (which, place, 0))
    whole = lambda shape: pl.BlockSpec(shape, lambda place: (0, 0))
    return pl.pallas_call(
        functools.partial(experts_kernel, count, width),
        grid=(units // step,),
        out_shape=(
            jax.ShapeDtypeStruct((count // 2, width), F32),
            jax.ShapeDtypeStruct((count // 2, width), BF16),
        ),
        in_specs=[part(0), part(1), part(2), pl.BlockSpec((1, EXPERTS, step), lambda place: (place, 0, 0))]
        + [whole(block.shape) for block in arrived],
        out_specs=(whole((count // 2, width)), whole((count // 2, width))),
        scratch_shapes=[
            pltpu.VMEM((count, padded), BF16),
            pltpu.VMEM((count, 2 * EXPERTS), BF16),
            pltpu.VMEM((count, width), F32),
        ],
        compiler_params=pltpu.CompilerParams(vmem_limit_bytes=VMEM_LIMIT),
        cost_estimate=pl.CostEstimate(flops=6 * count * units * width, bytes_accessed=6 * units * width, transcendentals=0),
        name="experts",
    )(weights, weights, weights, member, *arrived)


def swap(value):
    return lax.ppermute(value, "tensor", [(0, 1), (1, 0)])


def partners(count):
    half = count // 2
    power = count & (count - 1) == 0
    reach = lambda place, far: place ^ far if power else (place + far) % count
    turns = []
    for turn in range(half):
        pairs = []
        for place in range(count):
            pairs.append((2 * place, 2 * reach(place, turn)))
            pairs.append((2 * place + 1, 2 * reach(place, turn + half) + 1))
        turns.append(pairs)
    return turns


def per_device(residual, queries, new_kv, cache_kv, lengths, routing, router, out_proj, mantissa, exponent, placement):
    places = lax.axis_size("expert")
    place = lax.axis_index("expert")
    steps, rows, width = residual.shape
    count = steps * rows
    units = mantissa.shape[1]
    turns = partners(places)
    both = ("expert", "tensor")

    partial = attend(lengths, queries, new_kv, cache_kv, out_proj)
    weights = dequantize(mantissa[0], exponent[0])
    tile = place * (units // TILE_UNITS) + jnp.arange(units) // TILE_UNITS
    member = jnp.any(placement.reshape(EXPERTS, -1, 1) == tile, axis=1).astype(BF16)

    mixed, packed = normalize(
        residual.reshape(count, width), partial, swap(partial), routing.reshape(count, TOP), router
    )
    near = [lax.ppermute(packed, both, pairs) for pairs in turns]
    far = [swap(block) for block in near]
    mine, other = run_experts(weights, member, near + far)
    mine = mine + swap(other).astype(F32)
    back = [
        lax.ppermute(mine[turn * count : (turn + 1) * count].astype(BF16), both, [(to, back) for back, to in pairs])
        for turn, pairs in enumerate(turns)
    ]
    total = sum(block.astype(F32) for block in back)
    result = mixed + (total + swap(total))
    return result.astype(BF16).reshape(steps, rows, width)


def solution(mesh):
    placed = (
        P(None, ("group", "expert"), None),
        P(None, ("group", "expert"), "tensor"),
        P(None, ("group", "expert"), None, "tensor"),
        P(("group", "expert"), None, None, "tensor"),
        P(("group", "expert")),
        P(None, ("group", "expert"), None),
        P(),
        P("tensor", None),
        P("tensor", "expert", None, None),
        P("tensor", "expert", None, None),
        P("group"),
    )
    return jax.shard_map(
        per_device,
        mesh=mesh,
        in_specs=placed,
        out_specs=P(None, ("group", "expert"), None),
        check_vma=False,
    )
```

time: 625 us -> 70 us (0.11); the launches traced: 614 us -> 69.7 us
  waiting for transfers between devices: 315 us -> 7.42 us
  local copies, waits for them, and re-layouts: 126 us -> 7.34 us
  matrix products: 104 us -> 0 us
  Pallas kernels: 0 us -> 29.8 us
  starting transfers between devices: 47.4 us -> 23.2 us
  between operations: 14.1 us -> 0.16 us
    all_to_all x10 -> x0, waiting for transfers between devices: 299 us -> none  [the longest x1 270 us: per_device(): lax.all_to_all(sent_mant, 'expert', split_axis=0, concat_axis=0, tiled=True)]
    dot_general x44 -> x0, matrix products: 104 us -> none  [the longest x4 23 us: per_device(): jnp.einsum('rd,ud->ru', flat_rows, weights[:, 1, :], preferred_element_ty...]
    all_to_all x10 -> x0, starting transfers between devices: 47.1 us -> none  [the longest x4 17.5 us: per_device(): lax.all_to_all(partial_value.reshape(received.shape), 'expert', split_axi...]
    gather x17 -> x0, local copies, waits for them, and re-layouts: 34.2 us -> none  [the longest x1 14.4 us: per_device(): mant_tiles[send_index]]
    reshape x18 -> x3, local copies, waits for them, and re-layouts: 36.5 us -> 2.82 us  [the longest x1 1.47 us: attend(): queries.reshape(count, width)]
    pallas_call x0 -> x4, Pallas kernels: none -> 29.8 us  [the longest x1 12.1 us: dequantize(): pl.pallas_call(weights_kernel, grid=(parts,), out_shape=jax.ShapeDtypeStr...]
    ppermute x0 -> x15, starting transfers between devices: none -> 23.2 us  [the longest x7 12.5 us: swap(): return lax.ppermute(value, 'tensor', [(0, 1), (1, 0)])]
    another operation x15 -> x0, local copies, waits for them, and re-layouts: 21.8 us -> none  [the longest x1 20.5 us: per_device(): mant_tiles = mantissa[0].reshape(tiles_dev, TILE_UNITS, 3, model_width)]
  transfers between devices with their start and end apart: 13 -> 15, of which waited for: 9 -> 5; matrix products, arithmetic and copies ran while one was open for 34% -> 4% of each run, Pallas kernels for 0% -> 17%
where the time goes in v1:
time: 70 us; the launch traced here: 69.7 us
  Pallas kernels  29.8 us (43%)
  starting transfers between devices  23.2 us (33%)
  waiting for transfers between devices  7.42 us (11%)
  local copies, waits for them, and re-layouts  7.34 us (10%)
  other arithmetic  1.82 us (3%)
    ppermute x7, starting transfers between devices, swap(): return lax.ppermute(value, 'tensor', [(0, 1), (1, 0)])  12.5 us
    pallas_call x1, Pallas kernels, dequantize(): pl.pallas_call(weights_kernel, grid=(parts,), out_shape=jax.ShapeDtypeStr...  12.1 us
    pallas_call x1, Pallas kernels, run_experts(): pl.pallas_call(functools.partial(experts_kernel, count, width), grid=(uni...  9.22 us
    pallas_call x1, Pallas kernels, attend(): pl.pallas_call(functools.partial(attention_kernel, steps, rows), out_shap...  6.14 us
    ppermute x4, starting transfers between devices, per_device(): near = [lax.ppermute(packed, both, pairs) for pairs in turns]  6 us
    ppermute x4, starting transfers between devices, per_device(): lax.ppermute(mine[turn * count:(turn + 1) * count].astype(BF16), both, [(...  4.74 us
    ppermute x4, waiting for transfers between devices, per_device(): lax.ppermute(mine[turn * count:(turn + 1) * count].astype(BF16), both, [(...  4.09 us
    ppermute x7, waiting for transfers between devices, swap(): return lax.ppermute(value, 'tensor', [(0, 1), (1, 0)])  3.32 us
  transfers between devices with their start and end apart: 15, of which 5 were waited for; matrix products, arithmetic and copies ran while one was open for 4% of the time, Pallas kernels for 17%

profile of v1, /device:TPU:0, one launch (start us, length us, event | category | flops | bytes accessed | tf_op | source)
XLA Modules:
  0.0 69.7 jit_solution(3359388349290747971)
XLA Ops:
  0.0 1.5 %reshape.39.queries_ref = bf16[16,1024]{1,0:T(8,128)(2,1)} reshape(bf16[4,4,1024]{2,1,0:T(4,128)(2,1)} %param.12) | data formatting | bytes 65536 | tf_op jit(solution)/shard_map/reshape | solution.py:113
  1.5 1.3 %pad.4.fresh_ref = bf16[128,128]{1,0:T(8,128)(2,1)} pad(bf16[32,128]{1,0:T(8,128)(2,1)} %bitcast.23, bf16[]{:T(256)} %constant.7.clone.1), padding=0_96x0_0 | pad | bytes 40962 | tf_op jit(solution)/shard_map/jit(_pad)/pad | solution.py:92
  2.8 6.1 %attention.1.mine_ref = f32[16,2880]{1,0:T(8,128)} custom-call(s32[4]{0:T(128)} %lengths_ref.1, bf16[16,1024]{1,0:T(8,128)(2,1)} %reshape.39.queries_ref, bf16[128,128]{1,0:T(8,128)(2,1)} %pad.4.fresh_ref, bf16[4,512,128]{2,1,0:T(8,128)(2,1)} %bitcast.19, bf16[2880,1024]{1,0:T(8,128)(2,1)} %bitcast.17), custom_call_target="tpu_custom_call" | custom-call | flops 94371840 | bytes 7340032 | tf_op jit(solution)/shard_map/attention/pallas_call | solution.py:93
  9.5 0.7 reshape.38.residual_ref
  10.7 0.7 copy-done.2
  11.4 2.2 %normalize.1 = (f32[16,2880]{1,0:T(8,128)}, bf16[16,2944]{1,0:T(8,128)(2,1)}) custom-call(bf16[16,2880]{1,0:T(8,128)(2,1)} %reshape.38.residual_ref, f32[16,2880]{1,0:T(8,128)} %attention.1.mine_ref, f32[16,2880]{1,0:T(8,128)} %copy-done.2, s32[16,4]{1,0:T(8,128)} %bitcast.22, bf16[8,2880]{1,0:T(8,128)(2,1)} %bitcast.21), custom_call_target="tpu_custom_call" | custom-call | tf_op jit(solution)/shard_map/normalize/pallas_call | solution.py:143
  13.6 3.9 %collective-permute-start.4 = (bf16[16,2944]{1,0:T(8,128)(2,1)}, bf16[16,2944]{1,0:T(8,128)(2,1)S(1)}, u32[]{:S(2)}, u32[]{:S(2)}) collective-permute-start(bf16[16,2944]{1,0:T(8,128)(2,1)} %get-tuple-element.10), channel_id=1, source_target_pairs={{0,6},{1,15},{2,4},{3,13},{4,2},{5,11},{6,0},{7,9},{8,14},{9,7},{1... | collective-permute-start | bytes 282632 | tf_op jit(solution)/shard_map/ppermute | solution.py:283
  18.1 1.5 %collective-permute-start.1 = (bf16[16,2944]{1,0:T(8,128)(2,1)}, bf16[16,2944]{1,0:T(8,128)(2,1)S(1)}, u32[]{:S(2)}, u32[]{:S(2)}) collective-permute-start(bf16[16,2944]{1,0:T(8,128)(2,1)} %get-tuple-element.10), channel_id=1, source_target_pairs={{0,0},{1,9},{2,2},{3,11},{4,4},{5,13},{6,6},{7,15},{8,8},{9,1},{10... | collective-permute-start | bytes 282632 | tf_op jit(solution)/shard_map/ppermute | solution.py:283
  20.3 0.6 copy.25
  20.9 1.0 %copy.24 = s32[1,720,3,90]{1,3,0,2:T(8,128)} copy(s32[1,720,3,90]{1,0,3,2:T(1,128)S(1)} %copy-done) | data formatting | bytes 1555200
  21.9 4.1 %collective-permute-start.8 = (bf16[16,2944]{1,0:T(8,128)(2,1)S(1)}, bf16[16,2944]{1,0:T(8,128)(2,1)S(1)}, u32[]{:S(2)}, u32[]{:S(2)}) collective-permute-start(bf16[16,2944]{1,0:T(8,128)(2,1)S(1)} %collective-permute-done.4.refs_3_), channel_id=1, source_target_pairs={{0,1},{1,0},{2,3},{3,2},{4,5},{5,4},{6,7},{7,6},{8,9},{9,8},{10,11... | collective-permute-start | bytes 282632 | tf_op jit(solution)/shard_map/ppermute | solution.py:249
  26.0 0.8 %collective-permute-start.6 = (bf16[16,2944]{1,0:T(8,128)(2,1)S(1)}, bf16[16,2944]{1,0:T(8,128)(2,1)S(1)}, u32[]{:S(2)}, u32[]{:S(2)}) collective-permute-start(bf16[16,2944]{1,0:T(8,128)(2,1)S(1)} %collective-permute-done.2.refs_1_), channel_id=1, source_target_pairs={{0,1},{1,0},{2,3},{3,2},{4,5},{5,4},{6,7},{7,6},{8,9},{9,8},{10,11... | collective-permute-start | bytes 282632 | tf_op jit(solution)/shard_map/ppermute | solution.py:249
  27.2 12.1 %weights.1.gate_ref.up_ref.down_ref = bf16[3,720,2880]{2,1,0:T(8,128)(2,1)} custom-call(bf16[3,720,2880]{2,1,0:T(8,128)(2,1)} %bitcast.16, s32[3,90,720]{2,1,0:T(8,128)} %bitcast.18), custom_call_target="tpu_custom_call" | custom-call | flops 1119744000 | bytes 24883200 | tf_op jit(solution)/shard_map/weights/pallas_call | solution.py:169
  40.1 9.2 %experts.1 = (f32[64,2880]{1,0:T(8,128)}, bf16[64,2880]{1,0:T(8,128)(2,1)}) custom-call(bf16[3,720,2880]{2,1,0:T(8,128)(2,1)} %weights.1.gate_ref.up_ref.down_ref, bf16[3,720,2880]{2,1,0:T(8,128)(2,1)} %weights.1.gate_ref.up_ref.down_ref, bf16[3,720,2880]{2,1,0:T(8,128)(2,1)} %weights.1.gate_ref.up_ref.down_ref, bf16[3,8,240]{2,1,0:T(8,128)(2,1)} %bitcast.20, ...), custom_call_target="tpu_custom_call" | custom-call | flops 1592524800 | bytes 12441600 | tf_op jit(solution)/shard_map/experts/pallas_call | solution.py:227
  49.5 1.8 %collective-permute-done.9 = bf16[64,2880]{1,0:T(8,128)(2,1)S(1)} collective-permute-done((bf16[64,2880]{1,0:T(8,128)(2,1)}, bf16[64,2880]{1,0:T(8,128)(2,1)S(1)}, u32[]{:S(2)}, u32[]{:S(2)}) %collective-permute-start.9) | collective-permute-done | bytes 368672 | tf_op jit(solution)/shard_map/ppermute | solution.py:249
  51.3 1.2 %add_convert_fusion = bf16[64,2880]{1,0:T(8,128)(2,1)S(1)} fusion(f32[64,2880]{1,0:T(8,128)} %get-tuple-element.11, bf16[64,2880]{1,0:T(8,128)(2,1)S(1)} %collective-permute-done.9), kind=kLoop, calls=%fused_computation.2 | loop fusion | flops 552960 | bytes 1474560 | tf_op jit(solution)/shard_map/convert.5
  52.5 0.7 collective-permute-start.10
  53.2 3.4 %collective-permute-start.13 = (bf16[16,2880]{1,0:T(8,128)(2,1)S(1)}, bf16[16,2880]{1,0:T(8,128)(2,1)S(1)}, u32[]{:S(2)}, u32[]{:S(2)}) collective-permute-start(bf16[16,2880]{1,0:T(8,128)(2,1)S(1)} %get-tuple-element.14), channel_id=1, source_target_pairs={{6,0},{15,1},{4,2},{13,3},{2,4},{11,5},{0,6},{9,7},{14,8},{7,9},{1... | collective-permute-start | bytes 276488 | tf_op jit(solution)/shard_map/ppermute | solution.py:288
  56.6 0.6 collective-permute-start.11
  57.3 2.9 %collective-permute-done.13 = bf16[16,2880]{1,0:T(8,128)(2,1)S(1)} collective-permute-done((bf16[16,2880]{1,0:T(8,128)(2,1)S(1)}, bf16[16,2880]{1,0:T(8,128)(2,1)S(1)}, u32[]{:S(2)}, u32[]{:S(2)}) %collective-permute-start.13) | collective-permute-done | bytes 92192 | tf_op jit(solution)/shard_map/ppermute | solution.py:288
  60.2 1.2 %collective-permute-done.12 = bf16[16,2880]{1,0:T(8,128)(2,1)S(1)} collective-permute-done((bf16[16,2880]{1,0:T(8,128)(2,1)S(1)}, bf16[16,2880]{1,0:T(8,128)(2,1)S(1)}, u32[]{:S(2)}, u32[]{:S(2)}) %collective-permute-start.12) | collective-permute-done | bytes 92192 | tf_op jit(solution)/shard_map/ppermute | solution.py:288
  61.4 6.5 %collective-permute-start.14 = (f32[16,2880]{1,0:T(8,128)S(1)}, f32[16,2880]{1,0:T(8,128)S(1)}, u32[]{:S(2)}, u32[]{:S(2)}) collective-permute-start(f32[16,2880]{1,0:T(8,128)S(1)} %convert_add_fusion), channel_id=1, source_target_pairs={{0,1},{1,0},{2,3},{3,2},{4,5},{5,4},{6,7},{7,6},{8,9},{9,8},{10,11... | collective-permute-start | bytes 552968 | tf_op jit(solution)/shard_map/ppermute | solution.py:249
  67.9 1.1 %collective-permute-done.14 = f32[16,2880]{1,0:T(8,128)S(1)} collective-permute-done((f32[16,2880]{1,0:T(8,128)S(1)}, f32[16,2880]{1,0:T(8,128)S(1)}, u32[]{:S(2)}, u32[]{:S(2)}) %collective-permute-start.14) | collective-permute-done | bytes 184352 | tf_op jit(solution)/shard_map/ppermute | solution.py:249
  69.0 0.7 reshape.43
  (51 shorter events, 3.8 us)
Async XLA Ops:
  0.0 9.4 %copy-start.12 = (s32[960]{0:T(1024)S(1)}, s32[960]{0:T(1024)}, u32[]{:S(2)}) copy-start(s32[960]{0:T(1024)} %param.21) | copy-start | bytes 11524
  0.0 9.5 %copy-start.11 = (bf16[4,4,2880]{2,1,0:T(4,128)(2,1)S(1)}, bf16[4,4,2880]{2,1,0:T(4,128)(2,1)}, u32[]{:S(2)}) copy-start(bf16[4,4,2880]{2,1,0:T(4,128)(2,1)} %param.11) | copy-start | bytes 276484
  0.0 20.9 %copy-start = (s32[1,720,3,90]{1,0,3,2:T(1,128)S(1)}, s32[1,720,3,90]{1,0,3,2:T(1,128)}, u32[]{:S(2)}) copy-start(s32[1,720,3,90]{1,0,3,2:T(1,128)} %param.20) | copy-start | bytes 2332804
  8.9 1.8 %collective-permute-start = (f32[16,2880]{1,0:T(8,128)}, f32[16,2880]{1,0:T(8,128)S(1)}, u32[]{:S(2)}, u32[]{:S(2)}) collective-permute-start(f32[16,2880]{1,0:T(8,128)} %attention.1.mine_ref), channel_id=1, source_target_pairs={{0,1},{1,0},{2,3},{3,2},{4,5},{5,4},{6,7},{7,6},{8,9},{9,8},{10,11... | collective-permute-start | bytes 552968 | tf_op jit(solution)/shard_map/ppermute | solution.py:249
  13.6 8.3 %collective-permute-start.4 = (bf16[16,2944]{1,0:T(8,128)(2,1)}, bf16[16,2944]{1,0:T(8,128)(2,1)S(1)}, u32[]{:S(2)}, u32[]{:S(2)}) collective-permute-start(bf16[16,2944]{1,0:T(8,128)(2,1)} %get-tuple-element.10), channel_id=1, source_target_pairs={{0,6},{1,15},{2,4},{3,13},{4,2},{5,11},{6,0},{7,9},{8,14},{9,7},{1... | collective-permute-start | bytes 282632 | tf_op jit(solution)/shard_map/ppermute | solution.py:283
  17.5 8.4 %collective-permute-start.3 = (bf16[16,2944]{1,0:T(8,128)(2,1)}, bf16[16,2944]{1,0:T(8,128)(2,1)S(1)}, u32[]{:S(2)}, u32[]{:S(2)}) collective-permute-start(bf16[16,2944]{1,0:T(8,128)(2,1)} %get-tuple-element.10), channel_id=1, source_target_pairs={{0,4},{1,13},{2,6},{3,15},{4,0},{5,9},{6,2},{7,11},{8,12},{9,5},{1... | collective-permute-start | bytes 282632 | tf_op jit(solution)/shard_map/ppermute | solution.py:283
  18.0 8.1 %collective-permute-start.2 = (bf16[16,2944]{1,0:T(8,128)(2,1)}, bf16[16,2944]{1,0:T(8,128)(2,1)S(1)}, u32[]{:S(2)}, u32[]{:S(2)}) collective-permute-start(bf16[16,2944]{1,0:T(8,128)(2,1)} %get-tuple-element.10), channel_id=1, source_target_pairs={{0,2},{1,11},{2,0},{3,9},{4,6},{5,15},{6,4},{7,13},{8,10},{9,3},{1... | collective-permute-start | bytes 282632 | tf_op jit(solution)/shard_map/ppermute | solution.py:283
  18.1 8.7 %collective-permute-start.1 = (bf16[16,2944]{1,0:T(8,128)(2,1)}, bf16[16,2944]{1,0:T(8,128)(2,1)S(1)}, u32[]{:S(2)}, u32[]{:S(2)}) collective-permute-start(bf16[16,2944]{1,0:T(8,128)(2,1)} %get-tuple-element.10), channel_id=1, source_target_pairs={{0,0},{1,9},{2,2},{3,11},{4,4},{5,13},{6,6},{7,15},{8,8},{9,1},{10... | collective-permute-start | bytes 282632 | tf_op jit(solution)/shard_map/ppermute | solution.py:283
  21.9 17.5 %copy-start.3 = (bf16[16,2944]{1,0:T(8,128)(2,1)}, bf16[16,2944]{1,0:T(8,128)(2,1)S(1)}, u32[]{:S(2)}) copy-start(bf16[16,2944]{1,0:T(8,128)(2,1)S(1)} %collective-permute-done.4.refs_3_) | copy-start | bytes 282628
  21.9 17.5 %collective-permute-start.8 = (bf16[16,2944]{1,0:T(8,128)(2,1)S(1)}, bf16[16,2944]{1,0:T(8,128)(2,1)S(1)}, u32[]{:S(2)}, u32[]{:S(2)}) collective-permute-start(bf16[16,2944]{1,0:T(8,128)(2,1)S(1)} %collective-permute-done.4.refs_3_), channel_id=1, source_target_pairs={{0,1},{1,0},{2,3},{3,2},{4,5},{5,4},{6,7},{7,6},{8,9},{9,8},{10,11... | collective-permute-start | bytes 282632 | tf_op jit(solution)/shard_map/ppermute | solution.py:249
  26.0 13.4 %copy-start.4 = (bf16[16,2944]{1,0:T(8,128)(2,1)}, bf16[16,2944]{1,0:T(8,128)(2,1)S(1)}, u32[]{:S(2)}) copy-start(bf16[16,2944]{1,0:T(8,128)(2,1)S(1)} %collective-permute-done.3.refs_2_) | copy-start | bytes 282628
  26.0 13.4 %collective-permute-start.7 = (bf16[16,2944]{1,0:T(8,128)(2,1)S(1)}, bf16[16,2944]{1,0:T(8,128)(2,1)S(1)}, u32[]{:S(2)}, u32[]{:S(2)}) collective-permute-start(bf16[16,2944]{1,0:T(8,128)(2,1)S(1)} %collective-permute-done.3.refs_2_), channel_id=1, source_target_pairs={{0,1},{1,0},{2,3},{3,2},{4,5},{5,4},{6,7},{7,6},{8,9},{9,8},{10,11... | collective-permute-start | bytes 282632 | tf_op jit(solution)/shard_map/ppermute | solution.py:249
  26.0 13.3 %copy-start.5 = (bf16[16,2944]{1,0:T(8,128)(2,1)}, bf16[16,2944]{1,0:T(8,128)(2,1)S(1)}, u32[]{:S(2)}) copy-start(bf16[16,2944]{1,0:T(8,128)(2,1)S(1)} %collective-permute-done.2.refs_1_) | copy-start | bytes 282628
  26.0 13.4 %collective-permute-start.6 = (bf16[16,2944]{1,0:T(8,128)(2,1)S(1)}, bf16[16,2944]{1,0:T(8,128)(2,1)S(1)}, u32[]{:S(2)}, u32[]{:S(2)}) collective-permute-start(bf16[16,2944]{1,0:T(8,128)(2,1)S(1)} %collective-permute-done.2.refs_1_), channel_id=1, source_target_pairs={{0,1},{1,0},{2,3},{3,2},{4,5},{5,4},{6,7},{7,6},{8,9},{9,8},{10,11... | collective-permute-start | bytes 282632 | tf_op jit(solution)/shard_map/ppermute | solution.py:249
  26.8 12.5 %copy-start.6 = (bf16[16,2944]{1,0:T(8,128)(2,1)}, bf16[16,2944]{1,0:T(8,128)(2,1)S(1)}, u32[]{:S(2)}) copy-start(bf16[16,2944]{1,0:T(8,128)(2,1)S(1)} %collective-permute-done.1.refs_0_) | copy-start | bytes 282628
  26.8 12.6 %collective-permute-start.5 = (bf16[16,2944]{1,0:T(8,128)(2,1)S(1)}, bf16[16,2944]{1,0:T(8,128)(2,1)S(1)}, u32[]{:S(2)}, u32[]{:S(2)}) collective-permute-start(bf16[16,2944]{1,0:T(8,128)(2,1)S(1)} %collective-permute-done.1.refs_0_), channel_id=1, source_target_pairs={{0,1},{1,0},{2,3},{3,2},{4,5},{5,4},{6,7},{7,6},{8,9},{9,8},{10,11... | collective-permute-start | bytes 282632 | tf_op jit(solution)/shard_map/ppermute | solution.py:249
  39.4 0.7 %copy-start.10 = (bf16[16,2944]{1,0:T(8,128)(2,1)}, bf16[16,2944]{1,0:T(8,128)(2,1)S(1)}, u32[]{:S(2)}) copy-start(bf16[16,2944]{1,0:T(8,128)(2,1)S(1)} %collective-permute-done.5.refs_4_) | copy-start | bytes 282628
  40.1 28.8 %copy-start.1 = (f32[16,2880]{1,0:T(8,128)S(1)}, f32[16,2880]{1,0:T(8,128)}, u32[]{:S(2)}) copy-start(f32[16,2880]{1,0:T(8,128)} %get-tuple-element.9) | copy-start | bytes 552964
  49.4 1.9 %collective-permute-start.9 = (bf16[64,2880]{1,0:T(8,128)(2,1)}, bf16[64,2880]{1,0:T(8,128)(2,1)S(1)}, u32[]{:S(2)}, u32[]{:S(2)}) collective-permute-start(bf16[64,2880]{1,0:T(8,128)(2,1)} %get-tuple-element.12), channel_id=1, source_target_pairs={{0,1},{1,0},{2,3},{3,2},{4,5},{5,4},{6,7},{7,6},{8,9},{9,8},{10,11... | collective-permute-start | bytes 1105928 | tf_op jit(solution)/shard_map/ppermute | solution.py:249
  52.5 4.8 %collective-permute-start.10 = (bf16[16,2880]{1,0:T(8,128)(2,1)S(1)}, bf16[16,2880]{1,0:T(8,128)(2,1)S(1)}, u32[]{:S(2)}, u32[]{:S(2)}) collective-permute-start(bf16[16,2880]{1,0:T(8,128)(2,1)S(1)} %get-tuple-element.13), channel_id=1, source_target_pairs={{0,0},{9,1},{2,2},{11,3},{4,4},{13,5},{6,6},{15,7},{8,8},{1,9},{10... | collective-permute-start | bytes 276488 | tf_op jit(solution)/shard_map/ppermute | solution.py:288
  53.2 7.0 %collective-permute-start.13 = (bf16[16,2880]{1,0:T(8,128)(2,1)S(1)}, bf16[16,2880]{1,0:T(8,128)(2,1)S(1)}, u32[]{:S(2)}, u32[]{:S(2)}) collective-permute-start(bf16[16,2880]{1,0:T(8,128)(2,1)S(1)} %get-tuple-element.14), channel_id=1, source_target_pairs={{6,0},{15,1},{4,2},{13,3},{2,4},{11,5},{0,6},{9,7},{14,8},{7,9},{1... | collective-permute-start | bytes 276488 | tf_op jit(solution)/shard_map/ppermute | solution.py:288
  56.6 4.7 %collective-permute-start.12 = (bf16[16,2880]{1,0:T(8,128)(2,1)S(1)}, bf16[16,2880]{1,0:T(8,128)(2,1)S(1)}, u32[]{:S(2)}, u32[]{:S(2)}) collective-permute-start(bf16[16,2880]{1,0:T(8,128)(2,1)S(1)} %get-tuple-element.15), channel_id=1, source_target_pairs={{4,0},{13,1},{6,2},{15,3},{0,4},{9,5},{2,6},{11,7},{12,8},{5,9},{1... | collective-permute-start | bytes 276488 | tf_op jit(solution)/shard_map/ppermute | solution.py:288
  56.6 4.7 %collective-permute-start.11 = (bf16[16,2880]{1,0:T(8,128)(2,1)S(1)}, bf16[16,2880]{1,0:T(8,128)(2,1)S(1)}, u32[]{:S(2)}, u32[]{:S(2)}) collective-permute-start(bf16[16,2880]{1,0:T(8,128)(2,1)S(1)} %get-tuple-element.16), channel_id=1, source_target_pairs={{2,0},{11,1},{0,2},{9,3},{6,4},{15,5},{4,6},{13,7},{10,8},{3,9},{8... | collective-permute-start | bytes 276488 | tf_op jit(solution)/shard_map/ppermute | solution.py:288
  61.4 7.6 %collective-permute-start.14 = (f32[16,2880]{1,0:T(8,128)S(1)}, f32[16,2880]{1,0:T(8,128)S(1)}, u32[]{:S(2)}, u32[]{:S(2)}) collective-permute-start(f32[16,2880]{1,0:T(8,128)S(1)} %convert_add_fusion), channel_id=1, source_target_pairs={{0,1},{1,0},{2,3},{3,2},{4,5},{5,4},{6,7},{7,6},{8,9},{9,8},{10,11... | collective-permute-start | bytes 552968 | tf_op jit(solution)/shard_map/ppermute | solution.py:249
  (4 other events, 2.7 us)

commit v2 on v1

v2 whole, which is shorter than its diff:
```python
import functools

import jax
import jax.numpy as jnp
from jax import lax
from jax.experimental import pallas as pl
from jax.experimental.pallas import tpu as pltpu
from jax.sharding import PartitionSpec as P

HD = 64
EXPERTS = 8
TOP = 4
BLOCK = 32
TILE_UNITS = 6
LANES = 128
AHEAD = 3
F32 = jnp.float32
BF16 = jnp.bfloat16

NT = (((1,), (1,)), ((), ()))
TN = (((0,), (0,)), ((), ()))
TT = (((0,), (1,)), ((), ()))


def dot(a, b, dims=(((1,), (0,)), ((), ()))):
    return lax.dot_general(a, b, dims, preferred_element_type=F32)


def iota(shape, dim):
    return lax.broadcasted_iota(jnp.int32, shape, dim)


def vmem(shape, dtype):
    return pltpu.VMEM(shape, dtype)


def held(value):
    return pltpu.with_memory_space_constraint(value, pltpu.VMEM)


def afar(value):
    return pltpu.with_memory_space_constraint(value, pltpu.HBM)


def whole(count):
    return [pl.BlockSpec(memory_space=pltpu.VMEM)] * count


def params(mebibytes=8):
    return pltpu.CompilerParams(vmem_limit_bytes=mebibytes << 20)


def attention_kernel(
    lengths_ref,
    queries_hbm,
    fresh_hbm,
    cache_hbm,
    proj_hbm,
    out_ref,
    queries,
    fresh_rows,
    cache_rows,
    proj,
    packed,
    mixed,
    sems,
):
    late_width = fresh_hbm.shape[0]
    fresh_rows[...] = jnp.zeros_like(fresh_rows)
    moves = [
        pltpu.make_async_copy(queries_hbm, queries, sems.at[0]),
        pltpu.make_async_copy(fresh_hbm, fresh_rows.at[:late_width], sems.at[1]),
        pltpu.make_async_copy(cache_hbm, cache_rows, sems.at[2]),
        pltpu.make_async_copy(proj_hbm, proj, sems.at[3]),
    ]
    for move in moves:
        move.start()
    steps, rows, _ = queries.shape
    count = steps * rows
    groups = queries.shape[2] // LANES
    half = groups // 2
    lane = iota((rows, LANES), 1)
    moves[0].wait()
    for step in range(steps):
        for group in range(groups):
            piece = queries[step, :, group * LANES : (group + 1) * LANES].astype(F32) * (HD**-0.5)
            mine = (lane < HD) == (group < half)
            first = group * count + step * rows
            packed[first : first + rows, :] = jnp.where(mine, piece, 0.0)
            first += groups * count
            packed[first : first + rows, :] = jnp.where(mine, pltpu.roll(piece, HD, 1), 0.0)
    amount = 2 * groups * steps
    span = cache_rows.shape[1]
    width = fresh_rows.shape[0]
    spot = iota((amount, span), 1)
    step_of = iota((amount, width), 0) % steps
    fresh_spot = iota((amount, width), 1)
    fresh_step = fresh_spot // (2 * rows)
    moves[1].wait()
    moves[2].wait()
    fresh = fresh_rows[...]
    for row in range(rows):
        now = packed[pl.ds(row, amount, stride=rows), :].astype(BF16)
        cache = cache_rows[row]
        scores = dot(now, cache, NT)
        live = (spot % 2 == 0) & (spot < 2 * lengths_ref[row])
        scores = jnp.where(live, scores, -1e30)
        late = dot(now, fresh, NT)
        seen = (fresh_spot % (2 * rows) == 2 * row) & (fresh_step <= step_of)
        late = jnp.where(seen, late, -1e30)
        highest = jnp.maximum(
            jnp.max(scores, axis=1, keepdims=True), jnp.max(late, axis=1, keepdims=True)
        )
        scores = jnp.exp(scores - highest)
        late = jnp.exp(late - highest)
        total = jnp.sum(scores, axis=1, keepdims=True) + jnp.sum(late, axis=1, keepdims=True)
        probs = pltpu.roll(scores / total, 1, 1).astype(BF16)
        late_probs = pltpu.roll(late / total, 1, 1).astype(BF16)
        mixed[pl.ds(row, amount, stride=rows), :] = dot(probs, cache) + dot(late_probs, fresh)
    heads = []
    lane = iota((count, LANES), 1)
    for group in range(groups):
        straight = mixed[group * count : (group + 1) * count, :]
        turned = mixed[(groups + group) * count : (groups + group + 1) * count, :]
        mine = (lane < HD) == (group < half)
        heads.append(jnp.where(mine, straight, pltpu.roll(turned, HD, 1)).astype(BF16))
    moves[3].wait()
    out_ref[...] = dot(jnp.concatenate(heads, axis=1), proj[...], NT)


def attend(lengths, queries, new_kv, cache_kv, out_proj):
    steps, rows, width = queries.shape
    span = cache_kv.shape[1]
    proj = out_proj.T
    model_width = proj.shape[0]
    count = steps * rows
    groups = width // LANES
    fresh = new_kv.reshape(count * 2, LANES)
    cache = cache_kv.reshape(rows, 2 * span, LANES)
    padded = -(-fresh.shape[0] // LANES) * LANES
    return pl.pallas_call(
        attention_kernel,
        out_shape=vmem((count, model_width), F32),
        in_specs=[pl.BlockSpec(memory_space=pltpu.SMEM)] + [pl.BlockSpec(memory_space=pltpu.HBM)] * 4,
        out_specs=pl.BlockSpec(memory_space=pltpu.VMEM),
        scratch_shapes=[
            pltpu.VMEM(queries.shape, BF16),
            pltpu.VMEM((padded, LANES), BF16),
            pltpu.VMEM(cache.shape, BF16),
            pltpu.VMEM(proj.shape, BF16),
            pltpu.VMEM((2 * groups * count, LANES), F32),
            pltpu.VMEM((2 * groups * count, LANES), F32),
            pltpu.SemaphoreType.DMA((4,)),
        ],
        compiler_params=params(16),
        cost_estimate=pl.CostEstimate(
            flops=2 * count * width * model_width, bytes_accessed=7 << 20, transcendentals=0
        ),
        name="attention",
    )(lengths, afar(queries), afar(fresh), afar(cache), afar(proj))


def norm_kernel(residual_ref, mine_ref, other_ref, routing_ref, router_ref, mixed_ref, packed_ref):
    steps, rows, width = residual_ref.shape
    for step in range(steps):
        mixed_ref[step * rows : (step + 1) * rows, :] = residual_ref[step].astype(F32)
    mixed = mixed_ref[...] + (mine_ref[...] + other_ref[...])
    mixed_ref[...] = mixed
    scale = lax.rsqrt(jnp.mean(mixed * mixed, axis=1, keepdims=True) + 1e-05)
    normed = (mixed * scale).astype(BF16)
    logits = dot(normed, router_ref[...], NT)
    routing = routing_ref[...]
    expert = iota(logits.shape, 1)
    chosen = expert == routing[:, 0:1]
    for slot in range(1, TOP):
        chosen = chosen | (expert == routing[:, slot : slot + 1])
    sigmoids = jnp.where(chosen, jax.nn.sigmoid(logits), 0.0)
    gates = sigmoids / jnp.sum(sigmoids, axis=1, keepdims=True)
    high = gates.astype(BF16)
    low = (gates - high.astype(F32)).astype(BF16)
    first = width // LANES * LANES
    offset = width - first
    target = iota((EXPERTS, LANES), 1) - iota((EXPERTS, LANES), 0)
    tail = dot(high, (target == offset).astype(BF16)) + dot(low, (target == offset + EXPERTS).astype(BF16))
    packed_ref[:, :width] = normed
    packed_ref[:, width : width + LANES - offset] = tail[:, offset:].astype(BF16)


def normalize(residual, mine, other, routing, router):
    steps, rows, width = residual.shape
    count = steps * rows
    padded = -(-(width + 2 * EXPERTS) // LANES) * LANES
    return pl.pallas_call(
        norm_kernel,
        out_shape=(vmem((count, width), F32), vmem((count, padded), BF16)),
        in_specs=whole(5),
        out_specs=whole(2),
        compiler_params=params(),
        name="normalize",
    )(held(residual), held(mine), held(other), held(routing), held(router.T))


def weights_kernel(step, packed_ref, mantissa_hbm, exponent_ref, *refs):
    out_refs, (power, expander, sems) = refs[:-3], refs[-3:]
    units, blocks = power.shape
    width = expander.shape[1]
    pieces = [(part, first) for part in range(len(out_refs)) for first in range(0, units, step)]
    moves = [
        pltpu.make_async_copy(
            mantissa_hbm.at[part, pl.ds(first, step), :], out_refs[part].at[pl.ds(first, step), :], sems.at[place]
        )
        for place, (part, first) in enumerate(pieces)
    ]
    for move in moves[:AHEAD]:
        move.start()
    expander[...] = (iota((blocks, width), 1) // BLOCK == iota((blocks, width), 0)).astype(BF16)
    for place, (part, first) in enumerate(pieces):
        if first == 0:
            exponent = exponent_ref[part * blocks : (part + 1) * blocks, 0, :]
            power[...] = jnp.exp2(exponent.astype(F32)).T.astype(BF16)
        rows = slice(first, first + step)
        moves[place].wait()
        for move in moves[place + AHEAD : place + AHEAD + 1]:
            move.start()
        scale = dot(power[rows, :], expander[...])
        out_refs[part][rows, :] = (out_refs[part][rows, :].astype(F32) * scale).astype(BF16)


def dequantize(packed, mantissa, exponent):
    parts, units, width = mantissa.shape
    blocks = exponent.shape[0] // parts
    step = unit_step(units)
    return pl.pallas_call(
        functools.partial(weights_kernel, step),
        out_shape=(vmem((units, width), BF16),) * parts,
        in_specs=[whole(1)[0], pl.BlockSpec(memory_space=pltpu.HBM), whole(1)[0]],
        out_specs=whole(parts),
        scratch_shapes=[
            pltpu.VMEM((units, blocks), BF16),
            pltpu.VMEM((blocks, width), BF16),
            pltpu.SemaphoreType.DMA((parts * units // step,)),
        ],
        compiler_params=params(14),
        cost_estimate=pl.CostEstimate(
            flops=2 * parts * units * blocks * width, bytes_accessed=2 * parts * units * width, transcendentals=0
        ),
        name="weights",
    )(held(packed), afar(mantissa), held(exponent))


def experts_kernel(gate_ref, up_ref, down_ref, member_ref, *refs):
    arrived, (mine_ref, other_ref, rows, share) = refs[:-4], refs[-4:]
    units, width = gate_ref.shape
    place = 0
    for ref in arrived:
        rows[place : place + ref.shape[0], :] = ref[...]
        place += ref.shape[0]
    inputs = rows[:, :width]
    high = rows[:, width : width + EXPERTS]
    low = rows[:, width + EXPERTS : width + 2 * EXPERTS]
    share[...] = dot(member_ref[...], high, TT) + dot(member_ref[...], low, TT)
    step = unit_step(units)
    hidden = []
    for first in range(0, units, step):
        here = slice(first, first + step)
        gate = dot(gate_ref[here, :], inputs, NT)
        up = dot(up_ref[here, :], inputs, NT)
        hidden.append((gate * jax.nn.sigmoid(gate) * up * share[here, :]).astype(BF16))
    hidden = jnp.concatenate(hidden, axis=0).T
    half = mine_ref.shape[0]
    for first in range(0, width, 512):
        here = slice(first, min(first + 512, width))
        total = dot(hidden, down_ref[:, here])
        mine_ref[:, here] = total[:half, :]
        other_ref[:, here] = total[half:, :].astype(BF16)


def unit_step(units):
    for step in range(240, 15, -16):
        if units % step == 0:
            return step
    return units


def run_experts(weights, member, arrived):
    units, width = weights[0].shape
    count = sum(block.shape[0] for block in arrived)
    padded = arrived[0].shape[1]
    return pl.pallas_call(
        experts_kernel,
        out_shape=(vmem((count // 2, width), F32), vmem((count // 2, width), BF16)),
        in_specs=whole(4 + len(arrived)),
        out_specs=whole(2),
        scratch_shapes=[pltpu.VMEM((count, padded), BF16), pltpu.VMEM((units, count), F32)],
        compiler_params=params(16),
        cost_estimate=pl.CostEstimate(
            flops=6 * count * units * width, bytes_accessed=6 * units * width, transcendentals=0
        ),
        name="experts",
    )(*[held(kind) for kind in weights], held(member), *[held(block) for block in arrived])


def join_kernel(mine_ref, other_ref, *out_refs):
    count = out_refs[0].shape[0]
    for turn, out_ref in enumerate(out_refs):
        here = slice(turn * count, (turn + 1) * count)
        out_ref[...] = (mine_ref[here, :] + other_ref[here, :].astype(F32)).astype(BF16)


def join(mine, other, count):
    turns = mine.shape[0] // count
    return pl.pallas_call(
        join_kernel,
        out_shape=[vmem((count, mine.shape[1]), BF16)] * turns,
        in_specs=whole(2),
        out_specs=whole(turns),
        compiler_params=params(),
        name="join",
    )(held(mine), held(other))


def last_kernel(mixed_ref, mine_ref, other_ref, out_ref):
    steps, rows, _ = out_ref.shape
    result = (mixed_ref[...] + (mine_ref[...] + other_ref[...])).astype(BF16)
    for step in range(steps):
        out_ref[step] = result[step * rows : (step + 1) * rows, :]


def last(mixed, mine, other, shape):
    return pl.pallas_call(
        last_kernel,
        out_shape=jax.ShapeDtypeStruct(shape, BF16),
        in_specs=whole(3),
        out_specs=pl.BlockSpec(memory_space=pltpu.VMEM),
        compiler_params=params(),
        name="last",
    )(held(mixed), held(mine), held(other))


def swap(value):
    return lax.ppermute(value, "tensor", [(0, 1), (1, 0)])


def partners(count):
    half = count // 2
    power = count & (count - 1) == 0
    reach = lambda place, far: place ^ far if power else (place + far) % count
    turns = []
    for turn in range(half):
        pairs = []
        for place in range(count):
            pairs.append((2 * place, 2 * reach(place, turn)))
            pairs.append((2 * place + 1, 2 * reach(place, turn + half) + 1))
        turns.append(pairs)
    return turns


def per_device(residual, queries, new_kv, cache_kv, lengths, routing, router, out_proj, mantissa, exponent, placement):
    places = lax.axis_size("expert")
    place = lax.axis_index("expert")
    steps, rows, width = residual.shape
    count = steps * rows
    units = mantissa.shape[1]
    turns = partners(places)
    both = ("expert", "tensor")

    partial = attend(lengths, queries, new_kv, cache_kv, out_proj)
    mantissa = mantissa[0].transpose(1, 0, 2)
    exponent = exponent.transpose(2, 3, 0, 1).reshape(-1, 1, units)
    tile = place * (units // TILE_UNITS) + jnp.arange(units) // TILE_UNITS
    member = jnp.any(placement.reshape(EXPERTS, -1, 1) == tile, axis=1).astype(BF16)

    mixed, packed = normalize(residual, partial, swap(partial), routing.reshape(count, TOP), router)
    near = [lax.ppermute(packed, both, pairs) for pairs in turns]
    weights = dequantize(packed, mantissa, exponent)
    near, weights = lax.optimization_barrier((near, weights))
    far = [swap(block) for block in near]
    mine, other = run_experts(weights, member, near + far)
    sums = join(mine, swap(other), count)
    back = [
        lax.ppermute(block, both, [(to, back) for back, to in pairs]) for block, pairs in zip(sums, turns)
    ]
    total = sum(block.astype(F32) for block in back)
    return last(mixed, total, swap(total), residual.shape)


def solution(mesh):
    placed = (
        P(None, ("group", "expert"), None),
        P(None, ("group", "expert"), "tensor"),
        P(None, ("group", "expert"), None, "tensor"),
        P(("group", "expert"), None, None, "tensor"),
        P(("group", "expert")),
        P(None, ("group", "expert"), None),
        P(),
        P("tensor", None),
        P("tensor", "expert", None, None),
        P("tensor", "expert", None, None),
        P("group"),
    )
    return jax.shard_map(
        per_device,
        mesh=mesh,
        in_specs=placed,
        out_specs=P(None, ("group", "expert"), None),
        check_vma=False,
    )
```

time: 70 us -> 49.1 us (0.70)
  Pallas kernels: 29.8 us -> 16.8 us
  local copies, waits for them, and re-layouts: 7.34 us -> 0.83 us
  starting transfers between devices: 23.2 us -> 20.7 us
  waiting for transfers between devices: 7.42 us -> 9.86 us
  other arithmetic: 1.82 us -> 0.6 us
    pallas_call x4 -> x6, Pallas kernels: 29.8 us -> 16.8 us  [the longest x1 6.28 us: dequantize(): pl.pallas_call(functools.partial(weights_kernel, step), out_shape=(vmem((...]
    reshape x3 -> x0, local copies, waits for them, and re-layouts: 2.82 us -> none  [the longest x1 1.47 us: attend(): queries.reshape(count, width)]
    unnamed x27 -> x12, local copies, waits for them, and re-layouts: 2.42 us -> 0.75 us
    ppermute x4, waiting for transfers between devices: 4.09 us -> 5.61 us  [per_device(): lax.ppermute(block, both, [(to, back) for back, to in pairs])]
    pad x1 -> x0, local copies, waits for them, and re-layouts: 1.3 us -> none  [attend(): fresh = jnp.pad(fresh, ((0, -fresh.shape[0] % LANES), (0, 0)))]
    another operation x1 -> x0, other arithmetic: 1.19 us -> none
    ppermute x7, starting transfers between devices: 12.5 us -> 11.3 us  [swap(): return lax.ppermute(value, 'tensor', [(0, 1), (1, 0)])]
    ppermute x7, waiting for transfers between devices: 3.32 us -> 4.24 us  [swap(): return lax.ppermute(value, 'tensor', [(0, 1), (1, 0)])]
  transfers between devices with their start and end apart: 15 -> 15, of which waited for: 5 -> 9; matrix products, arithmetic and copies ran while one was open for 4% -> 1% of each run, Pallas kernels for 17% -> 13%
where the time goes in v2:
time: 49.1 us; the launch traced here: 48.9 us
  starting transfers between devices  20.7 us (42%)
  Pallas kernels  16.8 us (34%)
  waiting for transfers between devices  9.86 us (20%)
  local copies, waits for them, and re-layouts  0.83 us (2%)
  other arithmetic  0.6 us (1%)
    ppermute x7, starting transfers between devices, swap(): return lax.ppermute(value, 'tensor', [(0, 1), (1, 0)])  11.3 us
    pallas_call x1, Pallas kernels, dequantize(): pl.pallas_call(functools.partial(weights_kernel, step), out_shape=(vmem((...  6.28 us
    ppermute x4, waiting for transfers between devices, per_device(): lax.ppermute(block, both, [(to, back) for back, to in pairs])  5.61 us
    pallas_call x1, Pallas kernels, attend(): pl.pallas_call(attention_kernel, out_shape=vmem((count, model_width), F32...  5.44 us
    ppermute x4, starting transfers between devices, per_device(): near = [lax.ppermute(packed, both, pairs) for pairs in turns]  5.18 us
    ppermute x7, waiting for transfers between devices, swap(): return lax.ppermute(value, 'tensor', [(0, 1), (1, 0)])  4.24 us
    ppermute x4, starting transfers between devices, per_device(): lax.ppermute(block, both, [(to, back) for back, to in pairs])  4.22 us
    pallas_call x1, Pallas kernels, run_experts(): pl.pallas_call(experts_kernel, out_shape=(vmem((count // 2, width), F32),...  3.84 us
  transfers between devices with their start and end apart: 15, of which 9 were waited for; matrix products, arithmetic and copies ran while one was open for 1% of the time, Pallas kernels for 13%

profile of v2, /device:TPU:0, one launch (start us, length us, event | category | flops | bytes accessed | tf_op | source)
XLA Modules:
  0.0 48.9 jit_solution(16186037107177389585)
XLA Ops:
  0.0 0.7 %copy-done.4 = s32[4]{0:T(128)S(1)} copy-done((s32[4]{0:T(128)S(1)}, s32[4]{0:T(128)}, u32[]{:S(2)}) %copy-start.4) | copy-done | bytes 40
  0.7 5.4 %attention.1.mine_ref = f32[16,2880]{1,0:T(8,128)S(1)} custom-call(s32[4]{0:T(128)S(1)} %copy-done.4, bf16[4,4,1024]{2,1,0:T(4,128)(2,1)} %queries_hbm.1, bf16[32,128]{1,0:T(8,128)(2,1)} %bitcast.17, bf16[4,512,128]{2,1,0:T(8,128)(2,1)} %bitcast.16, bf16[2880,1024]{1,0:T(8,128)(2,1)} %bitcast.15), custom_call_target="tpu_custom_call" | custom-call | flops 94371840 | bytes 7340032 | tf_op jit(solution)/shard_map/attention/pallas_call | solution.py:141
  6.2 0.5 %collective-permute-start = (f32[16,2880]{1,0:T(8,128)S(1)}, f32[16,2880]{1,0:T(8,128)S(1)}, u32[]{:S(2)}, u32[]{:S(2)}) collective-permute-start(f32[16,2880]{1,0:T(8,128)S(1)} %attention.1.mine_ref), channel_id=1, source_target_pairs={{0,1},{1,0},{2,3},{3,2},{4,5},{5,4},{6,7},{7,6},{8,9},{9,8},{10,11... | collective-permute-start | bytes 552968 | tf_op jit(solution)/shard_map/ppermute | solution.py:341
  6.8 1.0 %collective-permute-done.other_ref = f32[16,2880]{1,0:T(8,128)S(1)} collective-permute-done((f32[16,2880]{1,0:T(8,128)S(1)}, f32[16,2880]{1,0:T(8,128)S(1)}, u32[]{:S(2)}, u32[]{:S(2)}) %collective-permute-start) | collective-permute-done | bytes 184352 | tf_op jit(solution)/shard_map/ppermute | solution.py:341
  7.8 0.5 %normalize.1 = (f32[16,2880]{1,0:T(8,128)S(1)}, bf16[16,2944]{1,0:T(8,128)(2,1)S(1)}) custom-call(bf16[4,4,2880]{2,1,0:T(4,128)(2,1)S(1)} %copy-done.1, f32[16,2880]{1,0:T(8,128)S(1)} %attention.1.mine_ref, f32[16,2880]{1,0:T(8,128)S(1)} %collective-permute-done.other_ref, s32[16,4]{1,0:T(8,128)S(1)} %bitcast.13, bf16[8,2880]{1,0:T(8,128)(2,1)S(1)} %bitcast.12), custom_call_target="tpu_custom_call" | custom-call | tf_op jit(solution)/shard_map/normalize/pallas_call | solution.py:193
  8.3 3.9 %collective-permute-start.4 = (bf16[16,2944]{1,0:T(8,128)(2,1)S(1)}, bf16[16,2944]{1,0:T(8,128)(2,1)S(1)}, u32[]{:S(2)}, u32[]{:S(2)}) collective-permute-start(bf16[16,2944]{1,0:T(8,128)(2,1)S(1)} %get-tuple-element.24.packed_ref), channel_id=1, source_target_pairs={{0,6},{1,15},{2,4},{3,13},{4,2},{5,11},{6,0},{7,9},{8,14},{9,7},{1... | collective-permute-start | bytes 282632 | tf_op jit(solution)/shard_map/ppermute | solution.py:374
  12.2 0.4 collective-permute-start.3
  12.8 0.7 %collective-permute-start.1 = (bf16[16,2944]{1,0:T(8,128)(2,1)S(1)}, bf16[16,2944]{1,0:T(8,128)(2,1)S(1)}, u32[]{:S(2)}, u32[]{:S(2)}) collective-permute-start(bf16[16,2944]{1,0:T(8,128)(2,1)S(1)} %get-tuple-element.24.packed_ref), channel_id=1, source_target_pairs={{0,0},{1,9},{2,2},{3,11},{4,4},{5,13},{6,6},{7,15},{8,8},{9,1},{10... | collective-permute-start | bytes 282632 | tf_op jit(solution)/shard_map/ppermute | solution.py:374
  13.5 6.3 %weights.1 = (bf16[720,2880]{1,0:T(8,128)(2,1)S(1)}, bf16[720,2880]{1,0:T(8,128)(2,1)S(1)}, bf16[720,2880]{1,0:T(8,128)(2,1)S(1)}) custom-call(bf16[16,2944]{1,0:T(8,128)(2,1)S(1)} %get-tuple-element.24.packed_ref, bf16[3,720,2880]{2,1,0:T(8,128)(2,1)} %bitcast.14, s32[270,1,720]{2,1,0:T(1,128)S(1)} %bitcast.11), custom_call_target="tpu_custom_call" | custom-call | flops 1119744000 | bytes 12441600 | tf_op jit(solution)/shard_map/weights/pallas_call | solution.py:233
  19.8 5.0 %collective-permute-start.5 = (bf16[16,2944]{1,0:T(8,128)(2,1)S(1)}, bf16[16,2944]{1,0:T(8,128)(2,1)S(1)}, u32[]{:S(2)}, u32[]{:S(2)}) collective-permute-start(bf16[16,2944]{1,0:T(8,128)(2,1)S(1)} %collective-permute-done.1.refs_0_), channel_id=1, source_target_pairs={{0,1},{1,0},{2,3},{3,2},{4,5},{5,4},{6,7},{7,6},{8,9},{9,8},{10,11... | collective-permute-start | bytes 282632 | tf_op jit(solution)/shard_map/ppermute | solution.py:341
  24.9 0.4 collective-permute-start.7
  25.4 0.5 %compare_reduce_fusion = pred[8,720]{1,0:T(8,128)(4,1)S(1)} fusion(s32[720]{0:T(1024)S(1)} %fusion, s32[8,120]{1,0:T(8,128)S(1)} %eq.15), kind=kLoop, calls=%fused_computation | loop fusion | flops 1376640 | bytes 12480 | tf_op jit(solution)/shard_map/reduce_or | solution.py:371
  26.6 3.8 %experts.1 = (f32[64,2880]{1,0:T(8,128)S(1)}, bf16[64,2880]{1,0:T(8,128)(2,1)S(1)}) custom-call(bf16[720,2880]{1,0:T(8,128)(2,1)S(1)} %get-tuple-element.28.gate_ref, bf16[720,2880]{1,0:T(8,128)(2,1)S(1)} %get-tuple-element.29.up_ref, bf16[720,2880]{1,0:T(8,128)(2,1)S(1)} %get-tuple-element.30.down_ref, bf16[8,720]{1,0:T(8,128)(2,1)S(1)} %convert_element_type.15.member_ref, ...), custom_call_target="tpu_custom_call" | custom-call | flops 1592524800 | bytes 12441600 | tf_op jit(solution)/shard_map/experts/pallas_call | solution.py:289
  30.7 1.5 %collective-permute-done.9.other_ref = bf16[64,2880]{1,0:T(8,128)(2,1)S(1)} collective-permute-done((bf16[64,2880]{1,0:T(8,128)(2,1)S(1)}, bf16[64,2880]{1,0:T(8,128)(2,1)S(1)}, u32[]{:S(2)}, u32[]{:S(2)}) %collective-permute-start.9) | collective-permute-done | bytes 368672 | tf_op jit(solution)/shard_map/ppermute | solution.py:341
  32.3 0.7 %collective-permute-start.10 = (bf16[16,2880]{1,0:T(8,128)(2,1)S(1)}, bf16[16,2880]{1,0:T(8,128)(2,1)S(1)}, u32[]{:S(2)}, u32[]{:S(2)}) collective-permute-start(bf16[16,2880]{1,0:T(8,128)(2,1)S(1)} %get-tuple-element.37), channel_id=1, source_target_pairs={{0,0},{9,1},{2,2},{11,3},{4,4},{13,5},{6,6},{15,7},{8,8},{1,9},{10... | collective-permute-start | bytes 276488 | tf_op jit(solution)/shard_map/ppermute | solution.py:381
  33.0 1.5 %collective-permute-start.11 = (bf16[16,2880]{1,0:T(8,128)(2,1)S(1)}, bf16[16,2880]{1,0:T(8,128)(2,1)S(1)}, u32[]{:S(2)}, u32[]{:S(2)}) collective-permute-start(bf16[16,2880]{1,0:T(8,128)(2,1)S(1)} %get-tuple-element.38), channel_id=1, source_target_pairs={{2,0},{11,1},{0,2},{9,3},{6,4},{15,5},{4,6},{13,7},{10,8},{3,9},{8... | collective-permute-start | bytes 276488 | tf_op jit(solution)/shard_map/ppermute | solution.py:381
  34.5 1.5 %collective-permute-start.12 = (bf16[16,2880]{1,0:T(8,128)(2,1)S(1)}, bf16[16,2880]{1,0:T(8,128)(2,1)S(1)}, u32[]{:S(2)}, u32[]{:S(2)}) collective-permute-start(bf16[16,2880]{1,0:T(8,128)(2,1)S(1)} %get-tuple-element.39), channel_id=1, source_target_pairs={{4,0},{13,1},{6,2},{15,3},{0,4},{9,5},{2,6},{11,7},{12,8},{5,9},{1... | collective-permute-start | bytes 276488 | tf_op jit(solution)/shard_map/ppermute | solution.py:381
  36.0 0.6 %collective-permute-start.13 = (bf16[16,2880]{1,0:T(8,128)(2,1)S(1)}, bf16[16,2880]{1,0:T(8,128)(2,1)S(1)}, u32[]{:S(2)}, u32[]{:S(2)}) collective-permute-start(bf16[16,2880]{1,0:T(8,128)(2,1)S(1)} %get-tuple-element.40), channel_id=1, source_target_pairs={{6,0},{15,1},{4,2},{13,3},{2,4},{11,5},{0,6},{9,7},{14,8},{7,9},{1... | collective-permute-start | bytes 276488 | tf_op jit(solution)/shard_map/ppermute | solution.py:381
  36.5 1.1 %collective-permute-done.11 = bf16[16,2880]{1,0:T(8,128)(2,1)S(1)} collective-permute-done((bf16[16,2880]{1,0:T(8,128)(2,1)S(1)}, bf16[16,2880]{1,0:T(8,128)(2,1)S(1)}, u32[]{:S(2)}, u32[]{:S(2)}) %collective-permute-start.11) | collective-permute-done | bytes 92192 | tf_op jit(solution)/shard_map/ppermute | solution.py:381
  37.6 2.3 %collective-permute-done.12 = bf16[16,2880]{1,0:T(8,128)(2,1)S(1)} collective-permute-done((bf16[16,2880]{1,0:T(8,128)(2,1)S(1)}, bf16[16,2880]{1,0:T(8,128)(2,1)S(1)}, u32[]{:S(2)}, u32[]{:S(2)}) %collective-permute-start.12) | collective-permute-done | bytes 92192 | tf_op jit(solution)/shard_map/ppermute | solution.py:381
  39.9 2.2 %collective-permute-done.13 = bf16[16,2880]{1,0:T(8,128)(2,1)S(1)} collective-permute-done((bf16[16,2880]{1,0:T(8,128)(2,1)S(1)}, bf16[16,2880]{1,0:T(8,128)(2,1)S(1)}, u32[]{:S(2)}, u32[]{:S(2)}) %collective-permute-start.13) | collective-permute-done | bytes 92192 | tf_op jit(solution)/shard_map/ppermute | solution.py:381
  42.2 5.0 %collective-permute-start.14 = (f32[16,2880]{1,0:T(8,128)S(1)}, f32[16,2880]{1,0:T(8,128)S(1)}, u32[]{:S(2)}, u32[]{:S(2)}) collective-permute-start(f32[16,2880]{1,0:T(8,128)S(1)} %convert_add_fusion.mine_ref), channel_id=1, source_target_pairs={{0,1},{1,0},{2,3},{3,2},{4,5},{5,4},{6,7},{7,6},{8,9},{9,8},{10,11... | collective-permute-start | bytes 552968 | tf_op jit(solution)/shard_map/ppermute | solution.py:341
  47.2 1.1 %collective-permute-done.14.other_ref = f32[16,2880]{1,0:T(8,128)S(1)} collective-permute-done((f32[16,2880]{1,0:T(8,128)S(1)}, f32[16,2880]{1,0:T(8,128)S(1)}, u32[]{:S(2)}, u32[]{:S(2)}) %collective-permute-start.14) | collective-permute-done | bytes 184352 | tf_op jit(solution)/shard_map/ppermute | solution.py:341
  48.3 0.7 %last.1 = bf16[4,4,2880]{2,1,0:T(4,128)(2,1)} custom-call(f32[16,2880]{1,0:T(8,128)S(1)} %get-tuple-element.23.mixed_ref, f32[16,2880]{1,0:T(8,128)S(1)} %convert_add_fusion.mine_ref, f32[16,2880]{1,0:T(8,128)S(1)} %collective-permute-done.14.other_ref), custom_call_target="tpu_custom_call" | custom-call | tf_op jit(solution)/shard_map/last/pallas_call | solution.py:330
  (29 shorter events, 1.4 us)
Async XLA Ops:
  0.0 7.8 %copy-start.2 = (bf16[2880,8]{0,1:T(8,128)(2,1)S(1)}, bf16[2880,8]{0,1:T(8,128)(2,1)}, u32[]{:S(2)}) copy-start(bf16[2880,8]{0,1:T(8,128)(2,1)} %param.17) | copy-start | bytes 138244
  0.0 7.8 %copy-start.3 = (s32[4,4,4]{2,1,0:T(4,128)S(1)}, s32[4,4,4]{2,1,0:T(4,128)}, u32[]{:S(2)}) copy-start(s32[4,4,4]{2,1,0:T(4,128)} %param.16) | copy-start | bytes 772
  0.0 7.8 %copy-start.1 = (bf16[4,4,2880]{2,1,0:T(4,128)(2,1)S(1)}, bf16[4,4,2880]{2,1,0:T(4,128)(2,1)}, u32[]{:S(2)}) copy-start(bf16[4,4,2880]{2,1,0:T(4,128)(2,1)} %residual_ref.1) | copy-start | bytes 276484
  0.0 13.5 %copy-start = (s32[1,720,3,90]{1,0,3,2:T(1,128)S(1)}, s32[1,720,3,90]{1,0,3,2:T(1,128)}, u32[]{:S(2)}) copy-start(s32[1,720,3,90]{1,0,3,2:T(1,128)} %param.20) | copy-start | bytes 2332804
  0.0 0.7 %copy-start.4 = (s32[4]{0:T(128)S(1)}, s32[4]{0:T(128)}, u32[]{:S(2)}) copy-start(s32[4]{0:T(128)} %lengths_ref.1) | copy-start | bytes 52
  0.7 6.0 %copy-start.5 = (s32[960]{0:T(1024)S(1)}, s32[960]{0:T(1024)}, u32[]{:S(2)}) copy-start(s32[960]{0:T(1024)} %param.21) | copy-start | bytes 11524
  6.2 1.6 %collective-permute-start = (f32[16,2880]{1,0:T(8,128)S(1)}, f32[16,2880]{1,0:T(8,128)S(1)}, u32[]{:S(2)}, u32[]{:S(2)}) collective-permute-start(f32[16,2880]{1,0:T(8,128)S(1)} %attention.1.mine_ref), channel_id=1, source_target_pairs={{0,1},{1,0},{2,3},{3,2},{4,5},{5,4},{6,7},{7,6},{8,9},{9,8},{10,11... | collective-permute-start | bytes 552968 | tf_op jit(solution)/shard_map/ppermute | solution.py:341
  8.3 11.5 %collective-permute-start.4 = (bf16[16,2944]{1,0:T(8,128)(2,1)S(1)}, bf16[16,2944]{1,0:T(8,128)(2,1)S(1)}, u32[]{:S(2)}, u32[]{:S(2)}) collective-permute-start(bf16[16,2944]{1,0:T(8,128)(2,1)S(1)} %get-tuple-element.24.packed_ref), channel_id=1, source_target_pairs={{0,6},{1,15},{2,4},{3,13},{4,2},{5,11},{6,0},{7,9},{8,14},{9,7},{1... | collective-permute-start | bytes 282632 | tf_op jit(solution)/shard_map/ppermute | solution.py:374
  12.2 7.6 %collective-permute-start.3 = (bf16[16,2944]{1,0:T(8,128)(2,1)S(1)}, bf16[16,2944]{1,0:T(8,128)(2,1)S(1)}, u32[]{:S(2)}, u32[]{:S(2)}) collective-permute-start(bf16[16,2944]{1,0:T(8,128)(2,1)S(1)} %get-tuple-element.24.packed_ref), channel_id=1, source_target_pairs={{0,4},{1,13},{2,6},{3,15},{4,0},{5,9},{6,2},{7,11},{8,12},{9,5},{1... | collective-permute-start | bytes 282632 | tf_op jit(solution)/shard_map/ppermute | solution.py:374
  12.7 7.1 %collective-permute-start.2 = (bf16[16,2944]{1,0:T(8,128)(2,1)S(1)}, bf16[16,2944]{1,0:T(8,128)(2,1)S(1)}, u32[]{:S(2)}, u32[]{:S(2)}) collective-permute-start(bf16[16,2944]{1,0:T(8,128)(2,1)S(1)} %get-tuple-element.24.packed_ref), channel_id=1, source_target_pairs={{0,2},{1,11},{2,0},{3,9},{4,6},{5,15},{6,4},{7,13},{8,10},{9,3},{1... | collective-permute-start | bytes 282632 | tf_op jit(solution)/shard_map/ppermute | solution.py:374
  12.8 7.0 %collective-permute-start.1 = (bf16[16,2944]{1,0:T(8,128)(2,1)S(1)}, bf16[16,2944]{1,0:T(8,128)(2,1)S(1)}, u32[]{:S(2)}, u32[]{:S(2)}) collective-permute-start(bf16[16,2944]{1,0:T(8,128)(2,1)S(1)} %get-tuple-element.24.packed_ref), channel_id=1, source_target_pairs={{0,0},{1,9},{2,2},{3,11},{4,4},{5,13},{6,6},{7,15},{8,8},{9,1},{10... | collective-permute-start | bytes 282632 | tf_op jit(solution)/shard_map/ppermute | solution.py:374
  19.8 6.1 %collective-permute-start.5 = (bf16[16,2944]{1,0:T(8,128)(2,1)S(1)}, bf16[16,2944]{1,0:T(8,128)(2,1)S(1)}, u32[]{:S(2)}, u32[]{:S(2)}) collective-permute-start(bf16[16,2944]{1,0:T(8,128)(2,1)S(1)} %collective-permute-done.1.refs_0_), channel_id=1, source_target_pairs={{0,1},{1,0},{2,3},{3,2},{4,5},{5,4},{6,7},{7,6},{8,9},{9,8},{10,11... | collective-permute-start | bytes 282632 | tf_op jit(solution)/shard_map/ppermute | solution.py:341
  24.8 1.3 %collective-permute-start.6 = (bf16[16,2944]{1,0:T(8,128)(2,1)S(1)}, bf16[16,2944]{1,0:T(8,128)(2,1)S(1)}, u32[]{:S(2)}, u32[]{:S(2)}) collective-permute-start(bf16[16,2944]{1,0:T(8,128)(2,1)S(1)} %collective-permute-done.2.refs_1_), channel_id=1, source_target_pairs={{0,1},{1,0},{2,3},{3,2},{4,5},{5,4},{6,7},{7,6},{8,9},{9,8},{10,11... | collective-permute-start | bytes 282632 | tf_op jit(solution)/shard_map/ppermute | solution.py:341
  24.9 1.4 %collective-permute-start.7 = (bf16[16,2944]{1,0:T(8,128)(2,1)S(1)}, bf16[16,2944]{1,0:T(8,128)(2,1)S(1)}, u32[]{:S(2)}, u32[]{:S(2)}) collective-permute-start(bf16[16,2944]{1,0:T(8,128)(2,1)S(1)} %collective-permute-done.3.refs_2_), channel_id=1, source_target_pairs={{0,1},{1,0},{2,3},{3,2},{4,5},{5,4},{6,7},{7,6},{8,9},{9,8},{10,11... | collective-permute-start | bytes 282632 | tf_op jit(solution)/shard_map/ppermute | solution.py:341
  25.3 1.3 %collective-permute-start.8 = (bf16[16,2944]{1,0:T(8,128)(2,1)S(1)}, bf16[16,2944]{1,0:T(8,128)(2,1)S(1)}, u32[]{:S(2)}, u32[]{:S(2)}) collective-permute-start(bf16[16,2944]{1,0:T(8,128)(2,1)S(1)} %collective-permute-done.4.refs_3_), channel_id=1, source_target_pairs={{0,1},{1,0},{2,3},{3,2},{4,5},{5,4},{6,7},{7,6},{8,9},{9,8},{10,11... | collective-permute-start | bytes 282632 | tf_op jit(solution)/shard_map/ppermute | solution.py:341
  30.5 1.8 %collective-permute-start.9 = (bf16[64,2880]{1,0:T(8,128)(2,1)S(1)}, bf16[64,2880]{1,0:T(8,128)(2,1)S(1)}, u32[]{:S(2)}, u32[]{:S(2)}) collective-permute-start(bf16[64,2880]{1,0:T(8,128)(2,1)S(1)} %get-tuple-element.36), channel_id=1, source_target_pairs={{0,1},{1,0},{2,3},{3,2},{4,5},{5,4},{6,7},{7,6},{8,9},{9,8},{10,11... | collective-permute-start | bytes 1105928 | tf_op jit(solution)/shard_map/ppermute | solution.py:341
  32.3 4.2 %collective-permute-start.10 = (bf16[16,2880]{1,0:T(8,128)(2,1)S(1)}, bf16[16,2880]{1,0:T(8,128)(2,1)S(1)}, u32[]{:S(2)}, u32[]{:S(2)}) collective-permute-start(bf16[16,2880]{1,0:T(8,128)(2,1)S(1)} %get-tuple-element.37), channel_id=1, source_target_pairs={{0,0},{9,1},{2,2},{11,3},{4,4},{13,5},{6,6},{15,7},{8,8},{1,9},{10... | collective-permute-start | bytes 276488 | tf_op jit(solution)/shard_map/ppermute | solution.py:381
  33.0 4.6 %collective-permute-start.11 = (bf16[16,2880]{1,0:T(8,128)(2,1)S(1)}, bf16[16,2880]{1,0:T(8,128)(2,1)S(1)}, u32[]{:S(2)}, u32[]{:S(2)}) collective-permute-start(bf16[16,2880]{1,0:T(8,128)(2,1)S(1)} %get-tuple-element.38), channel_id=1, source_target_pairs={{2,0},{11,1},{0,2},{9,3},{6,4},{15,5},{4,6},{13,7},{10,8},{3,9},{8... | collective-permute-start | bytes 276488 | tf_op jit(solution)/shard_map/ppermute | solution.py:381
  34.5 5.4 %collective-permute-start.12 = (bf16[16,2880]{1,0:T(8,128)(2,1)S(1)}, bf16[16,2880]{1,0:T(8,128)(2,1)S(1)}, u32[]{:S(2)}, u32[]{:S(2)}) collective-permute-start(bf16[16,2880]{1,0:T(8,128)(2,1)S(1)} %get-tuple-element.39), channel_id=1, source_target_pairs={{4,0},{13,1},{6,2},{15,3},{0,4},{9,5},{2,6},{11,7},{12,8},{5,9},{1... | collective-permute-start | bytes 276488 | tf_op jit(solution)/shard_map/ppermute | solution.py:381
  36.0 6.2 %collective-permute-start.13 = (bf16[16,2880]{1,0:T(8,128)(2,1)S(1)}, bf16[16,2880]{1,0:T(8,128)(2,1)S(1)}, u32[]{:S(2)}, u32[]{:S(2)}) collective-permute-start(bf16[16,2880]{1,0:T(8,128)(2,1)S(1)} %get-tuple-element.40), channel_id=1, source_target_pairs={{6,0},{15,1},{4,2},{13,3},{2,4},{11,5},{0,6},{9,7},{14,8},{7,9},{1... | collective-permute-start | bytes 276488 | tf_op jit(solution)/shard_map/ppermute | solution.py:381
  42.2 6.0 %collective-permute-start.14 = (f32[16,2880]{1,0:T(8,128)S(1)}, f32[16,2880]{1,0:T(8,128)S(1)}, u32[]{:S(2)}, u32[]{:S(2)}) collective-permute-start(f32[16,2880]{1,0:T(8,128)S(1)} %convert_add_fusion.mine_ref), channel_id=1, source_target_pairs={{0,1},{1,0},{2,3},{3,2},{4,5},{5,4},{6,7},{7,6},{8,9},{9,8},{10,11... | collective-permute-start | bytes 552968 | tf_op jit(solution)/shard_map/ppermute | solution.py:341

commit v3 on v2

--- a/solution.py
+++ b/solution.py
@@ -51,27 +51,33 @@
 
 
 def attention_kernel(
-    lengths_ref,
+    lengths_hbm,
     queries_hbm,
     fresh_hbm,
     cache_hbm,
     proj_hbm,
     out_ref,
+    lengths,
     queries,
     fresh_rows,
     cache_rows,
     proj,
+    spread,
     packed,
     mixed,
     sems,
 ):
-    late_width = fresh_hbm.shape[0]
-    fresh_rows[...] = jnp.zeros_like(fresh_rows)
     moves = [
-        pltpu.make_async_copy(queries_hbm, queries, sems.at[0]),
-        pltpu.make_async_copy(fresh_hbm, fresh_rows.at[:late_width], sems.at[1]),
-        pltpu.make_async_copy(cache_hbm, cache_rows, sems.at[2]),
-        pltpu.make_async_copy(proj_hbm, proj, sems.at[3]),
+        pltpu.make_async_copy(source, target, sems.at[place])
+        for place, (source, target) in enumerate(
+            (
+                (queries_hbm, queries),
+                (lengths_hbm, lengths),
+                (fresh_hbm, fresh_rows),
+                (cache_hbm, cache_rows),
+                (proj_hbm, proj),
+            )
+        )
     ]
     for move in moves:
         move.start()
@@ -90,33 +96,37 @@
             first += groups * count
             packed[first : first + rows, :] = jnp.where(mine, pltpu.roll(piece, HD, 1), 0.0)
     amount = 2 * groups * steps
-    span = cache_rows.shape[1]
-    width = fresh_rows.shape[0]
+    span = cache_rows.shape[1] // 2
     spot = iota((amount, span), 1)
-    step_of = iota((amount, width), 0) % steps
-    fresh_spot = iota((amount, width), 1)
-    fresh_step = fresh_spot // (2 * rows)
-    moves[1].wait()
-    moves[2].wait()
-    fresh = fresh_rows[...]
+    step_of = iota((amount, count), 0) % steps
+    fresh_spot = iota((amount, count), 1)
+    for move in moves[1:4]:
+        move.wait()
+
+    def apart(value, which):
+        size = value.shape[0]
+        here = spread.at[which, :size]
+        here[...] = value.astype(F32)
+        return tuple(
+            spread[which, pl.ds(first, size // 2, stride=2), :].astype(BF16) for first in range(2)
+        )
+
+    fresh_keys, fresh_values = apart(fresh_rows[...], rows)
     for row in range(rows):
         now = packed[pl.ds(row, amount, stride=rows), :].astype(BF16)
-        cache = cache_rows[row]
-        scores = dot(now, cache, NT)
-        live = (spot % 2 == 0) & (spot < 2 * lengths_ref[row])
-        scores = jnp.where(live, scores, -1e30)
-        late = dot(now, fresh, NT)
-        seen = (fresh_spot % (2 * rows) == 2 * row) & (fresh_step <= step_of)
-        late = jnp.where(seen, late, -1e30)
+        keys, values = apart(cache_rows[row], row)
+        scores = jnp.where(spot < lengths[row], dot(now, keys, NT), -1e30)
+        seen = (fresh_spot % rows == row) & (fresh_spot // rows <= step_of)
+        late = jnp.where(seen, dot(now, fresh_keys, NT), -1e30)
         highest = jnp.maximum(
             jnp.max(scores, axis=1, keepdims=True), jnp.max(late, axis=1, keepdims=True)
         )
         scores = jnp.exp(scores - highest)
         late = jnp.exp(late - highest)
         total = jnp.sum(scores, axis=1, keepdims=True) + jnp.sum(late, axis=1, keepdims=True)
-        probs = pltpu.roll(scores / total, 1, 1).astype(BF16)
-        late_probs = pltpu.roll(late / total, 1, 1).astype(BF16)
-        mixed[pl.ds(row, amount, stride=rows), :] = dot(probs, cache) + dot(late_probs, fresh)
+        probs = (scores / total).astype(BF16)
+        late_probs = (late / total).astype(BF16)
+        mixed[pl.ds(row, amount, stride=rows), :] = dot(probs, values) + dot(late_probs, fresh_values)
     heads = []
     lane = iota((count, LANES), 1)
     for group in range(groups):
@@ -124,7 +134,7 @@
         turned = mixed[(groups + group) * count : (groups + group + 1) * count, :]
         mine = (lane < HD) == (group < half)
         heads.append(jnp.where(mine, straight, pltpu.roll(turned, HD, 1)).astype(BF16))
-    moves[3].wait()
+    moves[4].wait()
     out_ref[...] = dot(jnp.concatenate(heads, axis=1), proj[...], NT)
 
 
@@ -137,27 +147,28 @@
     groups = width // LANES
     fresh = new_kv.reshape(count * 2, LANES)
     cache = cache_kv.reshape(rows, 2 * span, LANES)
-    padded = -(-fresh.shape[0] // LANES) * LANES
     return pl.pallas_call(
         attention_kernel,
         out_shape=vmem((count, model_width), F32),
-        in_specs=[pl.BlockSpec(memory_space=pltpu.SMEM)] + [pl.BlockSpec(memory_space=pltpu.HBM)] * 4,
+        in_specs=[pl.BlockSpec(memory_space=pltpu.HBM)] * 5,
         out_specs=pl.BlockSpec(memory_space=pltpu.VMEM),
         scratch_shapes=[
+            pltpu.SMEM(lengths.shape, jnp.int32),
             pltpu.VMEM(queries.shape, BF16),
-            pltpu.VMEM((padded, LANES), BF16),
+            pltpu.VMEM(fresh.shape, BF16),
             pltpu.VMEM(cache.shape, BF16),
             pltpu.VMEM(proj.shape, BF16),
+            pltpu.VMEM((rows + 1, 2 * span, LANES), F32),
             pltpu.VMEM((2 * groups * count, LANES), F32),
             pltpu.VMEM((2 * groups * count, LANES), F32),
-            pltpu.SemaphoreType.DMA((4,)),
+            pltpu.SemaphoreType.DMA((5,)),
         ],
         compiler_params=params(16),
         cost_estimate=pl.CostEstimate(
             flops=2 * count * width * model_width, bytes_accessed=7 << 20, transcendentals=0
         ),
         name="attention",
-    )(lengths, afar(queries), afar(fresh), afar(cache), afar(proj))
+    )(afar(lengths), afar(queries), afar(fresh), afar(cache), afar(proj))
 
 
 def norm_kernel(residual_ref, mine_ref, other_ref, routing_ref, router_ref, mixed_ref, packed_ref):
@@ -241,9 +252,7 @@
             pltpu.SemaphoreType.DMA((parts * units // step,)),
         ],
         compiler_params=params(14),
-        cost_estimate=pl.CostEstimate(
-            flops=2 * parts * units * blocks * width, bytes_accessed=2 * parts * units * width, transcendentals=0
-        ),
+        cost_estimate=pl.CostEstimate(flops=1000, bytes_accessed=1000, transcendentals=0),
         name="weights",
     )(held(packed), afar(mantissa), held(exponent))
 
@@ -342,17 +351,14 @@
 
 
 def partners(count):
-    half = count // 2
     power = count & (count - 1) == 0
     reach = lambda place, far: place ^ far if power else (place + far) % count
-    turns = []
-    for turn in range(half):
-        pairs = []
-        for place in range(count):
-            pairs.append((2 * place, 2 * reach(place, turn)))
-            pairs.append((2 * place + 1, 2 * reach(place, turn + half) + 1))
-        turns.append(pairs)
-    return turns
+    far = sorted(range(count), key=lambda k: (k.bit_count() % 2, -k))
+    half = count // 2
+    return [
+        [(2 * place + core, 2 * reach(place, far[turn + core * half]) + core) for place in range(count) for core in range(2)]
+        for turn in range(half)
+    ]
 
 
 def per_device(residual, queries, new_kv, cache_kv, lengths, routing, router, out_proj, mantissa, exponent, placement):
@@ -373,7 +379,8 @@
     mixed, packed = normalize(residual, partial, swap(partial), routing.reshape(count, TOP), router)
     near = [lax.ppermute(packed, both, pairs) for pairs in turns]
     weights = dequantize(packed, mantissa, exponent)
-    near, weights = lax.optimization_barrier((near, weights))
+    near, weights = lax.optimization_barrier((near[::-1], weights))
+    near = near[::-1]
     far = [swap(block) for block in near]
     mine, other = run_experts(weights, member, near + far)
     sums = join(mine, swap(other), count)

time: 49.1 us -> 44 us (0.90)
  starting transfers between devices: 20.7 us -> 15.2 us
  waiting for transfers between devices: 9.86 us -> 11.8 us
  Pallas kernels: 16.8 us -> 16 us
  local copies, waits for them, and re-layouts: 0.83 us -> 0.09 us
    ppermute x7, starting transfers between devices: 11.3 us -> 2.05 us  [swap(): return lax.ppermute(value, 'tensor', [(0, 1), (1, 0)])]
    ppermute x4, starting transfers between devices: 5.18 us -> 7.15 us  [per_device(): near = [lax.ppermute(packed, both, pairs) for pairs in turns]]
    ppermute x4, starting transfers between devices: 4.22 us -> 6.01 us  [per_device(): lax.ppermute(block, both, [(to, back) for back, to in pairs])]
    ppermute x4, waiting for transfers between devices: 5.61 us -> 6.6 us  [per_device(): lax.ppermute(block, both, [(to, back) for back, to in pairs])]
    pallas_call x1, Pallas kernels: 5.44 us -> 4.67 us  [attend(): pl.pallas_call(attention_kernel, out_shape=vmem((count, model_width), F32...]
    unnamed x12 -> x10, local copies, waits for them, and re-layouts: 0.75 us -> 0.02 us
    ppermute x4, waiting for transfers between devices: 0.01 us -> 0.64 us  [per_device(): near = [lax.ppermute(packed, both, pairs) for pairs in turns]]
  transfers between devices with their start and end apart: 15 -> 15, of which waited for: 9 -> 9; matrix products, arithmetic and copies ran while one was open for 1% -> 1% of each run, Pallas kernels for 13% -> 14%
where the time goes in v3:
time: 44 us; the launch traced here: 43.9 us
  Pallas kernels  16 us (36%)
  starting transfers between devices  15.2 us (35%)
  waiting for transfers between devices  11.8 us (27%)
  other arithmetic  0.6 us (1%)
    ppermute x4, starting transfers between devices, per_device(): near = [lax.ppermute(packed, both, pairs) for pairs in turns]  7.15 us
    ppermute x4, waiting for transfers between devices, per_device(): lax.ppermute(block, both, [(to, back) for back, to in pairs])  6.6 us
    pallas_call x1, Pallas kernels, dequantize(): pl.pallas_call(functools.partial(weights_kernel, step), out_shape=(vmem((...  6.29 us
    ppermute x4, starting transfers between devices, per_device(): lax.ppermute(block, both, [(to, back) for back, to in pairs])  6.01 us
    pallas_call x1, Pallas kernels, attend(): pl.pallas_call(attention_kernel, out_shape=vmem((count, model_width), F32...  4.67 us
    ppermute x7, waiting for transfers between devices, swap(): return lax.ppermute(value, 'tensor', [(0, 1), (1, 0)])  4.58 us
    pallas_call x1, Pallas kernels, run_experts(): pl.pallas_call(experts_kernel, out_shape=(vmem((count // 2, width), F32),...  3.83 us
    ppermute x7, starting transfers between devices, swap(): return lax.ppermute(value, 'tensor', [(0, 1), (1, 0)])  2.05 us
  transfers between devices with their start and end apart: 15, of which 9 were waited for; matrix products, arithmetic and copies ran while one was open for 1% of the time, Pallas kernels for 14%

profile of v3, /device:TPU:0, one launch (start us, length us, event | category | flops | bytes accessed | tf_op | source)
XLA Modules:
  0.0 43.9 jit_solution(612679179999705138)
XLA Ops:
  0.0 4.7 %attention.1.mine_ref = f32[16,2880]{1,0:T(8,128)S(1)} custom-call(s32[4]{0:T(128)} %lengths_hbm.1, bf16[4,4,1024]{2,1,0:T(4,128)(2,1)} %queries_hbm.1, bf16[32,128]{1,0:T(8,128)(2,1)} %bitcast.17, bf16[4,512,128]{2,1,0:T(8,128)(2,1)} %bitcast.16, bf16[2880,1024]{1,0:T(8,128)(2,1)} %bitcast.15), custom_call_target="tpu_custom_call" | custom-call | flops 94371840 | bytes 7340032 | tf_op jit(solution)/shard_map/attention/pallas_call | solution.py:150
  4.7 0.5 %collective-permute-start = (f32[16,2880]{1,0:T(8,128)S(1)}, f32[16,2880]{1,0:T(8,128)S(1)}, u32[]{:S(2)}, u32[]{:S(2)}) collective-permute-start(f32[16,2880]{1,0:T(8,128)S(1)} %attention.1.mine_ref), channel_id=1, source_target_pairs={{0,1},{1,0},{2,3},{3,2},{4,5},{5,4},{6,7},{7,6},{8,9},{9,8},{10,11... | collective-permute-start | bytes 552968 | tf_op jit(solution)/shard_map/ppermute | solution.py:350
  5.3 1.0 %collective-permute-done.other_ref = f32[16,2880]{1,0:T(8,128)S(1)} collective-permute-done((f32[16,2880]{1,0:T(8,128)S(1)}, f32[16,2880]{1,0:T(8,128)S(1)}, u32[]{:S(2)}, u32[]{:S(2)}) %collective-permute-start) | collective-permute-done | bytes 184352 | tf_op jit(solution)/shard_map/ppermute | solution.py:350
  6.3 0.5 %normalize.1 = (f32[16,2880]{1,0:T(8,128)S(1)}, bf16[16,2944]{1,0:T(8,128)(2,1)S(1)}) custom-call(bf16[4,4,2880]{2,1,0:T(4,128)(2,1)S(1)} %copy-done.1, f32[16,2880]{1,0:T(8,128)S(1)} %attention.1.mine_ref, f32[16,2880]{1,0:T(8,128)S(1)} %collective-permute-done.other_ref, s32[16,4]{1,0:T(8,128)S(1)} %bitcast.13, bf16[8,2880]{1,0:T(8,128)(2,1)S(1)} %bitcast.12), custom_call_target="tpu_custom_call" | custom-call | tf_op jit(solution)/shard_map/normalize/pallas_call | solution.py:204
  6.8 5.0 %collective-permute-start.4 = (bf16[16,2944]{1,0:T(8,128)(2,1)S(1)}, bf16[16,2944]{1,0:T(8,128)(2,1)S(1)}, u32[]{:S(2)}, u32[]{:S(2)}) collective-permute-start(bf16[16,2944]{1,0:T(8,128)(2,1)S(1)} %get-tuple-element.24.packed_ref), channel_id=1, source_target_pairs={{0,12},{1,15},{2,14},{3,13},{4,8},{5,11},{6,10},{7,9},{8,4},{9,7},... | collective-permute-start | bytes 282632 | tf_op jit(solution)/shard_map/ppermute | solution.py:380
  11.8 0.4 collective-permute-start.3
  12.2 1.1 %collective-permute-start.2 = (bf16[16,2944]{1,0:T(8,128)(2,1)S(1)}, bf16[16,2944]{1,0:T(8,128)(2,1)S(1)}, u32[]{:S(2)}, u32[]{:S(2)}) collective-permute-start(bf16[16,2944]{1,0:T(8,128)(2,1)S(1)} %get-tuple-element.24.packed_ref), channel_id=1, source_target_pairs={{0,6},{1,5},{2,4},{3,7},{4,2},{5,1},{6,0},{7,3},{8,14},{9,13},{10,... | collective-permute-start | bytes 282632 | tf_op jit(solution)/shard_map/ppermute | solution.py:380
  13.3 0.7 %collective-permute-start.1 = (bf16[16,2944]{1,0:T(8,128)(2,1)S(1)}, bf16[16,2944]{1,0:T(8,128)(2,1)S(1)}, u32[]{:S(2)}, u32[]{:S(2)}) collective-permute-start(bf16[16,2944]{1,0:T(8,128)(2,1)S(1)} %get-tuple-element.24.packed_ref), channel_id=1, source_target_pairs={{0,0},{1,3},{2,2},{3,1},{4,4},{5,7},{6,6},{7,5},{8,8},{9,11},{10,1... | collective-permute-start | bytes 282632 | tf_op jit(solution)/shard_map/ppermute | solution.py:380
  14.0 6.3 %weights.1 = (bf16[720,2880]{1,0:T(8,128)(2,1)S(1)}, bf16[720,2880]{1,0:T(8,128)(2,1)S(1)}, bf16[720,2880]{1,0:T(8,128)(2,1)S(1)}) custom-call(bf16[16,2944]{1,0:T(8,128)(2,1)S(1)} %get-tuple-element.24.packed_ref, bf16[3,720,2880]{2,1,0:T(8,128)(2,1)} %bitcast.14, s32[270,1,720]{2,1,0:T(1,128)S(1)} %bitcast.11), custom_call_target="tpu_custom_call" | custom-call | flops 1000 | bytes 1000 | tf_op jit(solution)/shard_map/weights/pallas_call | solution.py:244
  20.3 0.6 %collective-permute-done.3.refs_1_ = bf16[16,2944]{1,0:T(8,128)(2,1)S(1)} collective-permute-done((bf16[16,2944]{1,0:T(8,128)(2,1)S(1)}, bf16[16,2944]{1,0:T(8,128)(2,1)S(1)}, u32[]{:S(2)}, u32[]{:S(2)}) %collective-permute-start.3) | collective-permute-done | bytes 94240 | tf_op jit(solution)/shard_map/ppermute | solution.py:380
  20.9 0.6 %collective-permute-start.5 = (bf16[16,2944]{1,0:T(8,128)(2,1)S(1)}, bf16[16,2944]{1,0:T(8,128)(2,1)S(1)}, u32[]{:S(2)}, u32[]{:S(2)}) collective-permute-start(bf16[16,2944]{1,0:T(8,128)(2,1)S(1)} %collective-permute-done.4.refs_0_), channel_id=1, source_target_pairs={{0,1},{1,0},{2,3},{3,2},{4,5},{5,4},{6,7},{7,6},{8,9},{9,8},{10,11... | collective-permute-start | bytes 282632 | tf_op jit(solution)/shard_map/ppermute | solution.py:350
  21.6 0.4 collective-permute-start.7
  22.1 0.5 %compare_reduce_fusion = pred[8,720]{1,0:T(8,128)(4,1)S(1)} fusion(s32[720]{0:T(1024)S(1)} %fusion, s32[8,120]{1,0:T(8,128)S(1)} %eq.15), kind=kLoop, calls=%fused_computation | loop fusion | flops 1376640 | bytes 12480 | tf_op jit(solution)/shard_map/reduce_or | solution.py:377
  23.0 0.4 collective-permute-done.8.refs_7_
  23.4 3.8 %experts.1 = (f32[64,2880]{1,0:T(8,128)S(1)}, bf16[64,2880]{1,0:T(8,128)(2,1)S(1)}) custom-call(bf16[720,2880]{1,0:T(8,128)(2,1)S(1)} %get-tuple-element.28.gate_ref, bf16[720,2880]{1,0:T(8,128)(2,1)S(1)} %get-tuple-element.29.up_ref, bf16[720,2880]{1,0:T(8,128)(2,1)S(1)} %get-tuple-element.30.down_ref, bf16[8,720]{1,0:T(8,128)(2,1)S(1)} %convert_element_type.15.member_ref, ...), custom_call_target="tpu_custom_call" | custom-call | flops 1592524800 | bytes 12441600 | tf_op jit(solution)/shard_map/experts/pallas_call | solution.py:298
  27.4 1.5 %collective-permute-done.9.other_ref = bf16[64,2880]{1,0:T(8,128)(2,1)S(1)} collective-permute-done((bf16[64,2880]{1,0:T(8,128)(2,1)S(1)}, bf16[64,2880]{1,0:T(8,128)(2,1)S(1)}, u32[]{:S(2)}, u32[]{:S(2)}) %collective-permute-start.9) | collective-permute-done | bytes 368672 | tf_op jit(solution)/shard_map/ppermute | solution.py:350
  29.0 3.5 %collective-permute-start.10 = (bf16[16,2880]{1,0:T(8,128)(2,1)S(1)}, bf16[16,2880]{1,0:T(8,128)(2,1)S(1)}, u32[]{:S(2)}, u32[]{:S(2)}) collective-permute-start(bf16[16,2880]{1,0:T(8,128)(2,1)S(1)} %get-tuple-element.37), channel_id=1, source_target_pairs={{12,0},{15,1},{14,2},{13,3},{8,4},{11,5},{10,6},{9,7},{4,8},{7,9},... | collective-permute-start | bytes 276488 | tf_op jit(solution)/shard_map/ppermute | solution.py:388
  32.6 0.3 collective-permute-start.11
  32.9 1.5 %collective-permute-start.12 = (bf16[16,2880]{1,0:T(8,128)(2,1)S(1)}, bf16[16,2880]{1,0:T(8,128)(2,1)S(1)}, u32[]{:S(2)}, u32[]{:S(2)}) collective-permute-start(bf16[16,2880]{1,0:T(8,128)(2,1)S(1)} %get-tuple-element.39), channel_id=1, source_target_pairs={{6,0},{5,1},{4,2},{7,3},{2,4},{1,5},{0,6},{3,7},{14,8},{13,9},{12,... | collective-permute-start | bytes 276488 | tf_op jit(solution)/shard_map/ppermute | solution.py:388
  34.4 0.7 %collective-permute-start.13 = (bf16[16,2880]{1,0:T(8,128)(2,1)S(1)}, bf16[16,2880]{1,0:T(8,128)(2,1)S(1)}, u32[]{:S(2)}, u32[]{:S(2)}) collective-permute-start(bf16[16,2880]{1,0:T(8,128)(2,1)S(1)} %get-tuple-element.40), channel_id=1, source_target_pairs={{0,0},{3,1},{2,2},{1,3},{4,4},{7,5},{6,6},{5,7},{8,8},{11,9},{10,1... | collective-permute-start | bytes 276488 | tf_op jit(solution)/shard_map/ppermute | solution.py:388
  35.1 1.6 %collective-permute-done.10 = bf16[16,2880]{1,0:T(8,128)(2,1)S(1)} collective-permute-done((bf16[16,2880]{1,0:T(8,128)(2,1)S(1)}, bf16[16,2880]{1,0:T(8,128)(2,1)S(1)}, u32[]{:S(2)}, u32[]{:S(2)}) %collective-permute-start.10) | collective-permute-done | bytes 92192 | tf_op jit(solution)/shard_map/ppermute | solution.py:388
  36.6 5.0 %collective-permute-done.11 = bf16[16,2880]{1,0:T(8,128)(2,1)S(1)} collective-permute-done((bf16[16,2880]{1,0:T(8,128)(2,1)S(1)}, bf16[16,2880]{1,0:T(8,128)(2,1)S(1)}, u32[]{:S(2)}, u32[]{:S(2)}) %collective-permute-start.11) | collective-permute-done | bytes 92192 | tf_op jit(solution)/shard_map/ppermute | solution.py:388
  41.8 1.4 %collective-permute-done.14.other_ref = f32[16,2880]{1,0:T(8,128)S(1)} collective-permute-done((f32[16,2880]{1,0:T(8,128)S(1)}, f32[16,2880]{1,0:T(8,128)S(1)}, u32[]{:S(2)}, u32[]{:S(2)}) %collective-permute-start.14) | collective-permute-done | bytes 184352 | tf_op jit(solution)/shard_map/ppermute | solution.py:350
  43.2 0.7 %last.1 = bf16[4,4,2880]{2,1,0:T(4,128)(2,1)} custom-call(f32[16,2880]{1,0:T(8,128)S(1)} %get-tuple-element.23.mixed_ref, f32[16,2880]{1,0:T(8,128)S(1)} %convert_add_fusion.mine_ref, f32[16,2880]{1,0:T(8,128)S(1)} %collective-permute-done.14.other_ref), custom_call_target="tpu_custom_call" | custom-call | tf_op jit(solution)/shard_map/last/pallas_call | solution.py:339
  (27 shorter events, 1.0 us)
Async XLA Ops:
  0.0 5.2 %copy-start.4 = (s32[960]{0:T(1024)S(1)}, s32[960]{0:T(1024)}, u32[]{:S(2)}) copy-start(s32[960]{0:T(1024)} %param.21) | copy-start | bytes 11524
  0.0 6.3 %copy-start.2 = (bf16[2880,8]{0,1:T(8,128)(2,1)S(1)}, bf16[2880,8]{0,1:T(8,128)(2,1)}, u32[]{:S(2)}) copy-start(bf16[2880,8]{0,1:T(8,128)(2,1)} %param.17) | copy-start | bytes 138244
  0.0 6.3 %copy-start.3 = (s32[4,4,4]{2,1,0:T(4,128)S(1)}, s32[4,4,4]{2,1,0:T(4,128)}, u32[]{:S(2)}) copy-start(s32[4,4,4]{2,1,0:T(4,128)} %param.16) | copy-start | bytes 772
  0.0 6.3 %copy-start.1 = (bf16[4,4,2880]{2,1,0:T(4,128)(2,1)S(1)}, bf16[4,4,2880]{2,1,0:T(4,128)(2,1)}, u32[]{:S(2)}) copy-start(bf16[4,4,2880]{2,1,0:T(4,128)(2,1)} %residual_ref.1) | copy-start | bytes 276484
  0.0 14.0 %copy-start = (s32[1,720,3,90]{1,0,3,2:T(1,128)S(1)}, s32[1,720,3,90]{1,0,3,2:T(1,128)}, u32[]{:S(2)}) copy-start(s32[1,720,3,90]{1,0,3,2:T(1,128)} %param.20) | copy-start | bytes 2332804
  4.7 1.6 %collective-permute-start = (f32[16,2880]{1,0:T(8,128)S(1)}, f32[16,2880]{1,0:T(8,128)S(1)}, u32[]{:S(2)}, u32[]{:S(2)}) collective-permute-start(f32[16,2880]{1,0:T(8,128)S(1)} %attention.1.mine_ref), channel_id=1, source_target_pairs={{0,1},{1,0},{2,3},{3,2},{4,5},{5,4},{6,7},{7,6},{8,9},{9,8},{10,11... | collective-permute-start | bytes 552968 | tf_op jit(solution)/shard_map/ppermute | solution.py:350
  6.8 13.5 %collective-permute-start.4 = (bf16[16,2944]{1,0:T(8,128)(2,1)S(1)}, bf16[16,2944]{1,0:T(8,128)(2,1)S(1)}, u32[]{:S(2)}, u32[]{:S(2)}) collective-permute-start(bf16[16,2944]{1,0:T(8,128)(2,1)S(1)} %get-tuple-element.24.packed_ref), channel_id=1, source_target_pairs={{0,12},{1,15},{2,14},{3,13},{4,8},{5,11},{6,10},{7,9},{8,4},{9,7},... | collective-permute-start | bytes 282632 | tf_op jit(solution)/shard_map/ppermute | solution.py:380
  11.8 9.1 %collective-permute-start.3 = (bf16[16,2944]{1,0:T(8,128)(2,1)S(1)}, bf16[16,2944]{1,0:T(8,128)(2,1)S(1)}, u32[]{:S(2)}, u32[]{:S(2)}) collective-permute-start(bf16[16,2944]{1,0:T(8,128)(2,1)S(1)} %get-tuple-element.24.packed_ref), channel_id=1, source_target_pairs={{0,10},{1,9},{2,8},{3,11},{4,14},{5,13},{6,12},{7,15},{8,2},{9,1},... | collective-permute-start | bytes 282632 | tf_op jit(solution)/shard_map/ppermute | solution.py:380
  12.2 8.7 %collective-permute-start.2 = (bf16[16,2944]{1,0:T(8,128)(2,1)S(1)}, bf16[16,2944]{1,0:T(8,128)(2,1)S(1)}, u32[]{:S(2)}, u32[]{:S(2)}) collective-permute-start(bf16[16,2944]{1,0:T(8,128)(2,1)S(1)} %get-tuple-element.24.packed_ref), channel_id=1, source_target_pairs={{0,6},{1,5},{2,4},{3,7},{4,2},{5,1},{6,0},{7,3},{8,14},{9,13},{10,... | collective-permute-start | bytes 282632 | tf_op jit(solution)/shard_map/ppermute | solution.py:380
  13.3 7.6 %collective-permute-start.1 = (bf16[16,2944]{1,0:T(8,128)(2,1)S(1)}, bf16[16,2944]{1,0:T(8,128)(2,1)S(1)}, u32[]{:S(2)}, u32[]{:S(2)}) collective-permute-start(bf16[16,2944]{1,0:T(8,128)(2,1)S(1)} %get-tuple-element.24.packed_ref), channel_id=1, source_target_pairs={{0,0},{1,3},{2,2},{3,1},{4,4},{5,7},{6,6},{7,5},{8,8},{9,11},{10,1... | collective-permute-start | bytes 282632 | tf_op jit(solution)/shard_map/ppermute | solution.py:380
  20.9 1.8 %collective-permute-start.5 = (bf16[16,2944]{1,0:T(8,128)(2,1)S(1)}, bf16[16,2944]{1,0:T(8,128)(2,1)S(1)}, u32[]{:S(2)}, u32[]{:S(2)}) collective-permute-start(bf16[16,2944]{1,0:T(8,128)(2,1)S(1)} %collective-permute-done.4.refs_0_), channel_id=1, source_target_pairs={{0,1},{1,0},{2,3},{3,2},{4,5},{5,4},{6,7},{7,6},{8,9},{9,8},{10,11... | collective-permute-start | bytes 282632 | tf_op jit(solution)/shard_map/ppermute | solution.py:350
  21.6 1.3 %collective-permute-start.6 = (bf16[16,2944]{1,0:T(8,128)(2,1)S(1)}, bf16[16,2944]{1,0:T(8,128)(2,1)S(1)}, u32[]{:S(2)}, u32[]{:S(2)}) collective-permute-start(bf16[16,2944]{1,0:T(8,128)(2,1)S(1)} %collective-permute-done.3.refs_1_), channel_id=1, source_target_pairs={{0,1},{1,0},{2,3},{3,2},{4,5},{5,4},{6,7},{7,6},{8,9},{9,8},{10,11... | collective-permute-start | bytes 282632 | tf_op jit(solution)/shard_map/ppermute | solution.py:350
  21.6 1.4 %collective-permute-start.7 = (bf16[16,2944]{1,0:T(8,128)(2,1)S(1)}, bf16[16,2944]{1,0:T(8,128)(2,1)S(1)}, u32[]{:S(2)}, u32[]{:S(2)}) collective-permute-start(bf16[16,2944]{1,0:T(8,128)(2,1)S(1)} %collective-permute-done.2.refs_2_), channel_id=1, source_target_pairs={{0,1},{1,0},{2,3},{3,2},{4,5},{5,4},{6,7},{7,6},{8,9},{9,8},{10,11... | collective-permute-start | bytes 282632 | tf_op jit(solution)/shard_map/ppermute | solution.py:350
  22.1 1.3 %collective-permute-start.8 = (bf16[16,2944]{1,0:T(8,128)(2,1)S(1)}, bf16[16,2944]{1,0:T(8,128)(2,1)S(1)}, u32[]{:S(2)}, u32[]{:S(2)}) collective-permute-start(bf16[16,2944]{1,0:T(8,128)(2,1)S(1)} %collective-permute-done.1.refs_3_), channel_id=1, source_target_pairs={{0,1},{1,0},{2,3},{3,2},{4,5},{5,4},{6,7},{7,6},{8,9},{9,8},{10,11... | collective-permute-start | bytes 282632 | tf_op jit(solution)/shard_map/ppermute | solution.py:350
  27.2 1.8 %collective-permute-start.9 = (bf16[64,2880]{1,0:T(8,128)(2,1)S(1)}, bf16[64,2880]{1,0:T(8,128)(2,1)S(1)}, u32[]{:S(2)}, u32[]{:S(2)}) collective-permute-start(bf16[64,2880]{1,0:T(8,128)(2,1)S(1)} %get-tuple-element.36), channel_id=1, source_target_pairs={{0,1},{1,0},{2,3},{3,2},{4,5},{5,4},{6,7},{7,6},{8,9},{9,8},{10,11... | collective-permute-start | bytes 1105928 | tf_op jit(solution)/shard_map/ppermute | solution.py:350
  29.0 7.6 %collective-permute-start.10 = (bf16[16,2880]{1,0:T(8,128)(2,1)S(1)}, bf16[16,2880]{1,0:T(8,128)(2,1)S(1)}, u32[]{:S(2)}, u32[]{:S(2)}) collective-permute-start(bf16[16,2880]{1,0:T(8,128)(2,1)S(1)} %get-tuple-element.37), channel_id=1, source_target_pairs={{12,0},{15,1},{14,2},{13,3},{8,4},{11,5},{10,6},{9,7},{4,8},{7,9},... | collective-permute-start | bytes 276488 | tf_op jit(solution)/shard_map/ppermute | solution.py:388
  32.6 9.1 %collective-permute-start.11 = (bf16[16,2880]{1,0:T(8,128)(2,1)S(1)}, bf16[16,2880]{1,0:T(8,128)(2,1)S(1)}, u32[]{:S(2)}, u32[]{:S(2)}) collective-permute-start(bf16[16,2880]{1,0:T(8,128)(2,1)S(1)} %get-tuple-element.38), channel_id=1, source_target_pairs={{10,0},{9,1},{8,2},{11,3},{14,4},{13,5},{12,6},{15,7},{2,8},{1,9},... | collective-permute-start | bytes 276488 | tf_op jit(solution)/shard_map/ppermute | solution.py:388
  32.9 8.7 %collective-permute-start.12 = (bf16[16,2880]{1,0:T(8,128)(2,1)S(1)}, bf16[16,2880]{1,0:T(8,128)(2,1)S(1)}, u32[]{:S(2)}, u32[]{:S(2)}) collective-permute-start(bf16[16,2880]{1,0:T(8,128)(2,1)S(1)} %get-tuple-element.39), channel_id=1, source_target_pairs={{6,0},{5,1},{4,2},{7,3},{2,4},{1,5},{0,6},{3,7},{14,8},{13,9},{12,... | collective-permute-start | bytes 276488 | tf_op jit(solution)/shard_map/ppermute | solution.py:388
  34.4 7.3 %collective-permute-start.13 = (bf16[16,2880]{1,0:T(8,128)(2,1)S(1)}, bf16[16,2880]{1,0:T(8,128)(2,1)S(1)}, u32[]{:S(2)}, u32[]{:S(2)}) collective-permute-start(bf16[16,2880]{1,0:T(8,128)(2,1)S(1)} %get-tuple-element.40), channel_id=1, source_target_pairs={{0,0},{3,1},{2,2},{1,3},{4,4},{7,5},{6,6},{5,7},{8,8},{11,9},{10,1... | collective-permute-start | bytes 276488 | tf_op jit(solution)/shard_map/ppermute | solution.py:388
  41.7 1.5 %collective-permute-start.14 = (f32[16,2880]{1,0:T(8,128)S(1)}, f32[16,2880]{1,0:T(8,128)S(1)}, u32[]{:S(2)}, u32[]{:S(2)}) collective-permute-start(f32[16,2880]{1,0:T(8,128)S(1)} %convert_add_fusion.mine_ref), channel_id=1, source_target_pairs={{0,1},{1,0},{2,3},{3,2},{4,5},{5,4},{6,7},{7,6},{8,9},{9,8},{10,11... | collective-permute-start | bytes 552968 | tf_op jit(solution)/shard_map/ppermute | solution.py:350

commit v4 on v3

--- a/solution.py
+++ b/solution.py
@@ -18,8 +18,6 @@
 BF16 = jnp.bfloat16
 
 NT = (((1,), (1,)), ((), ()))
-TN = (((0,), (0,)), ((), ()))
-TT = (((0,), (1,)), ((), ()))
 
 
 def dot(a, b, dims=(((1,), (0,)), ((), ()))):
@@ -211,8 +209,8 @@
     )(held(residual), held(mine), held(other), held(routing), held(router.T))
 
 
-def weights_kernel(step, packed_ref, mantissa_hbm, exponent_ref, *refs):
-    out_refs, (power, expander, sems) = refs[:-3], refs[-3:]
+def weights_kernel(step, rows_ref, mantissa_hbm, exponent_ref, placement_ref, *refs):
+    out_refs, member_ref, (power, expander, sems) = refs[:-4], refs[-4], refs[-3:]
     units, blocks = power.shape
     width = expander.shape[1]
     pieces = [(part, first) for part in range(len(out_refs)) for first in range(0, units, step)]
@@ -224,6 +222,18 @@
     ]
     for move in moves[:AHEAD]:
         move.start()
+
+    experts, slots = placement_ref.shape
+    tiles = units // TILE_UNITS
+    tile = lax.axis_index("expert") * tiles + iota((tiles, slots), 0)
+    lane = iota((slots, LANES), 1) - width % LANES
+    found = jnp.zeros((tiles, LANES), F32)
+    for expert in range(experts):
+        here = (placement_ref[expert : expert + 1, :] == tile).astype(BF16)
+        found += dot(here, ((lane == expert) | (lane == expert + experts)).astype(BF16))
+    spread = (iota((units, tiles), 0) // TILE_UNITS == iota((units, tiles), 1)).astype(BF16)
+    member_ref[...] = dot(spread, found.astype(BF16)).astype(BF16)
+
     expander[...] = (iota((blocks, width), 1) // BLOCK == iota((blocks, width), 0)).astype(BF16)
     for place, (part, first) in enumerate(pieces):
         if first == 0:
@@ -237,15 +247,15 @@
         out_refs[part][rows, :] = (out_refs[part][rows, :].astype(F32) * scale).astype(BF16)
 
 
-def dequantize(packed, mantissa, exponent):
+def dequantize(rows, mantissa, exponent, placement):
     parts, units, width = mantissa.shape
     blocks = exponent.shape[0] // parts
     step = unit_step(units)
-    return pl.pallas_call(
+    *weights, member = pl.pallas_call(
         functools.partial(weights_kernel, step),
-        out_shape=(vmem((units, width), BF16),) * parts,
-        in_specs=[whole(1)[0], pl.BlockSpec(memory_space=pltpu.HBM), whole(1)[0]],
-        out_specs=whole(parts),
+        out_shape=(vmem((units, width), BF16),) * parts + (vmem((units, LANES), BF16),),
+        in_specs=whole(1) + [pl.BlockSpec(memory_space=pltpu.HBM)] + whole(2),
+        out_specs=whole(parts + 1),
         scratch_shapes=[
             pltpu.VMEM((units, blocks), BF16),
             pltpu.VMEM((blocks, width), BF16),
@@ -254,27 +264,27 @@
         compiler_params=params(14),
         cost_estimate=pl.CostEstimate(flops=1000, bytes_accessed=1000, transcendentals=0),
         name="weights",
-    )(held(packed), afar(mantissa), held(exponent))
+    )(held(rows), afar(mantissa), held(exponent), held(placement))
+    return weights, member
 
 
 def experts_kernel(gate_ref, up_ref, down_ref, member_ref, *refs):
-    arrived, (mine_ref, other_ref, rows, share) = refs[:-4], refs[-4:]
+    arrived, (mine_ref, other_ref, rows) = refs[:-3], refs[-3:]
     units, width = gate_ref.shape
     place = 0
     for ref in arrived:
         rows[place : place + ref.shape[0], :] = ref[...]
         place += ref.shape[0]
     inputs = rows[:, :width]
-    high = rows[:, width : width + EXPERTS]
-    low = rows[:, width + EXPERTS : width + 2 * EXPERTS]
-    share[...] = dot(member_ref[...], high, TT) + dot(member_ref[...], low, TT)
+    gates = rows[:, rows.shape[1] - LANES :]
     step = unit_step(units)
     hidden = []
     for first in range(0, units, step):
         here = slice(first, first + step)
         gate = dot(gate_ref[here, :], inputs, NT)
         up = dot(up_ref[here, :], inputs, NT)
-        hidden.append((gate * jax.nn.sigmoid(gate) * up * share[here, :]).astype(BF16))
+        share = dot(member_ref[here, :], gates, NT)
+        hidden.append((gate * jax.nn.sigmoid(gate) * up * share).astype(BF16))
     hidden = jnp.concatenate(hidden, axis=0).T
     half = mine_ref.shape[0]
     for first in range(0, width, 512):
@@ -300,7 +310,7 @@
         out_shape=(vmem((count // 2, width), F32), vmem((count // 2, width), BF16)),
         in_specs=whole(4 + len(arrived)),
         out_specs=whole(2),
-        scratch_shapes=[pltpu.VMEM((count, padded), BF16), pltpu.VMEM((units, count), F32)],
+        scratch_shapes=[pltpu.VMEM((count, padded), BF16)],
         compiler_params=params(16),
         cost_estimate=pl.CostEstimate(
             flops=6 * count * units * width, bytes_accessed=6 * units * width, transcendentals=0
@@ -309,23 +319,36 @@
     )(*[held(kind) for kind in weights], held(member), *[held(block) for block in arrived])
 
 
+def local(kernel, name, shapes, *values):
+    return pl.pallas_call(
+        kernel,
+        out_shape=[vmem(*shape) for shape in shapes],
+        in_specs=whole(len(values)),
+        out_specs=whole(len(shapes)),
+        compiler_params=params(),
+        name=name,
+    )(*[held(value) for value in values])
+
+
 def join_kernel(mine_ref, other_ref, *out_refs):
     count = out_refs[0].shape[0]
     for turn, out_ref in enumerate(out_refs):
         here = slice(turn * count, (turn + 1) * count)
-        out_ref[...] = (mine_ref[here, :] + other_ref[here, :].astype(F32)).astype(BF16)
-
-
-def join(mine, other, count):
-    turns = mine.shape[0] // count
-    return pl.pallas_call(
-        join_kernel,
-        out_shape=[vmem((count, mine.shape[1]), BF16)] * turns,
-        in_specs=whole(2),
-        out_specs=whole(turns),
-        compiler_params=params(),
-        name="join",
-    )(held(mine), held(other))
+        out_ref[...] = (mine_ref[here, :] + other_ref[here, :].astype(F32)).astype(out_ref.dtype)
+
+
+def join(mine, other, count, kept):
+    rows, width = mine.shape
+    shapes = [((count, width), F32 if turn < kept else BF16) for turn in range(rows // count)]
+    return local(join_kernel, "join", shapes, mine, other)
+
+
+def merge_kernel(mine_ref, other_ref, out_ref):
+    out_ref[...] = (mine_ref[...] + other_ref[...].astype(F32)).astype(BF16)
+
+
+def merge(mine, other):
+    return local(merge_kernel, "merge", [(mine.shape, BF16)], mine, other)[0]
 
 
 def last_kernel(mixed_ref, mine_ref, other_ref, out_ref):
@@ -351,42 +374,52 @@
 
 
 def partners(count):
-    power = count & (count - 1) == 0
-    reach = lambda place, far: place ^ far if power else (place + far) % count
-    far = sorted(range(count), key=lambda k: (k.bit_count() % 2, -k))
-    half = count // 2
-    return [
-        [(2 * place + core, 2 * reach(place, far[turn + core * half]) + core) for place in range(count) for core in range(2)]
-        for turn in range(half)
-    ]
+    share = count // 8
+    even = list(range(count - 2, count // 2 - 1, -2))
+    even = (even[:share], even[share:])
+    odd = [[k + 1 for k in core] for core in even]
+    near = tuple([k for k in range(count // 2 - 1, -1, -1) if (k + 1) % 4 // 2 == core] for core in range(2))
+
+    def turns(far):
+        return [
+            [(2 * place + core, 2 * (place ^ far[core][turn]) + core) for place in range(count) for core in range(2)]
+            for turn in range(len(far[0]))
+        ]
+
+    return turns(even), turns(odd), turns(near)
 
 
 def per_device(residual, queries, new_kv, cache_kv, lengths, routing, router, out_proj, mantissa, exponent, placement):
     places = lax.axis_size("expert")
-    place = lax.axis_index("expert")
     steps, rows, width = residual.shape
     count = steps * rows
     units = mantissa.shape[1]
-    turns = partners(places)
+    even, odd, close = partners(places)
+    turns = even + odd + close
+    beside = [(2 * spot + core, 2 * (spot ^ 1) + core) for spot in range(places) for core in range(2)]
     both = ("expert", "tensor")
 
     partial = attend(lengths, queries, new_kv, cache_kv, out_proj)
     mantissa = mantissa[0].transpose(1, 0, 2)
     exponent = exponent.transpose(2, 3, 0, 1).reshape(-1, 1, units)
-    tile = place * (units // TILE_UNITS) + jnp.arange(units) // TILE_UNITS
-    member = jnp.any(placement.reshape(EXPERTS, -1, 1) == tile, axis=1).astype(BF16)
 
     mixed, packed = normalize(residual, partial, swap(partial), routing.reshape(count, TOP), router)
     near = [lax.ppermute(packed, both, pairs) for pairs in turns]
-    weights = dequantize(packed, mantissa, exponent)
-    near, weights = lax.optimization_barrier((near[::-1], weights))
+    weights, member = dequantize(packed, mantissa, exponent, placement.reshape(EXPERTS, -1))
+    near, weights, member = lax.optimization_barrier((near[::-1], weights, member))
     near = near[::-1]
     far = [swap(block) for block in near]
     mine, other = run_experts(weights, member, near + far)
-    sums = join(mine, swap(other), count)
+    sums = join(mine, swap(other), count, len(even))
+    passed = [lax.ppermute(block, both, beside) for block in sums[len(even) : 2 * len(even)]]
     back = [
-        lax.ppermute(block, both, [(to, back) for back, to in pairs]) for block, pairs in zip(sums, turns)
+        lax.ppermute(block, both, [(to, back) for back, to in pairs])
+        for block, pairs in zip(sums[2 * len(even) :], close)
     ]
+    back = [
+        lax.ppermute(merge(block, extra), both, [(to, back) for back, to in pairs])
+        for block, extra, pairs in zip(sums, passed, even)
+    ] + back
     total = sum(block.astype(F32) for block in back)
     return last(mixed, total, swap(total), residual.shape)
 

time: 44 us -> 42.4 us (0.964)
  waiting for transfers between devices: 11.8 us -> 11.1 us
  other arithmetic: 0.6 us -> 0.04 us
    ppermute x4 -> x2, waiting for transfers between devices: 6.6 us -> 0.01 us  [per_device(): lax.ppermute(block, both, [(to, back) for back, to in pairs])]
    ppermute x0 -> x2, waiting for transfers between devices: none -> 5.96 us  [the longest x1 3.85 us: per_device(): lax.ppermute(merge(block, extra), both, [(to, back) for back, to in pairs])]
    ppermute x4 -> x2, starting transfers between devices: 6.01 us -> 1.13 us  [per_device(): lax.ppermute(block, both, [(to, back) for back, to in pairs])]
    ppermute x0 -> x2, starting transfers between devices: none -> 4.15 us  [the longest x1 2.58 us: per_device(): lax.ppermute(merge(block, extra), both, [(to, back) for back, to in pairs])]
    ppermute x7, starting transfers between devices: 2.05 us -> 3.09 us  [swap(): return lax.ppermute(value, 'tensor', [(0, 1), (1, 0)])]
    reduce_or x1 -> x0, other arithmetic: 0.53 us -> none  [per_device(): jnp.any(placement.reshape(EXPERTS, -1, 1) == tile, axis=1).astype(BF16)]
    pallas_call x1, Pallas kernels: 3.83 us -> 3.38 us  [run_experts(): pl.pallas_call(experts_kernel, out_shape=(vmem((count // 2, width), F32),...]
  transfers between devices with their start and end apart: 15 -> 15, of which waited for: 9 -> 10; matrix products, arithmetic and copies ran while one was open for 1% -> 0% of each run, Pallas kernels for 14% -> 15%
where the time goes in v4:
time: 42.4 us; the launch traced here: 42.2 us
  Pallas kernels  15.7 us (37%)
  starting transfers between devices  15.2 us (36%)
  waiting for transfers between devices  11.1 us (26%)
    ppermute x4, starting transfers between devices, per_device(): near = [lax.ppermute(packed, both, pairs) for pairs in turns]  6.85 us
    pallas_call x1, Pallas kernels, dequantize(): pl.pallas_call(functools.partial(weights_kernel, step), out_shape=(vmem((...  6.31 us
    ppermute x7, waiting for transfers between devices, swap(): return lax.ppermute(value, 'tensor', [(0, 1), (1, 0)])  4.88 us
    pallas_call x1, Pallas kernels, attend(): pl.pallas_call(attention_kernel, out_shape=vmem((count, model_width), F32...  4.67 us
    ppermute x1, waiting for transfers between devices, per_device(): lax.ppermute(merge(block, extra), both, [(to, back) for back, to in pairs])  3.85 us
    pallas_call x1, Pallas kernels, run_experts(): pl.pallas_call(experts_kernel, out_shape=(vmem((count // 2, width), F32),...  3.38 us
    ppermute x7, starting transfers between devices, swap(): return lax.ppermute(value, 'tensor', [(0, 1), (1, 0)])  3.09 us
    ppermute x1, starting transfers between devices, per_device(): lax.ppermute(merge(block, extra), both, [(to, back) for back, to in pairs])  2.58 us
  transfers between devices with their start and end apart: 15, of which 10 were waited for; matrix products, arithmetic and copies ran while one was open for 0% of the time, Pallas kernels for 15%

profile of v4, /device:TPU:0, one launch (start us, length us, event | category | flops | bytes accessed | tf_op | source)
XLA Modules:
  0.0 42.2 jit_solution(11712998469678540650)
XLA Ops:
  0.0 4.7 %attention.1.mine_ref = f32[16,2880]{1,0:T(8,128)S(1)} custom-call(s32[4]{0:T(128)} %lengths_hbm.1, bf16[4,4,1024]{2,1,0:T(4,128)(2,1)} %queries_hbm.1, bf16[32,128]{1,0:T(8,128)(2,1)} %bitcast.17, bf16[4,512,128]{2,1,0:T(8,128)(2,1)} %bitcast.16, bf16[2880,1024]{1,0:T(8,128)(2,1)} %bitcast.15), custom_call_target="tpu_custom_call" | custom-call | flops 94371840 | bytes 7340032 | tf_op jit(solution)/shard_map/attention/pallas_call | solution.py:148
  4.7 0.5 %collective-permute-start = (f32[16,2880]{1,0:T(8,128)S(1)}, f32[16,2880]{1,0:T(8,128)S(1)}, u32[]{:S(2)}, u32[]{:S(2)}) collective-permute-start(f32[16,2880]{1,0:T(8,128)S(1)} %attention.1.mine_ref), channel_id=1, source_target_pairs={{0,1},{1,0},{2,3},{3,2},{4,5},{5,4},{6,7},{7,6},{8,9},{9,8},{10,11... | collective-permute-start | bytes 552968 | tf_op jit(solution)/shard_map/ppermute | solution.py:373
  5.2 1.1 %collective-permute-done.other_ref = f32[16,2880]{1,0:T(8,128)S(1)} collective-permute-done((f32[16,2880]{1,0:T(8,128)S(1)}, f32[16,2880]{1,0:T(8,128)S(1)}, u32[]{:S(2)}, u32[]{:S(2)}) %collective-permute-start) | collective-permute-done | bytes 184352 | tf_op jit(solution)/shard_map/ppermute | solution.py:373
  6.3 0.5 %normalize.1 = (f32[16,2880]{1,0:T(8,128)S(1)}, bf16[16,2944]{1,0:T(8,128)(2,1)S(1)}) custom-call(bf16[4,4,2880]{2,1,0:T(4,128)(2,1)S(1)} %copy-done.1, f32[16,2880]{1,0:T(8,128)S(1)} %attention.1.mine_ref, f32[16,2880]{1,0:T(8,128)S(1)} %collective-permute-done.other_ref, s32[16,4]{1,0:T(8,128)S(1)} %bitcast.13, bf16[8,2880]{1,0:T(8,128)(2,1)S(1)} %bitcast.12), custom_call_target="tpu_custom_call" | custom-call | tf_op jit(solution)/shard_map/normalize/pallas_call | solution.py:202
  6.8 5.0 %collective-permute-start.4 = (bf16[16,2944]{1,0:T(8,128)(2,1)S(1)}, bf16[16,2944]{1,0:T(8,128)(2,1)S(1)}, u32[]{:S(2)}, u32[]{:S(2)}) collective-permute-start(bf16[16,2944]{1,0:T(8,128)(2,1)S(1)} %get-tuple-element.26.rows_ref), channel_id=1, source_target_pairs={{0,12},{1,9},{2,14},{3,11},{4,8},{5,13},{6,10},{7,15},{8,4},{9,1},... | collective-permute-start | bytes 282632 | tf_op jit(solution)/shard_map/ppermute | solution.py:407
  11.8 1.2 %collective-permute-start.3 = (bf16[16,2944]{1,0:T(8,128)(2,1)S(1)}, bf16[16,2944]{1,0:T(8,128)(2,1)S(1)}, u32[]{:S(2)}, u32[]{:S(2)}) collective-permute-start(bf16[16,2944]{1,0:T(8,128)(2,1)S(1)} %get-tuple-element.26.rows_ref), channel_id=1, source_target_pairs={{0,14},{1,11},{2,12},{3,9},{4,10},{5,15},{6,8},{7,13},{8,6},{9,3},... | collective-permute-start | bytes 282632 | tf_op jit(solution)/shard_map/ppermute | solution.py:407
  13.0 0.7 %collective-permute-start.1 = (bf16[16,2944]{1,0:T(8,128)(2,1)S(1)}, bf16[16,2944]{1,0:T(8,128)(2,1)S(1)}, u32[]{:S(2)}, u32[]{:S(2)}) collective-permute-start(bf16[16,2944]{1,0:T(8,128)(2,1)S(1)} %get-tuple-element.26.rows_ref), channel_id=1, source_target_pairs={{0,0},{1,3},{2,2},{3,1},{4,4},{5,7},{6,6},{7,5},{8,8},{9,11},{10,1... | collective-permute-start | bytes 282632 | tf_op jit(solution)/shard_map/ppermute | solution.py:407
  13.8 6.3 %weights.1 = (bf16[720,2880]{1,0:T(8,128)(2,1)S(1)}, bf16[720,2880]{1,0:T(8,128)(2,1)S(1)}, bf16[720,2880]{1,0:T(8,128)(2,1)S(1)}, bf16[720,128]{1,0:T(8,128)(2,1)S(1)}) custom-call(bf16[16,2944]{1,0:T(8,128)(2,1)S(1)} %get-tuple-element.26.rows_ref, bf16[3,720,2880]{2,1,0:T(8,128)(2,1)} %bitcast.14, s32[270,1,720]{2,1,0:T(1,128)S(1)} %bitcast.11, ...), custom_call_target="tpu_custom_call" | custom-call | flops 1000 | bytes 1000 | tf_op jit(solution)/shard_map/weights/pallas_call | solution.py:254
  20.3 1.3 %collective-permute-start.5 = (bf16[16,2944]{1,0:T(8,128)(2,1)S(1)}, bf16[16,2944]{1,0:T(8,128)(2,1)S(1)}, u32[]{:S(2)}, u32[]{:S(2)}) collective-permute-start(bf16[16,2944]{1,0:T(8,128)(2,1)S(1)} %collective-permute-done.4.refs_0_), channel_id=1, source_target_pairs={{0,1},{1,0},{2,3},{3,2},{4,5},{5,4},{6,7},{7,6},{8,9},{9,8},{10,11... | collective-permute-start | bytes 282632 | tf_op jit(solution)/shard_map/ppermute | solution.py:373
  21.7 0.4 %collective-permute-start.7 = (bf16[16,2944]{1,0:T(8,128)(2,1)S(1)}, bf16[16,2944]{1,0:T(8,128)(2,1)S(1)}, u32[]{:S(2)}, u32[]{:S(2)}) collective-permute-start(bf16[16,2944]{1,0:T(8,128)(2,1)S(1)} %collective-permute-done.2.refs_2_), channel_id=1, source_target_pairs={{0,1},{1,0},{2,3},{3,2},{4,5},{5,4},{6,7},{7,6},{8,9},{9,8},{10,11... | collective-permute-start | bytes 282632 | tf_op jit(solution)/shard_map/ppermute | solution.py:373
  22.2 0.3 collective-permute-done.5.refs_4_
  22.6 0.4 collective-permute-done.6.refs_5_
  23.1 0.4 collective-permute-done.8.refs_7_
  23.4 3.4 %experts.1 = (f32[64,2880]{1,0:T(8,128)S(1)}, bf16[64,2880]{1,0:T(8,128)(2,1)S(1)}) custom-call(bf16[720,2880]{1,0:T(8,128)(2,1)S(1)} %get-tuple-element.31.gate_ref, bf16[720,2880]{1,0:T(8,128)(2,1)S(1)} %get-tuple-element.32.up_ref, bf16[720,2880]{1,0:T(8,128)(2,1)S(1)} %get-tuple-element.33.down_ref, bf16[720,128]{1,0:T(8,128)(2,1)S(1)} %get-tuple-element.34.member_ref, ...), custom_call_target="tpu_custom_call" | custom-call | flops 1592524800 | bytes 12441600 | tf_op jit(solution)/shard_map/experts/pallas_call | solution.py:308
  27.0 1.5 %collective-permute-done.9.other_ref = bf16[64,2880]{1,0:T(8,128)(2,1)S(1)} collective-permute-done((bf16[64,2880]{1,0:T(8,128)(2,1)S(1)}, bf16[64,2880]{1,0:T(8,128)(2,1)S(1)}, u32[]{:S(2)}, u32[]{:S(2)}) %collective-permute-start.9) | collective-permute-done | bytes 368672 | tf_op jit(solution)/shard_map/ppermute | solution.py:373
  28.7 1.6 %collective-permute-start.10 = (bf16[16,2880]{1,0:T(8,128)(2,1)S(1)}, bf16[16,2880]{1,0:T(8,128)(2,1)S(1)}, u32[]{:S(2)}, u32[]{:S(2)}) collective-permute-start(bf16[16,2880]{1,0:T(8,128)(2,1)S(1)} %get-tuple-element.42), channel_id=1, source_target_pairs={{0,2},{1,3},{2,0},{3,1},{4,6},{5,7},{6,4},{7,5},{8,10},{9,11},{10,... | collective-permute-start | bytes 276488 | tf_op jit(solution)/shard_map/ppermute | solution.py:414
  30.2 0.5 %collective-permute-start.12 = (bf16[16,2880]{1,0:T(8,128)(2,1)S(1)}, bf16[16,2880]{1,0:T(8,128)(2,1)S(1)}, u32[]{:S(2)}, u32[]{:S(2)}) collective-permute-start(bf16[16,2880]{1,0:T(8,128)(2,1)S(1)} %get-tuple-element.43), channel_id=1, source_target_pairs={{6,0},{5,1},{4,2},{7,3},{2,4},{1,5},{0,6},{3,7},{14,8},{13,9},{12,... | collective-permute-start | bytes 276488 | tf_op jit(solution)/shard_map/ppermute | solution.py:416
  30.7 0.7 %collective-permute-start.13 = (bf16[16,2880]{1,0:T(8,128)(2,1)S(1)}, bf16[16,2880]{1,0:T(8,128)(2,1)S(1)}, u32[]{:S(2)}, u32[]{:S(2)}) collective-permute-start(bf16[16,2880]{1,0:T(8,128)(2,1)S(1)} %get-tuple-element.44), channel_id=1, source_target_pairs={{0,0},{3,1},{2,2},{1,3},{4,4},{7,5},{6,6},{5,7},{8,8},{11,9},{10,1... | collective-permute-start | bytes 276488 | tf_op jit(solution)/shard_map/ppermute | solution.py:416
  31.4 2.1 %collective-permute-done.10.other_ref = bf16[16,2880]{1,0:T(8,128)(2,1)S(1)} collective-permute-done((bf16[16,2880]{1,0:T(8,128)(2,1)S(1)}, bf16[16,2880]{1,0:T(8,128)(2,1)S(1)}, u32[]{:S(2)}, u32[]{:S(2)}) %collective-permute-start.10) | collective-permute-done | bytes 92192 | tf_op jit(solution)/shard_map/ppermute | solution.py:414
  33.5 2.6 %collective-permute-start.11 = (bf16[16,2880]{1,0:T(8,128)(2,1)S(1)}, bf16[16,2880]{1,0:T(8,128)(2,1)S(1)}, u32[]{:S(2)}, u32[]{:S(2)}) collective-permute-start(bf16[16,2880]{1,0:T(8,128)(2,1)S(1)} %merge.1), channel_id=1, source_target_pairs={{12,0},{9,1},{14,2},{11,3},{8,4},{13,5},{10,6},{15,7},{4,8},{1,9},... | collective-permute-start | bytes 276488 | tf_op jit(solution)/shard_map/ppermute | solution.py:420
  36.1 3.9 %collective-permute-done.11 = bf16[16,2880]{1,0:T(8,128)(2,1)S(1)} collective-permute-done((bf16[16,2880]{1,0:T(8,128)(2,1)S(1)}, bf16[16,2880]{1,0:T(8,128)(2,1)S(1)}, u32[]{:S(2)}, u32[]{:S(2)}) %collective-permute-start.11) | collective-permute-done | bytes 92192 | tf_op jit(solution)/shard_map/ppermute | solution.py:420
  40.0 0.5 %collective-permute-start.14 = (f32[16,2880]{1,0:T(8,128)S(1)}, f32[16,2880]{1,0:T(8,128)S(1)}, u32[]{:S(2)}, u32[]{:S(2)}) collective-permute-start(f32[16,2880]{1,0:T(8,128)S(1)} %convert_add_fusion.mine_ref), channel_id=1, source_target_pairs={{0,1},{1,0},{2,3},{3,2},{4,5},{5,4},{6,7},{7,6},{8,9},{9,8},{10,11... | collective-permute-start | bytes 552968 | tf_op jit(solution)/shard_map/ppermute | solution.py:373
  40.5 1.1 %collective-permute-done.14.other_ref = f32[16,2880]{1,0:T(8,128)S(1)} collective-permute-done((f32[16,2880]{1,0:T(8,128)S(1)}, f32[16,2880]{1,0:T(8,128)S(1)}, u32[]{:S(2)}, u32[]{:S(2)}) %collective-permute-start.14) | collective-permute-done | bytes 184352 | tf_op jit(solution)/shard_map/ppermute | solution.py:373
  41.5 0.7 %last.1 = bf16[4,4,2880]{2,1,0:T(4,128)(2,1)} custom-call(f32[16,2880]{1,0:T(8,128)S(1)} %get-tuple-element.25.mixed_ref, f32[16,2880]{1,0:T(8,128)S(1)} %convert_add_fusion.mine_ref, f32[16,2880]{1,0:T(8,128)S(1)} %collective-permute-done.14.other_ref), custom_call_target="tpu_custom_call" | custom-call | tf_op jit(solution)/shard_map/last/pallas_call | solution.py:362
  (25 shorter events, 1.0 us)
Async XLA Ops:
  0.0 6.3 %copy-start.2 = (bf16[2880,8]{0,1:T(8,128)(2,1)S(1)}, bf16[2880,8]{0,1:T(8,128)(2,1)}, u32[]{:S(2)}) copy-start(bf16[2880,8]{0,1:T(8,128)(2,1)} %param.17) | copy-start | bytes 138244
  0.0 6.3 %copy-start.3 = (s32[4,4,4]{2,1,0:T(4,128)S(1)}, s32[4,4,4]{2,1,0:T(4,128)}, u32[]{:S(2)}) copy-start(s32[4,4,4]{2,1,0:T(4,128)} %param.16) | copy-start | bytes 772
  0.0 6.3 %copy-start.1 = (bf16[4,4,2880]{2,1,0:T(4,128)(2,1)S(1)}, bf16[4,4,2880]{2,1,0:T(4,128)(2,1)}, u32[]{:S(2)}) copy-start(bf16[4,4,2880]{2,1,0:T(4,128)(2,1)} %residual_ref.1) | copy-start | bytes 276484
  0.0 13.7 %copy-start.4 = (s32[960]{0:T(1024)S(1)}, s32[960]{0:T(1024)}, u32[]{:S(2)}) copy-start(s32[960]{0:T(1024)} %param.21) | copy-start | bytes 11524
  0.0 13.7 %copy-start = (s32[1,720,3,90]{1,0,3,2:T(1,128)S(1)}, s32[1,720,3,90]{1,0,3,2:T(1,128)}, u32[]{:S(2)}) copy-start(s32[1,720,3,90]{1,0,3,2:T(1,128)} %param.20) | copy-start | bytes 2332804
  4.7 1.6 %collective-permute-start = (f32[16,2880]{1,0:T(8,128)S(1)}, f32[16,2880]{1,0:T(8,128)S(1)}, u32[]{:S(2)}, u32[]{:S(2)}) collective-permute-start(f32[16,2880]{1,0:T(8,128)S(1)} %attention.1.mine_ref), channel_id=1, source_target_pairs={{0,1},{1,0},{2,3},{3,2},{4,5},{5,4},{6,7},{7,6},{8,9},{9,8},{10,11... | collective-permute-start | bytes 552968 | tf_op jit(solution)/shard_map/ppermute | solution.py:373
  6.8 13.3 %collective-permute-start.4 = (bf16[16,2944]{1,0:T(8,128)(2,1)S(1)}, bf16[16,2944]{1,0:T(8,128)(2,1)S(1)}, u32[]{:S(2)}, u32[]{:S(2)}) collective-permute-start(bf16[16,2944]{1,0:T(8,128)(2,1)S(1)} %get-tuple-element.26.rows_ref), channel_id=1, source_target_pairs={{0,12},{1,9},{2,14},{3,11},{4,8},{5,13},{6,10},{7,15},{8,4},{9,1},... | collective-permute-start | bytes 282632 | tf_op jit(solution)/shard_map/ppermute | solution.py:407
  11.8 8.3 %collective-permute-start.3 = (bf16[16,2944]{1,0:T(8,128)(2,1)S(1)}, bf16[16,2944]{1,0:T(8,128)(2,1)S(1)}, u32[]{:S(2)}, u32[]{:S(2)}) collective-permute-start(bf16[16,2944]{1,0:T(8,128)(2,1)S(1)} %get-tuple-element.26.rows_ref), channel_id=1, source_target_pairs={{0,14},{1,11},{2,12},{3,9},{4,10},{5,15},{6,8},{7,13},{8,6},{9,3},... | collective-permute-start | bytes 282632 | tf_op jit(solution)/shard_map/ppermute | solution.py:407
  13.0 7.3 %collective-permute-start.2 = (bf16[16,2944]{1,0:T(8,128)(2,1)S(1)}, bf16[16,2944]{1,0:T(8,128)(2,1)S(1)}, u32[]{:S(2)}, u32[]{:S(2)}) collective-permute-start(bf16[16,2944]{1,0:T(8,128)(2,1)S(1)} %get-tuple-element.26.rows_ref), channel_id=1, source_target_pairs={{0,6},{1,5},{2,4},{3,7},{4,2},{5,1},{6,0},{7,3},{8,14},{9,13},{10,... | collective-permute-start | bytes 282632 | tf_op jit(solution)/shard_map/ppermute | solution.py:407
  13.0 7.3 %collective-permute-start.1 = (bf16[16,2944]{1,0:T(8,128)(2,1)S(1)}, bf16[16,2944]{1,0:T(8,128)(2,1)S(1)}, u32[]{:S(2)}, u32[]{:S(2)}) collective-permute-start(bf16[16,2944]{1,0:T(8,128)(2,1)S(1)} %get-tuple-element.26.rows_ref), channel_id=1, source_target_pairs={{0,0},{1,3},{2,2},{3,1},{4,4},{5,7},{6,6},{7,5},{8,8},{9,11},{10,1... | collective-permute-start | bytes 282632 | tf_op jit(solution)/shard_map/ppermute | solution.py:407
  20.3 2.2 %collective-permute-start.5 = (bf16[16,2944]{1,0:T(8,128)(2,1)S(1)}, bf16[16,2944]{1,0:T(8,128)(2,1)S(1)}, u32[]{:S(2)}, u32[]{:S(2)}) collective-permute-start(bf16[16,2944]{1,0:T(8,128)(2,1)S(1)} %collective-permute-done.4.refs_0_), channel_id=1, source_target_pairs={{0,1},{1,0},{2,3},{3,2},{4,5},{5,4},{6,7},{7,6},{8,9},{9,8},{10,11... | collective-permute-start | bytes 282632 | tf_op jit(solution)/shard_map/ppermute | solution.py:373
  21.6 1.3 %collective-permute-start.6 = (bf16[16,2944]{1,0:T(8,128)(2,1)S(1)}, bf16[16,2944]{1,0:T(8,128)(2,1)S(1)}, u32[]{:S(2)}, u32[]{:S(2)}) collective-permute-start(bf16[16,2944]{1,0:T(8,128)(2,1)S(1)} %collective-permute-done.3.refs_1_), channel_id=1, source_target_pairs={{0,1},{1,0},{2,3},{3,2},{4,5},{5,4},{6,7},{7,6},{8,9},{9,8},{10,11... | collective-permute-start | bytes 282632 | tf_op jit(solution)/shard_map/ppermute | solution.py:373
  21.7 1.4 %collective-permute-start.7 = (bf16[16,2944]{1,0:T(8,128)(2,1)S(1)}, bf16[16,2944]{1,0:T(8,128)(2,1)S(1)}, u32[]{:S(2)}, u32[]{:S(2)}) collective-permute-start(bf16[16,2944]{1,0:T(8,128)(2,1)S(1)} %collective-permute-done.2.refs_2_), channel_id=1, source_target_pairs={{0,1},{1,0},{2,3},{3,2},{4,5},{5,4},{6,7},{7,6},{8,9},{9,8},{10,11... | collective-permute-start | bytes 282632 | tf_op jit(solution)/shard_map/ppermute | solution.py:373
  22.1 1.3 %collective-permute-start.8 = (bf16[16,2944]{1,0:T(8,128)(2,1)S(1)}, bf16[16,2944]{1,0:T(8,128)(2,1)S(1)}, u32[]{:S(2)}, u32[]{:S(2)}) collective-permute-start(bf16[16,2944]{1,0:T(8,128)(2,1)S(1)} %collective-permute-done.1.refs_3_), channel_id=1, source_target_pairs={{0,1},{1,0},{2,3},{3,2},{4,5},{5,4},{6,7},{7,6},{8,9},{9,8},{10,11... | collective-permute-start | bytes 282632 | tf_op jit(solution)/shard_map/ppermute | solution.py:373
  26.8 1.8 %collective-permute-start.9 = (bf16[64,2880]{1,0:T(8,128)(2,1)S(1)}, bf16[64,2880]{1,0:T(8,128)(2,1)S(1)}, u32[]{:S(2)}, u32[]{:S(2)}) collective-permute-start(bf16[64,2880]{1,0:T(8,128)(2,1)S(1)} %get-tuple-element.40), channel_id=1, source_target_pairs={{0,1},{1,0},{2,3},{3,2},{4,5},{5,4},{6,7},{7,6},{8,9},{9,8},{10,11... | collective-permute-start | bytes 1105928 | tf_op jit(solution)/shard_map/ppermute | solution.py:373
  28.7 4.8 %collective-permute-start.10 = (bf16[16,2880]{1,0:T(8,128)(2,1)S(1)}, bf16[16,2880]{1,0:T(8,128)(2,1)S(1)}, u32[]{:S(2)}, u32[]{:S(2)}) collective-permute-start(bf16[16,2880]{1,0:T(8,128)(2,1)S(1)} %get-tuple-element.42), channel_id=1, source_target_pairs={{0,2},{1,3},{2,0},{3,1},{4,6},{5,7},{6,4},{7,5},{8,10},{9,11},{10,... | collective-permute-start | bytes 276488 | tf_op jit(solution)/shard_map/ppermute | solution.py:414
  30.2 5.9 %collective-permute-start.12 = (bf16[16,2880]{1,0:T(8,128)(2,1)S(1)}, bf16[16,2880]{1,0:T(8,128)(2,1)S(1)}, u32[]{:S(2)}, u32[]{:S(2)}) collective-permute-start(bf16[16,2880]{1,0:T(8,128)(2,1)S(1)} %get-tuple-element.43), channel_id=1, source_target_pairs={{6,0},{5,1},{4,2},{7,3},{2,4},{1,5},{0,6},{3,7},{14,8},{13,9},{12,... | collective-permute-start | bytes 276488 | tf_op jit(solution)/shard_map/ppermute | solution.py:416
  30.7 5.4 %collective-permute-start.13 = (bf16[16,2880]{1,0:T(8,128)(2,1)S(1)}, bf16[16,2880]{1,0:T(8,128)(2,1)S(1)}, u32[]{:S(2)}, u32[]{:S(2)}) collective-permute-start(bf16[16,2880]{1,0:T(8,128)(2,1)S(1)} %get-tuple-element.44), channel_id=1, source_target_pairs={{0,0},{3,1},{2,2},{1,3},{4,4},{7,5},{6,6},{5,7},{8,8},{11,9},{10,1... | collective-permute-start | bytes 276488 | tf_op jit(solution)/shard_map/ppermute | solution.py:416
  33.5 6.4 %collective-permute-start.11 = (bf16[16,2880]{1,0:T(8,128)(2,1)S(1)}, bf16[16,2880]{1,0:T(8,128)(2,1)S(1)}, u32[]{:S(2)}, u32[]{:S(2)}) collective-permute-start(bf16[16,2880]{1,0:T(8,128)(2,1)S(1)} %merge.1), channel_id=1, source_target_pairs={{12,0},{9,1},{14,2},{11,3},{8,4},{13,5},{10,6},{15,7},{4,8},{1,9},... | collective-permute-start | bytes 276488 | tf_op jit(solution)/shard_map/ppermute | solution.py:420
  40.0 1.5 %collective-permute-start.14 = (f32[16,2880]{1,0:T(8,128)S(1)}, f32[16,2880]{1,0:T(8,128)S(1)}, u32[]{:S(2)}, u32[]{:S(2)}) collective-permute-start(f32[16,2880]{1,0:T(8,128)S(1)} %convert_add_fusion.mine_ref), channel_id=1, source_target_pairs={{0,1},{1,0},{2,3},{3,2},{4,5},{5,4},{6,7},{7,6},{8,9},{9,8},{10,11... | collective-permute-start | bytes 552968 | tf_op jit(solution)/shard_map/ppermute | solution.py:373

commit v5 on v4

--- a/solution.py
+++ b/solution.py
@@ -13,11 +13,11 @@
 BLOCK = 32
 TILE_UNITS = 6
 LANES = 128
-AHEAD = 3
 F32 = jnp.float32
 BF16 = jnp.bfloat16
 
 NT = (((1,), (1,)), ((), ()))
+TN = (((0,), (0,)), ((), ()))
 
 
 def dot(a, b, dims=(((1,), (0,)), ((), ()))):
@@ -73,11 +73,15 @@
                 (lengths_hbm, lengths),
                 (fresh_hbm, fresh_rows),
                 (cache_hbm, cache_rows),
-                (proj_hbm, proj),
             )
         )
     ]
-    for move in moves:
+    chunk = proj.shape[0] // 4
+    parts = [
+        pltpu.make_async_copy(proj_hbm.at[pl.ds(part * chunk, chunk)], proj.at[pl.ds(part * chunk, chunk)], sems.at[4 + part])
+        for part in range(4)
+    ]
+    for move in moves + parts[:2]:
         move.start()
     steps, rows, _ = queries.shape
     count = steps * rows
@@ -93,6 +97,8 @@
             packed[first : first + rows, :] = jnp.where(mine, piece, 0.0)
             first += groups * count
             packed[first : first + rows, :] = jnp.where(mine, pltpu.roll(piece, HD, 1), 0.0)
+    for move in parts[2:2]:
+        move.start()
     amount = 2 * groups * steps
     span = cache_rows.shape[1] // 2
     spot = iota((amount, span), 1)
@@ -100,6 +106,8 @@
     fresh_spot = iota((amount, count), 1)
     for move in moves[1:4]:
         move.wait()
+    for move in parts[2:]:
+        move.start()
 
     def apart(value, which):
         size = value.shape[0]
@@ -110,21 +118,26 @@
         )
 
     fresh_keys, fresh_values = apart(fresh_rows[...], rows)
+    todo = []
     for row in range(rows):
         now = packed[pl.ds(row, amount, stride=rows), :].astype(BF16)
         keys, values = apart(cache_rows[row], row)
-        scores = jnp.where(spot < lengths[row], dot(now, keys, NT), -1e30)
+        todo.append((row, values, dot(now, keys, NT), dot(now, fresh_keys, NT)))
+    probs = []
+    for row, values, scores, late in todo:
+        scores = jnp.where(spot < lengths[row], scores, -1e30)
         seen = (fresh_spot % rows == row) & (fresh_spot // rows <= step_of)
-        late = jnp.where(seen, dot(now, fresh_keys, NT), -1e30)
+        late = jnp.where(seen, late, -1e30)
         highest = jnp.maximum(
             jnp.max(scores, axis=1, keepdims=True), jnp.max(late, axis=1, keepdims=True)
         )
         scores = jnp.exp(scores - highest)
         late = jnp.exp(late - highest)
         total = jnp.sum(scores, axis=1, keepdims=True) + jnp.sum(late, axis=1, keepdims=True)
-        probs = (scores / total).astype(BF16)
-        late_probs = (late / total).astype(BF16)
-        mixed[pl.ds(row, amount, stride=rows), :] = dot(probs, values) + dot(late_probs, fresh_values)
+        total = 1.0 / total
+        probs.append((row, values, (scores * total).astype(BF16), (late * total).astype(BF16)))
+    for row, values, scores, late in probs:
+        mixed[pl.ds(row, amount, stride=rows), :] = dot(scores, values) + dot(late, fresh_values)
     heads = []
     lane = iota((count, LANES), 1)
     for group in range(groups):
@@ -132,8 +145,11 @@
         turned = mixed[(groups + group) * count : (groups + group + 1) * count, :]
         mine = (lane < HD) == (group < half)
         heads.append(jnp.where(mine, straight, pltpu.roll(turned, HD, 1)).astype(BF16))
-    moves[4].wait()
-    out_ref[...] = dot(jnp.concatenate(heads, axis=1), proj[...], NT)
+    heads = jnp.concatenate(heads, axis=1)
+    for part, move in enumerate(parts):
+        move.wait()
+        here = slice(part * chunk, (part + 1) * chunk)
+        out_ref[:, here] = dot(heads, proj[here, :], NT)
 
 
 def attend(lengths, queries, new_kv, cache_kv, out_proj):
@@ -159,12 +175,10 @@
             pltpu.VMEM((rows + 1, 2 * span, LANES), F32),
             pltpu.VMEM((2 * groups * count, LANES), F32),
             pltpu.VMEM((2 * groups * count, LANES), F32),
-            pltpu.SemaphoreType.DMA((5,)),
+            pltpu.SemaphoreType.DMA((8,)),
         ],
         compiler_params=params(16),
-        cost_estimate=pl.CostEstimate(
-            flops=2 * count * width * model_width, bytes_accessed=7 << 20, transcendentals=0
-        ),
+        cost_estimate=pl.CostEstimate(flops=1000, bytes_accessed=1000, transcendentals=0),
         name="attention",
     )(afar(lengths), afar(queries), afar(fresh), afar(cache), afar(proj))
 
@@ -205,67 +219,47 @@
         in_specs=whole(5),
         out_specs=whole(2),
         compiler_params=params(),
+        cost_estimate=pl.CostEstimate(flops=20_000_000_000, bytes_accessed=40_000_000, transcendentals=0),
         name="normalize",
     )(held(residual), held(mine), held(other), held(routing), held(router.T))
 
 
-def weights_kernel(step, rows_ref, mantissa_hbm, exponent_ref, placement_ref, *refs):
-    out_refs, member_ref, (power, expander, sems) = refs[:-4], refs[-4], refs[-3:]
+def weights_kernel(step, rows_ref, mantissa_ref, exponent_ref, member_ref, *refs):
+    out_refs, table_ref, (power, expander) = refs[:-3], refs[-3], refs[-2:]
     units, blocks = power.shape
     width = expander.shape[1]
-    pieces = [(part, first) for part in range(len(out_refs)) for first in range(0, units, step)]
-    moves = [
-        pltpu.make_async_copy(
-            mantissa_hbm.at[part, pl.ds(first, step), :], out_refs[part].at[pl.ds(first, step), :], sems.at[place]
-        )
-        for place, (part, first) in enumerate(pieces)
-    ]
-    for move in moves[:AHEAD]:
-        move.start()
-
-    experts, slots = placement_ref.shape
-    tiles = units // TILE_UNITS
-    tile = lax.axis_index("expert") * tiles + iota((tiles, slots), 0)
-    lane = iota((slots, LANES), 1) - width % LANES
-    found = jnp.zeros((tiles, LANES), F32)
-    for expert in range(experts):
-        here = (placement_ref[expert : expert + 1, :] == tile).astype(BF16)
-        found += dot(here, ((lane == expert) | (lane == expert + experts)).astype(BF16))
-    spread = (iota((units, tiles), 0) // TILE_UNITS == iota((units, tiles), 1)).astype(BF16)
-    member_ref[...] = dot(spread, found.astype(BF16)).astype(BF16)
+
+    experts = member_ref.shape[0]
+    lane = iota((experts, LANES), 1) - iota((experts, LANES), 0) - width % LANES
+    table_ref[...] = dot(member_ref[...], ((lane == 0) | (lane == experts)).astype(BF16), TN).astype(BF16)
 
     expander[...] = (iota((blocks, width), 1) // BLOCK == iota((blocks, width), 0)).astype(BF16)
-    for place, (part, first) in enumerate(pieces):
-        if first == 0:
-            exponent = exponent_ref[part * blocks : (part + 1) * blocks, 0, :]
-            power[...] = jnp.exp2(exponent.astype(F32)).T.astype(BF16)
-        rows = slice(first, first + step)
-        moves[place].wait()
-        for move in moves[place + AHEAD : place + AHEAD + 1]:
-            move.start()
-        scale = dot(power[rows, :], expander[...])
-        out_refs[part][rows, :] = (out_refs[part][rows, :].astype(F32) * scale).astype(BF16)
-
-
-def dequantize(rows, mantissa, exponent, placement):
+    for part, out_ref in enumerate(out_refs):
+        exponent = exponent_ref[part * blocks : (part + 1) * blocks, 0, :]
+        power[...] = jnp.exp2(exponent.astype(F32)).T.astype(BF16)
+        for first in range(0, units, step):
+            here = slice(first, first + step)
+            scale = dot(power[here, :], expander[...])
+            out_ref[here, :] = (mantissa_ref[part, here, :].astype(F32) * scale).astype(BF16)
+
+
+def dequantize(rows, mantissa, exponent, member):
     parts, units, width = mantissa.shape
     blocks = exponent.shape[0] // parts
-    step = unit_step(units)
-    *weights, member = pl.pallas_call(
-        functools.partial(weights_kernel, step),
+    *weights, table = pl.pallas_call(
+        functools.partial(weights_kernel, unit_step(units)),
         out_shape=(vmem((units, width), BF16),) * parts + (vmem((units, LANES), BF16),),
-        in_specs=whole(1) + [pl.BlockSpec(memory_space=pltpu.HBM)] + whole(2),
+        in_specs=whole(4),
         out_specs=whole(parts + 1),
         scratch_shapes=[
             pltpu.VMEM((units, blocks), BF16),
             pltpu.VMEM((blocks, width), BF16),
-            pltpu.SemaphoreType.DMA((parts * units // step,)),
         ],
         compiler_params=params(14),
         cost_estimate=pl.CostEstimate(flops=1000, bytes_accessed=1000, transcendentals=0),
         name="weights",
-    )(held(rows), afar(mantissa), held(exponent), held(placement))
-    return weights, member
+    )(held(rows), held(mantissa), held(exponent), held(member))
+    return weights, table
 
 
 def experts_kernel(gate_ref, up_ref, down_ref, member_ref, *refs):
@@ -312,9 +306,7 @@
         out_specs=whole(2),
         scratch_shapes=[pltpu.VMEM((count, padded), BF16)],
         compiler_params=params(16),
-        cost_estimate=pl.CostEstimate(
-            flops=6 * count * units * width, bytes_accessed=6 * units * width, transcendentals=0
-        ),
+        cost_estimate=pl.CostEstimate(flops=1000, bytes_accessed=1000, transcendentals=0),
         name="experts",
     )(*[held(kind) for kind in weights], held(member), *[held(block) for block in arrived])
 
@@ -394,6 +386,8 @@
     steps, rows, width = residual.shape
     count = steps * rows
     units = mantissa.shape[1]
+    tile = lax.axis_index("expert") * (units // TILE_UNITS) + jnp.arange(units) // TILE_UNITS
+    member = jnp.any(placement.reshape(EXPERTS, -1, 1) == tile, axis=1).astype(BF16)
     even, odd, close = partners(places)
     turns = even + odd + close
     beside = [(2 * spot + core, 2 * (spot ^ 1) + core) for spot in range(places) for core in range(2)]
@@ -405,7 +399,7 @@
 
     mixed, packed = normalize(residual, partial, swap(partial), routing.reshape(count, TOP), router)
     near = [lax.ppermute(packed, both, pairs) for pairs in turns]
-    weights, member = dequantize(packed, mantissa, exponent, placement.reshape(EXPERTS, -1))
+    weights, member = dequantize(packed, mantissa, exponent, member)
     near, weights, member = lax.optimization_barrier((near[::-1], weights, member))
     near = near[::-1]
     far = [swap(block) for block in near]

time: 42.4 us -> 41.8 us (0.986)
  Pallas kernels: 15.7 us -> 13.1 us
  waiting for transfers between devices: 11.1 us -> 12.7 us
  other arithmetic: 0.04 us -> 0.59 us
    pallas_call x1, Pallas kernels: 6.31 us -> 3.96 us  [dequantize(): pl.pallas_call(functools.partial(weights_kernel, unit_step(units)), out_s...]
    ppermute x4, waiting for transfers between devices: 0.25 us -> 2.1 us  [per_device(): near = [lax.ppermute(packed, both, pairs) for pairs in turns]]
    ppermute x2, starting transfers between devices: 1.13 us -> 2.59 us  [per_device(): lax.ppermute(block, both, [(to, back) for back, to in pairs])]
    ppermute x1, starting transfers between devices: 1.58 us -> 0.32 us  [per_device(): lax.ppermute(block, both, beside)]
    ppermute x7, starting transfers between devices: 3.09 us -> 2.07 us  [swap(): return lax.ppermute(value, 'tensor', [(0, 1), (1, 0)])]
    ppermute x1, starting transfers between devices: 2.58 us -> 3.11 us  [per_device(): lax.ppermute(merge(block, extra), both, [(to, back) for back, to in pairs])]
    reduce_or x0 -> x1, other arithmetic: none -> 0.53 us  [per_device(): jnp.any(placement.reshape(EXPERTS, -1, 1) == tile, axis=1).astype(BF16)]
    ppermute x1, waiting for transfers between devices: 3.85 us -> 3.42 us  [per_device(): lax.ppermute(merge(block, extra), both, [(to, back) for back, to in pairs])]
  transfers between devices with their start and end apart: 15 -> 15, of which waited for: 10 -> 11; matrix products, arithmetic and copies ran while one was open for 0% -> 1% of each run, Pallas kernels for 15% -> 10%
where the time goes in v5:
time: 41.8 us; the launch traced here: 41.6 us
  starting transfers between devices  14.9 us (36%)
  Pallas kernels  13.1 us (31%)
  waiting for transfers between devices  12.7 us (30%)
  other arithmetic  0.59 us (1%)
    ppermute x4, starting transfers between devices, per_device(): near = [lax.ppermute(packed, both, pairs) for pairs in turns]  6.85 us
    ppermute x7, waiting for transfers between devices, swap(): return lax.ppermute(value, 'tensor', [(0, 1), (1, 0)])  5.21 us
    pallas_call x1, Pallas kernels, attend(): pl.pallas_call(attention_kernel, out_shape=vmem((count, model_width), F32...  4.51 us
    pallas_call x1, Pallas kernels, dequantize(): pl.pallas_call(functools.partial(weights_kernel, unit_step(units)), out_s...  3.96 us
    ppermute x1, waiting for transfers between devices, per_device(): lax.ppermute(merge(block, extra), both, [(to, back) for back, to in pairs])  3.42 us
    pallas_call x1, Pallas kernels, run_experts(): pl.pallas_call(experts_kernel, out_shape=(vmem((count // 2, width), F32),...  3.37 us
    ppermute x1, starting transfers between devices, per_device(): lax.ppermute(merge(block, extra), both, [(to, back) for back, to in pairs])  3.11 us
    ppermute x2, starting transfers between devices, per_device(): lax.ppermute(block, both, [(to, back) for back, to in pairs])  2.59 us
  transfers between devices with their start and end apart: 15, of which 11 were waited for; matrix products, arithmetic and copies ran while one was open for 1% of the time, Pallas kernels for 10%

profile of v5, /device:TPU:0, one launch (start us, length us, event | category | flops | bytes accessed | tf_op | source)
XLA Modules:
  0.0 41.6 jit_solution(11517418942210629421)
XLA Ops:
  0.0 4.5 %attention.1.mine_ref = f32[16,2880]{1,0:T(8,128)S(1)} custom-call(s32[4]{0:T(128)} %lengths_hbm.1, bf16[4,4,1024]{2,1,0:T(4,128)(2,1)} %queries_hbm.1, bf16[32,128]{1,0:T(8,128)(2,1)} %bitcast.19, bf16[4,512,128]{2,1,0:T(8,128)(2,1)} %bitcast.18, bf16[2880,1024]{1,0:T(8,128)(2,1)} %bitcast.17), custom_call_target="tpu_custom_call" | custom-call | flops 1000 | bytes 1000 | tf_op jit(solution)/shard_map/attention/pallas_call | solution.py:164
  4.5 0.5 %collective-permute-start = (f32[16,2880]{1,0:T(8,128)S(1)}, f32[16,2880]{1,0:T(8,128)S(1)}, u32[]{:S(2)}, u32[]{:S(2)}) collective-permute-start(f32[16,2880]{1,0:T(8,128)S(1)} %attention.1.mine_ref), channel_id=1, source_target_pairs={{0,1},{1,0},{2,3},{3,2},{4,5},{5,4},{6,7},{7,6},{8,9},{9,8},{10,11... | collective-permute-start | bytes 552968 | tf_op jit(solution)/shard_map/ppermute | solution.py:365
  5.2 1.0 %collective-permute-done.other_ref = f32[16,2880]{1,0:T(8,128)S(1)} collective-permute-done((f32[16,2880]{1,0:T(8,128)S(1)}, f32[16,2880]{1,0:T(8,128)S(1)}, u32[]{:S(2)}, u32[]{:S(2)}) %collective-permute-start) | collective-permute-done | bytes 184352 | tf_op jit(solution)/shard_map/ppermute | solution.py:365
  6.2 0.5 %normalize.1 = (f32[16,2880]{1,0:T(8,128)S(1)}, bf16[16,2944]{1,0:T(8,128)(2,1)S(1)}) custom-call(bf16[4,4,2880]{2,1,0:T(4,128)(2,1)S(1)} %copy-done.1, f32[16,2880]{1,0:T(8,128)S(1)} %attention.1.mine_ref, f32[16,2880]{1,0:T(8,128)S(1)} %collective-permute-done.other_ref, s32[16,4]{1,0:T(8,128)S(1)} %bitcast.16, bf16[8,2880]{1,0:T(8,128)(2,1)S(1)} %bitcast.15), custom_call_target="tpu_custom_call" | custom-call | flops 20000000000 | bytes 40000000 | tf_op jit(solution)/shard_map/normalize/pallas_call | solution.py:216
  6.7 5.0 %collective-permute-start.4 = (bf16[16,2944]{1,0:T(8,128)(2,1)S(1)}, bf16[16,2944]{1,0:T(8,128)(2,1)S(1)}, u32[]{:S(2)}, u32[]{:S(2)}) collective-permute-start(bf16[16,2944]{1,0:T(8,128)(2,1)S(1)} %get-tuple-element.26.rows_ref), channel_id=1, source_target_pairs={{0,12},{1,9},{2,14},{3,11},{4,8},{5,13},{6,10},{7,15},{8,4},{9,1},... | collective-permute-start | bytes 282632 | tf_op jit(solution)/shard_map/ppermute | solution.py:401
  11.7 1.2 %collective-permute-start.3 = (bf16[16,2944]{1,0:T(8,128)(2,1)S(1)}, bf16[16,2944]{1,0:T(8,128)(2,1)S(1)}, u32[]{:S(2)}, u32[]{:S(2)}) collective-permute-start(bf16[16,2944]{1,0:T(8,128)(2,1)S(1)} %get-tuple-element.26.rows_ref), channel_id=1, source_target_pairs={{0,14},{1,11},{2,12},{3,9},{4,10},{5,15},{6,8},{7,13},{8,6},{9,3},... | collective-permute-start | bytes 282632 | tf_op jit(solution)/shard_map/ppermute | solution.py:401
  12.9 0.7 %collective-permute-start.1 = (bf16[16,2944]{1,0:T(8,128)(2,1)S(1)}, bf16[16,2944]{1,0:T(8,128)(2,1)S(1)}, u32[]{:S(2)}, u32[]{:S(2)}) collective-permute-start(bf16[16,2944]{1,0:T(8,128)(2,1)S(1)} %get-tuple-element.26.rows_ref), channel_id=1, source_target_pairs={{0,0},{1,3},{2,2},{3,1},{4,4},{5,7},{6,6},{7,5},{8,8},{9,11},{10,1... | collective-permute-start | bytes 282632 | tf_op jit(solution)/shard_map/ppermute | solution.py:401
  13.6 0.5 %compare_reduce_fusion = pred[8,720]{1,0:T(8,128)(4,1)S(1)} fusion(s32[720]{0:T(1024)S(1)} %fusion, s32[8,120]{1,0:T(8,128)S(1)} %eq.15), kind=kLoop, calls=%fused_computation | loop fusion | flops 1376640 | bytes 12480 | tf_op jit(solution)/shard_map/reduce_or | solution.py:390
  14.2 4.0 %weights.1 = (bf16[720,2880]{1,0:T(8,128)(2,1)S(1)}, bf16[720,2880]{1,0:T(8,128)(2,1)S(1)}, bf16[720,2880]{1,0:T(8,128)(2,1)S(1)}, bf16[720,128]{1,0:T(8,128)(2,1)S(1)}) custom-call(bf16[16,2944]{1,0:T(8,128)(2,1)S(1)} %get-tuple-element.26.rows_ref, bf16[3,720,2880]{2,1,0:T(8,128)(2,1)S(1)} %bitcast.13, s32[270,1,720]{2,1,0:T(1,128)S(1)} %bitcast.14, ...), custom_call_target="tpu_custom_call" | custom-call | flops 1000 | bytes 1000 | tf_op jit(solution)/shard_map/weights/pallas_call | solution.py:249
  18.1 1.1 %collective-permute-done.3.refs_1_ = bf16[16,2944]{1,0:T(8,128)(2,1)S(1)} collective-permute-done((bf16[16,2944]{1,0:T(8,128)(2,1)S(1)}, bf16[16,2944]{1,0:T(8,128)(2,1)S(1)}, u32[]{:S(2)}, u32[]{:S(2)}) %collective-permute-start.3) | collective-permute-done | bytes 94240 | tf_op jit(solution)/shard_map/ppermute | solution.py:401
  19.2 1.0 %collective-permute-done.2.refs_2_ = bf16[16,2944]{1,0:T(8,128)(2,1)S(1)} collective-permute-done((bf16[16,2944]{1,0:T(8,128)(2,1)S(1)}, bf16[16,2944]{1,0:T(8,128)(2,1)S(1)}, u32[]{:S(2)}, u32[]{:S(2)}) %collective-permute-start.2) | collective-permute-done | bytes 94240 | tf_op jit(solution)/shard_map/ppermute | solution.py:401
  20.2 0.7 %collective-permute-start.5 = (bf16[16,2944]{1,0:T(8,128)(2,1)S(1)}, bf16[16,2944]{1,0:T(8,128)(2,1)S(1)}, u32[]{:S(2)}, u32[]{:S(2)}) collective-permute-start(bf16[16,2944]{1,0:T(8,128)(2,1)S(1)} %collective-permute-done.4.refs_0_), channel_id=1, source_target_pairs={{0,1},{1,0},{2,3},{3,2},{4,5},{5,4},{6,7},{7,6},{8,9},{9,8},{10,11... | collective-permute-start | bytes 282632 | tf_op jit(solution)/shard_map/ppermute | solution.py:365
  21.0 0.5 %collective-permute-start.7 = (bf16[16,2944]{1,0:T(8,128)(2,1)S(1)}, bf16[16,2944]{1,0:T(8,128)(2,1)S(1)}, u32[]{:S(2)}, u32[]{:S(2)}) collective-permute-start(bf16[16,2944]{1,0:T(8,128)(2,1)S(1)} %collective-permute-done.2.refs_2_), channel_id=1, source_target_pairs={{0,1},{1,0},{2,3},{3,2},{4,5},{5,4},{6,7},{7,6},{8,9},{9,8},{10,11... | collective-permute-start | bytes 282632 | tf_op jit(solution)/shard_map/ppermute | solution.py:365
  21.5 0.4 %collective-permute-done.5.refs_4_ = bf16[16,2944]{1,0:T(8,128)(2,1)S(1)} collective-permute-done((bf16[16,2944]{1,0:T(8,128)(2,1)S(1)}, bf16[16,2944]{1,0:T(8,128)(2,1)S(1)}, u32[]{:S(2)}, u32[]{:S(2)}) %collective-permute-start.5) | collective-permute-done | bytes 94240 | tf_op jit(solution)/shard_map/ppermute | solution.py:365
  21.9 0.4 collective-permute-done.6.refs_5_
  22.8 3.4 %experts.1 = (f32[64,2880]{1,0:T(8,128)S(1)}, bf16[64,2880]{1,0:T(8,128)(2,1)S(1)}) custom-call(bf16[720,2880]{1,0:T(8,128)(2,1)S(1)} %get-tuple-element.31.gate_ref, bf16[720,2880]{1,0:T(8,128)(2,1)S(1)} %get-tuple-element.32.up_ref, bf16[720,2880]{1,0:T(8,128)(2,1)S(1)} %get-tuple-element.33.down_ref, bf16[720,128]{1,0:T(8,128)(2,1)S(1)} %get-tuple-element.34.member_ref, ...), custom_call_target="tpu_custom_call" | custom-call | flops 1000 | bytes 1000 | tf_op jit(solution)/shard_map/experts/pallas_call | solution.py:302
  26.4 1.5 %collective-permute-done.9.other_ref = bf16[64,2880]{1,0:T(8,128)(2,1)S(1)} collective-permute-done((bf16[64,2880]{1,0:T(8,128)(2,1)S(1)}, bf16[64,2880]{1,0:T(8,128)(2,1)S(1)}, u32[]{:S(2)}, u32[]{:S(2)}) %collective-permute-start.9) | collective-permute-done | bytes 368672 | tf_op jit(solution)/shard_map/ppermute | solution.py:365
  28.3 1.9 %collective-permute-start.12 = (bf16[16,2880]{1,0:T(8,128)(2,1)S(1)}, bf16[16,2880]{1,0:T(8,128)(2,1)S(1)}, u32[]{:S(2)}, u32[]{:S(2)}) collective-permute-start(bf16[16,2880]{1,0:T(8,128)(2,1)S(1)} %get-tuple-element.43), channel_id=1, source_target_pairs={{6,0},{5,1},{4,2},{7,3},{2,4},{1,5},{0,6},{3,7},{14,8},{13,9},{12,... | collective-permute-start | bytes 276488 | tf_op jit(solution)/shard_map/ppermute | solution.py:410
  30.2 0.7 %collective-permute-start.13 = (bf16[16,2880]{1,0:T(8,128)(2,1)S(1)}, bf16[16,2880]{1,0:T(8,128)(2,1)S(1)}, u32[]{:S(2)}, u32[]{:S(2)}) collective-permute-start(bf16[16,2880]{1,0:T(8,128)(2,1)S(1)} %get-tuple-element.44), channel_id=1, source_target_pairs={{0,0},{3,1},{2,2},{1,3},{4,4},{7,5},{6,6},{5,7},{8,8},{11,9},{10,1... | collective-permute-start | bytes 276488 | tf_op jit(solution)/shard_map/ppermute | solution.py:410
  30.9 1.9 %collective-permute-done.10.other_ref = bf16[16,2880]{1,0:T(8,128)(2,1)S(1)} collective-permute-done((bf16[16,2880]{1,0:T(8,128)(2,1)S(1)}, bf16[16,2880]{1,0:T(8,128)(2,1)S(1)}, u32[]{:S(2)}, u32[]{:S(2)}) %collective-permute-start.10) | collective-permute-done | bytes 92192 | tf_op jit(solution)/shard_map/ppermute | solution.py:408
  32.9 3.1 %collective-permute-start.11 = (bf16[16,2880]{1,0:T(8,128)(2,1)S(1)}, bf16[16,2880]{1,0:T(8,128)(2,1)S(1)}, u32[]{:S(2)}, u32[]{:S(2)}) collective-permute-start(bf16[16,2880]{1,0:T(8,128)(2,1)S(1)} %merge.1), channel_id=1, source_target_pairs={{12,0},{9,1},{14,2},{11,3},{8,4},{13,5},{10,6},{15,7},{4,8},{1,9},... | collective-permute-start | bytes 276488 | tf_op jit(solution)/shard_map/ppermute | solution.py:414
  36.0 3.4 %collective-permute-done.11 = bf16[16,2880]{1,0:T(8,128)(2,1)S(1)} collective-permute-done((bf16[16,2880]{1,0:T(8,128)(2,1)S(1)}, bf16[16,2880]{1,0:T(8,128)(2,1)S(1)}, u32[]{:S(2)}, u32[]{:S(2)}) %collective-permute-start.11) | collective-permute-done | bytes 92192 | tf_op jit(solution)/shard_map/ppermute | solution.py:414
  39.5 1.4 %collective-permute-done.14.other_ref = f32[16,2880]{1,0:T(8,128)S(1)} collective-permute-done((f32[16,2880]{1,0:T(8,128)S(1)}, f32[16,2880]{1,0:T(8,128)S(1)}, u32[]{:S(2)}, u32[]{:S(2)}) %collective-permute-start.14) | collective-permute-done | bytes 184352 | tf_op jit(solution)/shard_map/ppermute | solution.py:365
  40.9 0.7 %last.1 = bf16[4,4,2880]{2,1,0:T(4,128)(2,1)} custom-call(f32[16,2880]{1,0:T(8,128)S(1)} %get-tuple-element.25.mixed_ref, f32[16,2880]{1,0:T(8,128)S(1)} %convert_add_fusion.mine_ref, f32[16,2880]{1,0:T(8,128)S(1)} %collective-permute-done.14.other_ref), custom_call_target="tpu_custom_call" | custom-call | tf_op jit(solution)/shard_map/last/pallas_call | solution.py:354
  (37 shorter events, 1.4 us)
Async XLA Ops:
  0.0 5.1 %copy-start.4 = (s32[960]{0:T(1024)S(1)}, s32[960]{0:T(1024)}, u32[]{:S(2)}) copy-start(s32[960]{0:T(1024)} %param.21) | copy-start | bytes 11524
  0.0 6.1 %copy-start.2 = (bf16[2880,8]{0,1:T(8,128)(2,1)S(1)}, bf16[2880,8]{0,1:T(8,128)(2,1)}, u32[]{:S(2)}) copy-start(bf16[2880,8]{0,1:T(8,128)(2,1)} %param.17) | copy-start | bytes 138244
  0.0 6.1 %copy-start.3 = (s32[4,4,4]{2,1,0:T(4,128)S(1)}, s32[4,4,4]{2,1,0:T(4,128)}, u32[]{:S(2)}) copy-start(s32[4,4,4]{2,1,0:T(4,128)} %param.16) | copy-start | bytes 772
  0.0 6.1 %copy-start.1 = (bf16[4,4,2880]{2,1,0:T(4,128)(2,1)S(1)}, bf16[4,4,2880]{2,1,0:T(4,128)(2,1)}, u32[]{:S(2)}) copy-start(bf16[4,4,2880]{2,1,0:T(4,128)(2,1)} %residual_ref.1) | copy-start | bytes 276484
  4.5 1.6 %collective-permute-start = (f32[16,2880]{1,0:T(8,128)S(1)}, f32[16,2880]{1,0:T(8,128)S(1)}, u32[]{:S(2)}, u32[]{:S(2)}) collective-permute-start(f32[16,2880]{1,0:T(8,128)S(1)} %attention.1.mine_ref), channel_id=1, source_target_pairs={{0,1},{1,0},{2,3},{3,2},{4,5},{5,4},{6,7},{7,6},{8,9},{9,8},{10,11... | collective-permute-start | bytes 552968 | tf_op jit(solution)/shard_map/ppermute | solution.py:365
  6.1 8.0 %slice-start = ((s8[12718080]{0:T(1024)(128)(4,1)}), s8[4194304]{0:T(1024)(128)(4,1)S(1)}, s32[]{:S(2)}) async-start(s8[12718080]{0:T(1024)(128)(4,1)} %bitcast.11), calls=%async_computation | async-start | bytes 8388608
  6.1 8.0 %slice-start.1 = ((s8[12718080]{0:T(1024)(128)(4,1)}), s8[4194304]{0:T(1024)(128)(4,1)S(1)}, s32[]{:S(2)}) async-start(s8[12718080]{0:T(1024)(128)(4,1)} %bitcast.11), calls=%async_computation.1 | async-start | bytes 8388608
  6.2 8.0 %slice-start.2 = ((s8[12718080]{0:T(1024)(128)(4,1)}), s8[4194304]{0:T(1024)(128)(4,1)S(1)}, s32[]{:S(2)}) async-start(s8[12718080]{0:T(1024)(128)(4,1)} %bitcast.11), calls=%async_computation.2 | async-start | bytes 8388608
  6.2 8.0 %slice-start.3 = ((s8[12718080]{0:T(1024)(128)(4,1)}), s8[135168]{0:T(1024)(128)(4,1)S(1)}, s32[]{:S(2)}) async-start(s8[12718080]{0:T(1024)(128)(4,1)} %bitcast.11), calls=%async_computation.3 | async-start | bytes 270336
  6.2 8.0 %copy-start = (s32[1,720,3,90]{1,0,3,2:T(1,128)S(1)}, s32[1,720,3,90]{1,0,3,2:T(1,128)}, u32[]{:S(2)}) copy-start(s32[1,720,3,90]{1,0,3,2:T(1,128)} %param.20) | copy-start | bytes 2332804
  6.7 11.4 %collective-permute-start.4 = (bf16[16,2944]{1,0:T(8,128)(2,1)S(1)}, bf16[16,2944]{1,0:T(8,128)(2,1)S(1)}, u32[]{:S(2)}, u32[]{:S(2)}) collective-permute-start(bf16[16,2944]{1,0:T(8,128)(2,1)S(1)} %get-tuple-element.26.rows_ref), channel_id=1, source_target_pairs={{0,12},{1,9},{2,14},{3,11},{4,8},{5,13},{6,10},{7,15},{8,4},{9,1},... | collective-permute-start | bytes 282632 | tf_op jit(solution)/shard_map/ppermute | solution.py:401
  11.7 7.5 %collective-permute-start.3 = (bf16[16,2944]{1,0:T(8,128)(2,1)S(1)}, bf16[16,2944]{1,0:T(8,128)(2,1)S(1)}, u32[]{:S(2)}, u32[]{:S(2)}) collective-permute-start(bf16[16,2944]{1,0:T(8,128)(2,1)S(1)} %get-tuple-element.26.rows_ref), channel_id=1, source_target_pairs={{0,14},{1,11},{2,12},{3,9},{4,10},{5,15},{6,8},{7,13},{8,6},{9,3},... | collective-permute-start | bytes 282632 | tf_op jit(solution)/shard_map/ppermute | solution.py:401
  12.9 7.3 %collective-permute-start.2 = (bf16[16,2944]{1,0:T(8,128)(2,1)S(1)}, bf16[16,2944]{1,0:T(8,128)(2,1)S(1)}, u32[]{:S(2)}, u32[]{:S(2)}) collective-permute-start(bf16[16,2944]{1,0:T(8,128)(2,1)S(1)} %get-tuple-element.26.rows_ref), channel_id=1, source_target_pairs={{0,6},{1,5},{2,4},{3,7},{4,2},{5,1},{6,0},{7,3},{8,14},{9,13},{10,... | collective-permute-start | bytes 282632 | tf_op jit(solution)/shard_map/ppermute | solution.py:401
  12.9 7.3 %collective-permute-start.1 = (bf16[16,2944]{1,0:T(8,128)(2,1)S(1)}, bf16[16,2944]{1,0:T(8,128)(2,1)S(1)}, u32[]{:S(2)}, u32[]{:S(2)}) collective-permute-start(bf16[16,2944]{1,0:T(8,128)(2,1)S(1)} %get-tuple-element.26.rows_ref), channel_id=1, source_target_pairs={{0,0},{1,3},{2,2},{3,1},{4,4},{5,7},{6,6},{7,5},{8,8},{9,11},{10,1... | collective-permute-start | bytes 282632 | tf_op jit(solution)/shard_map/ppermute | solution.py:401
  20.2 1.7 %collective-permute-start.5 = (bf16[16,2944]{1,0:T(8,128)(2,1)S(1)}, bf16[16,2944]{1,0:T(8,128)(2,1)S(1)}, u32[]{:S(2)}, u32[]{:S(2)}) collective-permute-start(bf16[16,2944]{1,0:T(8,128)(2,1)S(1)} %collective-permute-done.4.refs_0_), channel_id=1, source_target_pairs={{0,1},{1,0},{2,3},{3,2},{4,5},{5,4},{6,7},{7,6},{8,9},{9,8},{10,11... | collective-permute-start | bytes 282632 | tf_op jit(solution)/shard_map/ppermute | solution.py:365
  20.9 1.3 %collective-permute-start.6 = (bf16[16,2944]{1,0:T(8,128)(2,1)S(1)}, bf16[16,2944]{1,0:T(8,128)(2,1)S(1)}, u32[]{:S(2)}, u32[]{:S(2)}) collective-permute-start(bf16[16,2944]{1,0:T(8,128)(2,1)S(1)} %collective-permute-done.3.refs_1_), channel_id=1, source_target_pairs={{0,1},{1,0},{2,3},{3,2},{4,5},{5,4},{6,7},{7,6},{8,9},{9,8},{10,11... | collective-permute-start | bytes 282632 | tf_op jit(solution)/shard_map/ppermute | solution.py:365
  21.0 1.4 %collective-permute-start.7 = (bf16[16,2944]{1,0:T(8,128)(2,1)S(1)}, bf16[16,2944]{1,0:T(8,128)(2,1)S(1)}, u32[]{:S(2)}, u32[]{:S(2)}) collective-permute-start(bf16[16,2944]{1,0:T(8,128)(2,1)S(1)} %collective-permute-done.2.refs_2_), channel_id=1, source_target_pairs={{0,1},{1,0},{2,3},{3,2},{4,5},{5,4},{6,7},{7,6},{8,9},{9,8},{10,11... | collective-permute-start | bytes 282632 | tf_op jit(solution)/shard_map/ppermute | solution.py:365
  21.5 1.3 %collective-permute-start.8 = (bf16[16,2944]{1,0:T(8,128)(2,1)S(1)}, bf16[16,2944]{1,0:T(8,128)(2,1)S(1)}, u32[]{:S(2)}, u32[]{:S(2)}) collective-permute-start(bf16[16,2944]{1,0:T(8,128)(2,1)S(1)} %collective-permute-done.1.refs_3_), channel_id=1, source_target_pairs={{0,1},{1,0},{2,3},{3,2},{4,5},{5,4},{6,7},{7,6},{8,9},{9,8},{10,11... | collective-permute-start | bytes 282632 | tf_op jit(solution)/shard_map/ppermute | solution.py:365
  26.1 1.8 %collective-permute-start.9 = (bf16[64,2880]{1,0:T(8,128)(2,1)S(1)}, bf16[64,2880]{1,0:T(8,128)(2,1)S(1)}, u32[]{:S(2)}, u32[]{:S(2)}) collective-permute-start(bf16[64,2880]{1,0:T(8,128)(2,1)S(1)} %get-tuple-element.40), channel_id=1, source_target_pairs={{0,1},{1,0},{2,3},{3,2},{4,5},{5,4},{6,7},{7,6},{8,9},{9,8},{10,11... | collective-permute-start | bytes 1105928 | tf_op jit(solution)/shard_map/ppermute | solution.py:365
  28.0 4.8 %collective-permute-start.10 = (bf16[16,2880]{1,0:T(8,128)(2,1)S(1)}, bf16[16,2880]{1,0:T(8,128)(2,1)S(1)}, u32[]{:S(2)}, u32[]{:S(2)}) collective-permute-start(bf16[16,2880]{1,0:T(8,128)(2,1)S(1)} %get-tuple-element.42), channel_id=1, source_target_pairs={{0,2},{1,3},{2,0},{3,1},{4,6},{5,7},{6,4},{7,5},{8,10},{9,11},{10,... | collective-permute-start | bytes 276488 | tf_op jit(solution)/shard_map/ppermute | solution.py:408
  28.3 7.7 %collective-permute-start.12 = (bf16[16,2880]{1,0:T(8,128)(2,1)S(1)}, bf16[16,2880]{1,0:T(8,128)(2,1)S(1)}, u32[]{:S(2)}, u32[]{:S(2)}) collective-permute-start(bf16[16,2880]{1,0:T(8,128)(2,1)S(1)} %get-tuple-element.43), channel_id=1, source_target_pairs={{6,0},{5,1},{4,2},{7,3},{2,4},{1,5},{0,6},{3,7},{14,8},{13,9},{12,... | collective-permute-start | bytes 276488 | tf_op jit(solution)/shard_map/ppermute | solution.py:410
  30.2 5.7 %collective-permute-start.13 = (bf16[16,2880]{1,0:T(8,128)(2,1)S(1)}, bf16[16,2880]{1,0:T(8,128)(2,1)S(1)}, u32[]{:S(2)}, u32[]{:S(2)}) collective-permute-start(bf16[16,2880]{1,0:T(8,128)(2,1)S(1)} %get-tuple-element.44), channel_id=1, source_target_pairs={{0,0},{3,1},{2,2},{1,3},{4,4},{7,5},{6,6},{5,7},{8,8},{11,9},{10,1... | collective-permute-start | bytes 276488 | tf_op jit(solution)/shard_map/ppermute | solution.py:410
  32.9 6.5 %collective-permute-start.11 = (bf16[16,2880]{1,0:T(8,128)(2,1)S(1)}, bf16[16,2880]{1,0:T(8,128)(2,1)S(1)}, u32[]{:S(2)}, u32[]{:S(2)}) collective-permute-start(bf16[16,2880]{1,0:T(8,128)(2,1)S(1)} %merge.1), channel_id=1, source_target_pairs={{12,0},{9,1},{14,2},{11,3},{8,4},{13,5},{10,6},{15,7},{4,8},{1,9},... | collective-permute-start | bytes 276488 | tf_op jit(solution)/shard_map/ppermute | solution.py:414
  39.5 1.5 %collective-permute-start.14 = (f32[16,2880]{1,0:T(8,128)S(1)}, f32[16,2880]{1,0:T(8,128)S(1)}, u32[]{:S(2)}, u32[]{:S(2)}) collective-permute-start(f32[16,2880]{1,0:T(8,128)S(1)} %convert_add_fusion.mine_ref), channel_id=1, source_target_pairs={{0,1},{1,0},{2,3},{3,2},{4,5},{5,4},{6,7},{7,6},{8,9},{9,8},{10,11... | collective-permute-start | bytes 552968 | tf_op jit(solution)/shard_map/ppermute | solution.py:365

commit v6 on v5

--- a/solution.py
+++ b/solution.py
@@ -400,8 +400,10 @@
     mixed, packed = normalize(residual, partial, swap(partial), routing.reshape(count, TOP), router)
     near = [lax.ppermute(packed, both, pairs) for pairs in turns]
     weights, member = dequantize(packed, mantissa, exponent, member)
-    near, weights, member = lax.optimization_barrier((near[::-1], weights, member))
-    near = near[::-1]
+    order = list(range(len(turns)))[::-1]
+    order = order[: len(close)] + order[len(close) + len(odd) :] + order[len(close) : len(close) + len(odd)]
+    arrived, weights, member = lax.optimization_barrier(([near[turn] for turn in order], weights, member))
+    near = [arrived[order.index(turn)] for turn in range(len(turns))]
     far = [swap(block) for block in near]
     mine, other = run_experts(weights, member, near + far)
     sums = join(mine, swap(other), count, len(even))

time: 41.8 us -> 41.3 us (0.988)
  waiting for transfers between devices: 12.7 us -> 10.7 us
  starting transfers between devices: 14.9 us -> 16.5 us
    ppermute x7, waiting for transfers between devices: 5.21 us -> 4.31 us  [swap(): return lax.ppermute(value, 'tensor', [(0, 1), (1, 0)])]
    ppermute x1, starting transfers between devices: 0.32 us -> 1.01 us  [per_device(): lax.ppermute(block, both, beside)]
    ppermute x1, waiting for transfers between devices: 3.42 us -> 2.8 us  [per_device(): lax.ppermute(merge(block, extra), both, [(to, back) for back, to in pairs])]
    ppermute x1, starting transfers between devices: 3.11 us -> 3.63 us  [per_device(): lax.ppermute(merge(block, extra), both, [(to, back) for back, to in pairs])]
    ppermute x7, starting transfers between devices: 2.07 us -> 2.53 us  [swap(): return lax.ppermute(value, 'tensor', [(0, 1), (1, 0)])]
  transfers between devices with their start and end apart: 15 -> 15, of which waited for: 11 -> 11; matrix products, arithmetic and copies ran while one was open for 1% -> 2% of each run, Pallas kernels for 10% -> 10%
where the time goes in v6:
time: 41.3 us; the launch traced here: 41.1 us
  starting transfers between devices  16.5 us (40%)
  Pallas kernels  13.1 us (32%)
  waiting for transfers between devices  10.7 us (26%)
  other arithmetic  0.59 us (1%)
    ppermute x4, starting transfers between devices, per_device(): near = [lax.ppermute(packed, both, pairs) for pairs in turns]  6.85 us
    pallas_call x1, Pallas kernels, attend(): pl.pallas_call(attention_kernel, out_shape=vmem((count, model_width), F32...  4.51 us
    ppermute x7, waiting for transfers between devices, swap(): return lax.ppermute(value, 'tensor', [(0, 1), (1, 0)])  4.31 us
    pallas_call x1, Pallas kernels, dequantize(): pl.pallas_call(functools.partial(weights_kernel, unit_step(units)), out_s...  3.96 us
    ppermute x1, starting transfers between devices, per_device(): lax.ppermute(merge(block, extra), both, [(to, back) for back, to in pairs])  3.63 us
    pallas_call x1, Pallas kernels, run_experts(): pl.pallas_call(experts_kernel, out_shape=(vmem((count // 2, width), F32),...  3.37 us
    ppermute x1, waiting for transfers between devices, per_device(): lax.ppermute(merge(block, extra), both, [(to, back) for back, to in pairs])  2.8 us
    ppermute x7, starting transfers between devices, swap(): return lax.ppermute(value, 'tensor', [(0, 1), (1, 0)])  2.53 us
  transfers between devices with their start and end apart: 15, of which 11 were waited for; matrix products, arithmetic and copies ran while one was open for 2% of the time, Pallas kernels for 10%

profile of v6, /device:TPU:0, one launch (start us, length us, event | category | flops | bytes accessed | tf_op | source)
XLA Modules:
  0.0 41.1 jit_solution(12436872094155222611)
XLA Ops:
  0.0 4.5 %attention.1.mine_ref = f32[16,2880]{1,0:T(8,128)S(1)} custom-call(s32[4]{0:T(128)} %lengths_hbm.1, bf16[4,4,1024]{2,1,0:T(4,128)(2,1)} %queries_hbm.1, bf16[32,128]{1,0:T(8,128)(2,1)} %bitcast.19, bf16[4,512,128]{2,1,0:T(8,128)(2,1)} %bitcast.18, bf16[2880,1024]{1,0:T(8,128)(2,1)} %bitcast.17), custom_call_target="tpu_custom_call" | custom-call | flops 1000 | bytes 1000 | tf_op jit(solution)/shard_map/attention/pallas_call | solution.py:164
  4.5 0.5 %collective-permute-start = (f32[16,2880]{1,0:T(8,128)S(1)}, f32[16,2880]{1,0:T(8,128)S(1)}, u32[]{:S(2)}, u32[]{:S(2)}) collective-permute-start(f32[16,2880]{1,0:T(8,128)S(1)} %attention.1.mine_ref), channel_id=1, source_target_pairs={{0,1},{1,0},{2,3},{3,2},{4,5},{5,4},{6,7},{7,6},{8,9},{9,8},{10,11... | collective-permute-start | bytes 552968 | tf_op jit(solution)/shard_map/ppermute | solution.py:365
  5.2 1.0 %collective-permute-done.other_ref = f32[16,2880]{1,0:T(8,128)S(1)} collective-permute-done((f32[16,2880]{1,0:T(8,128)S(1)}, f32[16,2880]{1,0:T(8,128)S(1)}, u32[]{:S(2)}, u32[]{:S(2)}) %collective-permute-start) | collective-permute-done | bytes 184352 | tf_op jit(solution)/shard_map/ppermute | solution.py:365
  6.2 0.5 %normalize.1 = (f32[16,2880]{1,0:T(8,128)S(1)}, bf16[16,2944]{1,0:T(8,128)(2,1)S(1)}) custom-call(bf16[4,4,2880]{2,1,0:T(4,128)(2,1)S(1)} %copy-done.1, f32[16,2880]{1,0:T(8,128)S(1)} %attention.1.mine_ref, f32[16,2880]{1,0:T(8,128)S(1)} %collective-permute-done.other_ref, s32[16,4]{1,0:T(8,128)S(1)} %bitcast.16, bf16[8,2880]{1,0:T(8,128)(2,1)S(1)} %bitcast.15), custom_call_target="tpu_custom_call" | custom-call | flops 20000000000 | bytes 40000000 | tf_op jit(solution)/shard_map/normalize/pallas_call | solution.py:216
  6.7 6.0 %collective-permute-start.4 = (bf16[16,2944]{1,0:T(8,128)(2,1)S(1)}, bf16[16,2944]{1,0:T(8,128)(2,1)S(1)}, u32[]{:S(2)}, u32[]{:S(2)}) collective-permute-start(bf16[16,2944]{1,0:T(8,128)(2,1)S(1)} %get-tuple-element.26.rows_ref), channel_id=1, source_target_pairs={{0,14},{1,11},{2,12},{3,9},{4,10},{5,15},{6,8},{7,13},{8,6},{9,3},... | collective-permute-start | bytes 282632 | tf_op jit(solution)/shard_map/ppermute | solution.py:401
  12.9 0.7 %collective-permute-start.1 = (bf16[16,2944]{1,0:T(8,128)(2,1)S(1)}, bf16[16,2944]{1,0:T(8,128)(2,1)S(1)}, u32[]{:S(2)}, u32[]{:S(2)}) collective-permute-start(bf16[16,2944]{1,0:T(8,128)(2,1)S(1)} %get-tuple-element.26.rows_ref), channel_id=1, source_target_pairs={{0,0},{1,3},{2,2},{3,1},{4,4},{5,7},{6,6},{7,5},{8,8},{9,11},{10,1... | collective-permute-start | bytes 282632 | tf_op jit(solution)/shard_map/ppermute | solution.py:401
  13.6 0.5 %compare_reduce_fusion = pred[8,720]{1,0:T(8,128)(4,1)S(1)} fusion(s32[720]{0:T(1024)S(1)} %fusion, s32[8,120]{1,0:T(8,128)S(1)} %eq.15), kind=kLoop, calls=%fused_computation | loop fusion | flops 1376640 | bytes 12480 | tf_op jit(solution)/shard_map/reduce_or | solution.py:390
  14.2 4.0 %weights.1 = (bf16[720,2880]{1,0:T(8,128)(2,1)S(1)}, bf16[720,2880]{1,0:T(8,128)(2,1)S(1)}, bf16[720,2880]{1,0:T(8,128)(2,1)S(1)}, bf16[720,128]{1,0:T(8,128)(2,1)S(1)}) custom-call(bf16[16,2944]{1,0:T(8,128)(2,1)S(1)} %get-tuple-element.26.rows_ref, bf16[3,720,2880]{2,1,0:T(8,128)(2,1)S(1)} %bitcast.13, s32[270,1,720]{2,1,0:T(1,128)S(1)} %bitcast.14, ...), custom_call_target="tpu_custom_call" | custom-call | flops 1000 | bytes 1000 | tf_op jit(solution)/shard_map/weights/pallas_call | solution.py:249
  18.1 1.0 %collective-permute-done.3.refs_0_ = bf16[16,2944]{1,0:T(8,128)(2,1)S(1)} collective-permute-done((bf16[16,2944]{1,0:T(8,128)(2,1)S(1)}, bf16[16,2944]{1,0:T(8,128)(2,1)S(1)}, u32[]{:S(2)}, u32[]{:S(2)}) %collective-permute-start.3) | collective-permute-done | bytes 94240 | tf_op jit(solution)/shard_map/ppermute | solution.py:401
  19.1 0.9 %collective-permute-done.2.refs_2_ = bf16[16,2944]{1,0:T(8,128)(2,1)S(1)} collective-permute-done((bf16[16,2944]{1,0:T(8,128)(2,1)S(1)}, bf16[16,2944]{1,0:T(8,128)(2,1)S(1)}, u32[]{:S(2)}, u32[]{:S(2)}) %collective-permute-start.2) | collective-permute-done | bytes 94240 | tf_op jit(solution)/shard_map/ppermute | solution.py:401
  20.1 0.5 %collective-permute-start.6 = (bf16[16,2944]{1,0:T(8,128)(2,1)S(1)}, bf16[16,2944]{1,0:T(8,128)(2,1)S(1)}, u32[]{:S(2)}, u32[]{:S(2)}) collective-permute-start(bf16[16,2944]{1,0:T(8,128)(2,1)S(1)} %collective-permute-done.4.refs_1_), channel_id=1, source_target_pairs={{0,1},{1,0},{2,3},{3,2},{4,5},{5,4},{6,7},{7,6},{8,9},{9,8},{10,11... | collective-permute-start | bytes 282632 | tf_op jit(solution)/shard_map/ppermute | solution.py:365
  20.6 0.5 %collective-permute-start.8 = (bf16[16,2944]{1,0:T(8,128)(2,1)S(1)}, bf16[16,2944]{1,0:T(8,128)(2,1)S(1)}, u32[]{:S(2)}, u32[]{:S(2)}) collective-permute-start(bf16[16,2944]{1,0:T(8,128)(2,1)S(1)} %collective-permute-done.1.refs_3_), channel_id=1, source_target_pairs={{0,1},{1,0},{2,3},{3,2},{4,5},{5,4},{6,7},{7,6},{8,9},{9,8},{10,11... | collective-permute-start | bytes 282632 | tf_op jit(solution)/shard_map/ppermute | solution.py:365
  22.1 3.4 %experts.1 = (f32[64,2880]{1,0:T(8,128)S(1)}, bf16[64,2880]{1,0:T(8,128)(2,1)S(1)}) custom-call(bf16[720,2880]{1,0:T(8,128)(2,1)S(1)} %get-tuple-element.31.gate_ref, bf16[720,2880]{1,0:T(8,128)(2,1)S(1)} %get-tuple-element.32.up_ref, bf16[720,2880]{1,0:T(8,128)(2,1)S(1)} %get-tuple-element.33.down_ref, bf16[720,128]{1,0:T(8,128)(2,1)S(1)} %get-tuple-element.34.member_ref, ...), custom_call_target="tpu_custom_call" | custom-call | flops 1000 | bytes 1000 | tf_op jit(solution)/shard_map/experts/pallas_call | solution.py:302
  25.4 0.4 %collective-permute-start.9 = (bf16[64,2880]{1,0:T(8,128)(2,1)S(1)}, bf16[64,2880]{1,0:T(8,128)(2,1)S(1)}, u32[]{:S(2)}, u32[]{:S(2)}) collective-permute-start(bf16[64,2880]{1,0:T(8,128)(2,1)S(1)} %get-tuple-element.40), channel_id=1, source_target_pairs={{0,1},{1,0},{2,3},{3,2},{4,5},{5,4},{6,7},{7,6},{8,9},{9,8},{10,11... | collective-permute-start | bytes 1105928 | tf_op jit(solution)/shard_map/ppermute | solution.py:365
  25.9 1.3 %collective-permute-done.9.other_ref = bf16[64,2880]{1,0:T(8,128)(2,1)S(1)} collective-permute-done((bf16[64,2880]{1,0:T(8,128)(2,1)S(1)}, bf16[64,2880]{1,0:T(8,128)(2,1)S(1)}, u32[]{:S(2)}, u32[]{:S(2)}) %collective-permute-start.9) | collective-permute-done | bytes 368672 | tf_op jit(solution)/shard_map/ppermute | solution.py:365
  27.3 1.0 %collective-permute-start.10 = (bf16[16,2880]{1,0:T(8,128)(2,1)S(1)}, bf16[16,2880]{1,0:T(8,128)(2,1)S(1)}, u32[]{:S(2)}, u32[]{:S(2)}) collective-permute-start(bf16[16,2880]{1,0:T(8,128)(2,1)S(1)} %get-tuple-element.42), channel_id=1, source_target_pairs={{0,2},{1,3},{2,0},{3,1},{4,6},{5,7},{6,4},{7,5},{8,10},{9,11},{10,... | collective-permute-start | bytes 276488 | tf_op jit(solution)/shard_map/ppermute | solution.py:410
  28.3 1.8 %collective-permute-start.12 = (bf16[16,2880]{1,0:T(8,128)(2,1)S(1)}, bf16[16,2880]{1,0:T(8,128)(2,1)S(1)}, u32[]{:S(2)}, u32[]{:S(2)}) collective-permute-start(bf16[16,2880]{1,0:T(8,128)(2,1)S(1)} %get-tuple-element.43), channel_id=1, source_target_pairs={{6,0},{5,1},{4,2},{7,3},{2,4},{1,5},{0,6},{3,7},{14,8},{13,9},{12,... | collective-permute-start | bytes 276488 | tf_op jit(solution)/shard_map/ppermute | solution.py:412
  30.1 0.7 %collective-permute-start.13 = (bf16[16,2880]{1,0:T(8,128)(2,1)S(1)}, bf16[16,2880]{1,0:T(8,128)(2,1)S(1)}, u32[]{:S(2)}, u32[]{:S(2)}) collective-permute-start(bf16[16,2880]{1,0:T(8,128)(2,1)S(1)} %get-tuple-element.44), channel_id=1, source_target_pairs={{0,0},{3,1},{2,2},{1,3},{4,4},{7,5},{6,6},{5,7},{8,8},{11,9},{10,1... | collective-permute-start | bytes 276488 | tf_op jit(solution)/shard_map/ppermute | solution.py:412
  30.8 1.6 %collective-permute-done.10.other_ref = bf16[16,2880]{1,0:T(8,128)(2,1)S(1)} collective-permute-done((bf16[16,2880]{1,0:T(8,128)(2,1)S(1)}, bf16[16,2880]{1,0:T(8,128)(2,1)S(1)}, u32[]{:S(2)}, u32[]{:S(2)}) %collective-permute-start.10) | collective-permute-done | bytes 92192 | tf_op jit(solution)/shard_map/ppermute | solution.py:410
  32.4 3.6 %collective-permute-start.11 = (bf16[16,2880]{1,0:T(8,128)(2,1)S(1)}, bf16[16,2880]{1,0:T(8,128)(2,1)S(1)}, u32[]{:S(2)}, u32[]{:S(2)}) collective-permute-start(bf16[16,2880]{1,0:T(8,128)(2,1)S(1)} %merge.1), channel_id=1, source_target_pairs={{12,0},{9,1},{14,2},{11,3},{8,4},{13,5},{10,6},{15,7},{4,8},{1,9},... | collective-permute-start | bytes 276488 | tf_op jit(solution)/shard_map/ppermute | solution.py:416
  36.0 2.8 %collective-permute-done.11 = bf16[16,2880]{1,0:T(8,128)(2,1)S(1)} collective-permute-done((bf16[16,2880]{1,0:T(8,128)(2,1)S(1)}, bf16[16,2880]{1,0:T(8,128)(2,1)S(1)}, u32[]{:S(2)}, u32[]{:S(2)}) %collective-permute-start.11) | collective-permute-done | bytes 92192 | tf_op jit(solution)/shard_map/ppermute | solution.py:416
  38.8 0.5 %collective-permute-start.14 = (f32[16,2880]{1,0:T(8,128)S(1)}, f32[16,2880]{1,0:T(8,128)S(1)}, u32[]{:S(2)}, u32[]{:S(2)}) collective-permute-start(f32[16,2880]{1,0:T(8,128)S(1)} %convert_add_fusion.mine_ref), channel_id=1, source_target_pairs={{0,1},{1,0},{2,3},{3,2},{4,5},{5,4},{6,7},{7,6},{8,9},{9,8},{10,11... | collective-permute-start | bytes 552968 | tf_op jit(solution)/shard_map/ppermute | solution.py:365
  39.4 1.1 %collective-permute-done.14.other_ref = f32[16,2880]{1,0:T(8,128)S(1)} collective-permute-done((f32[16,2880]{1,0:T(8,128)S(1)}, f32[16,2880]{1,0:T(8,128)S(1)}, u32[]{:S(2)}, u32[]{:S(2)}) %collective-permute-start.14) | collective-permute-done | bytes 184352 | tf_op jit(solution)/shard_map/ppermute | solution.py:365
  40.4 0.7 %last.1 = bf16[4,4,2880]{2,1,0:T(4,128)(2,1)} custom-call(f32[16,2880]{1,0:T(8,128)S(1)} %get-tuple-element.25.mixed_ref, f32[16,2880]{1,0:T(8,128)S(1)} %convert_add_fusion.mine_ref, f32[16,2880]{1,0:T(8,128)S(1)} %collective-permute-done.14.other_ref), custom_call_target="tpu_custom_call" | custom-call | tf_op jit(solution)/shard_map/last/pallas_call | solution.py:354
  (37 shorter events, 1.5 us)
Async XLA Ops:
  0.0 5.1 %copy-start.4 = (s32[960]{0:T(1024)S(1)}, s32[960]{0:T(1024)}, u32[]{:S(2)}) copy-start(s32[960]{0:T(1024)} %param.21) | copy-start | bytes 11524
  0.0 6.1 %copy-start.2 = (bf16[2880,8]{0,1:T(8,128)(2,1)S(1)}, bf16[2880,8]{0,1:T(8,128)(2,1)}, u32[]{:S(2)}) copy-start(bf16[2880,8]{0,1:T(8,128)(2,1)} %param.17) | copy-start | bytes 138244
  0.0 6.1 %copy-start.3 = (s32[4,4,4]{2,1,0:T(4,128)S(1)}, s32[4,4,4]{2,1,0:T(4,128)}, u32[]{:S(2)}) copy-start(s32[4,4,4]{2,1,0:T(4,128)} %param.16) | copy-start | bytes 772
  0.0 6.1 %copy-start.1 = (bf16[4,4,2880]{2,1,0:T(4,128)(2,1)S(1)}, bf16[4,4,2880]{2,1,0:T(4,128)(2,1)}, u32[]{:S(2)}) copy-start(bf16[4,4,2880]{2,1,0:T(4,128)(2,1)} %residual_ref.1) | copy-start | bytes 276484
  4.5 1.6 %collective-permute-start = (f32[16,2880]{1,0:T(8,128)S(1)}, f32[16,2880]{1,0:T(8,128)S(1)}, u32[]{:S(2)}, u32[]{:S(2)}) collective-permute-start(f32[16,2880]{1,0:T(8,128)S(1)} %attention.1.mine_ref), channel_id=1, source_target_pairs={{0,1},{1,0},{2,3},{3,2},{4,5},{5,4},{6,7},{7,6},{8,9},{9,8},{10,11... | collective-permute-start | bytes 552968 | tf_op jit(solution)/shard_map/ppermute | solution.py:365
  6.1 8.0 %slice-start = ((s8[12718080]{0:T(1024)(128)(4,1)}), s8[4194304]{0:T(1024)(128)(4,1)S(1)}, s32[]{:S(2)}) async-start(s8[12718080]{0:T(1024)(128)(4,1)} %bitcast.11), calls=%async_computation | async-start | bytes 8388608
  6.1 8.0 %slice-start.1 = ((s8[12718080]{0:T(1024)(128)(4,1)}), s8[4194304]{0:T(1024)(128)(4,1)S(1)}, s32[]{:S(2)}) async-start(s8[12718080]{0:T(1024)(128)(4,1)} %bitcast.11), calls=%async_computation.1 | async-start | bytes 8388608
  6.2 8.0 %slice-start.2 = ((s8[12718080]{0:T(1024)(128)(4,1)}), s8[4194304]{0:T(1024)(128)(4,1)S(1)}, s32[]{:S(2)}) async-start(s8[12718080]{0:T(1024)(128)(4,1)} %bitcast.11), calls=%async_computation.2 | async-start | bytes 8388608
  6.2 8.0 %slice-start.3 = ((s8[12718080]{0:T(1024)(128)(4,1)}), s8[135168]{0:T(1024)(128)(4,1)S(1)}, s32[]{:S(2)}) async-start(s8[12718080]{0:T(1024)(128)(4,1)} %bitcast.11), calls=%async_computation.3 | async-start | bytes 270336
  6.2 8.0 %copy-start = (s32[1,720,3,90]{1,0,3,2:T(1,128)S(1)}, s32[1,720,3,90]{1,0,3,2:T(1,128)}, u32[]{:S(2)}) copy-start(s32[1,720,3,90]{1,0,3,2:T(1,128)} %param.20) | copy-start | bytes 2332804
  6.7 11.4 %collective-permute-start.4 = (bf16[16,2944]{1,0:T(8,128)(2,1)S(1)}, bf16[16,2944]{1,0:T(8,128)(2,1)S(1)}, u32[]{:S(2)}, u32[]{:S(2)}) collective-permute-start(bf16[16,2944]{1,0:T(8,128)(2,1)S(1)} %get-tuple-element.26.rows_ref), channel_id=1, source_target_pairs={{0,14},{1,11},{2,12},{3,9},{4,10},{5,15},{6,8},{7,13},{8,6},{9,3},... | collective-permute-start | bytes 282632 | tf_op jit(solution)/shard_map/ppermute | solution.py:401
  12.7 6.5 %collective-permute-start.3 = (bf16[16,2944]{1,0:T(8,128)(2,1)S(1)}, bf16[16,2944]{1,0:T(8,128)(2,1)S(1)}, u32[]{:S(2)}, u32[]{:S(2)}) collective-permute-start(bf16[16,2944]{1,0:T(8,128)(2,1)S(1)} %get-tuple-element.26.rows_ref), channel_id=1, source_target_pairs={{0,12},{1,9},{2,14},{3,11},{4,8},{5,13},{6,10},{7,15},{8,4},{9,1},... | collective-permute-start | bytes 282632 | tf_op jit(solution)/shard_map/ppermute | solution.py:401
  12.9 7.2 %collective-permute-start.2 = (bf16[16,2944]{1,0:T(8,128)(2,1)S(1)}, bf16[16,2944]{1,0:T(8,128)(2,1)S(1)}, u32[]{:S(2)}, u32[]{:S(2)}) collective-permute-start(bf16[16,2944]{1,0:T(8,128)(2,1)S(1)} %get-tuple-element.26.rows_ref), channel_id=1, source_target_pairs={{0,6},{1,5},{2,4},{3,7},{4,2},{5,1},{6,0},{7,3},{8,14},{9,13},{10,... | collective-permute-start | bytes 282632 | tf_op jit(solution)/shard_map/ppermute | solution.py:401
  12.9 7.2 %collective-permute-start.1 = (bf16[16,2944]{1,0:T(8,128)(2,1)S(1)}, bf16[16,2944]{1,0:T(8,128)(2,1)S(1)}, u32[]{:S(2)}, u32[]{:S(2)}) collective-permute-start(bf16[16,2944]{1,0:T(8,128)(2,1)S(1)} %get-tuple-element.26.rows_ref), channel_id=1, source_target_pairs={{0,0},{1,3},{2,2},{3,1},{4,4},{5,7},{6,6},{7,5},{8,8},{9,11},{10,1... | collective-permute-start | bytes 282632 | tf_op jit(solution)/shard_map/ppermute | solution.py:401
  20.1 1.3 %collective-permute-start.5 = (bf16[16,2944]{1,0:T(8,128)(2,1)S(1)}, bf16[16,2944]{1,0:T(8,128)(2,1)S(1)}, u32[]{:S(2)}, u32[]{:S(2)}) collective-permute-start(bf16[16,2944]{1,0:T(8,128)(2,1)S(1)} %collective-permute-done.3.refs_0_), channel_id=1, source_target_pairs={{0,1},{1,0},{2,3},{3,2},{4,5},{5,4},{6,7},{7,6},{8,9},{9,8},{10,11... | collective-permute-start | bytes 282632 | tf_op jit(solution)/shard_map/ppermute | solution.py:365
  20.1 1.4 %collective-permute-start.6 = (bf16[16,2944]{1,0:T(8,128)(2,1)S(1)}, bf16[16,2944]{1,0:T(8,128)(2,1)S(1)}, u32[]{:S(2)}, u32[]{:S(2)}) collective-permute-start(bf16[16,2944]{1,0:T(8,128)(2,1)S(1)} %collective-permute-done.4.refs_1_), channel_id=1, source_target_pairs={{0,1},{1,0},{2,3},{3,2},{4,5},{5,4},{6,7},{7,6},{8,9},{9,8},{10,11... | collective-permute-start | bytes 282632 | tf_op jit(solution)/shard_map/ppermute | solution.py:365
  20.6 1.3 %collective-permute-start.7 = (bf16[16,2944]{1,0:T(8,128)(2,1)S(1)}, bf16[16,2944]{1,0:T(8,128)(2,1)S(1)}, u32[]{:S(2)}, u32[]{:S(2)}) collective-permute-start(bf16[16,2944]{1,0:T(8,128)(2,1)S(1)} %collective-permute-done.2.refs_2_), channel_id=1, source_target_pairs={{0,1},{1,0},{2,3},{3,2},{4,5},{5,4},{6,7},{7,6},{8,9},{9,8},{10,11... | collective-permute-start | bytes 282632 | tf_op jit(solution)/shard_map/ppermute | solution.py:365
  20.6 1.4 %collective-permute-start.8 = (bf16[16,2944]{1,0:T(8,128)(2,1)S(1)}, bf16[16,2944]{1,0:T(8,128)(2,1)S(1)}, u32[]{:S(2)}, u32[]{:S(2)}) collective-permute-start(bf16[16,2944]{1,0:T(8,128)(2,1)S(1)} %collective-permute-done.1.refs_3_), channel_id=1, source_target_pairs={{0,1},{1,0},{2,3},{3,2},{4,5},{5,4},{6,7},{7,6},{8,9},{9,8},{10,11... | collective-permute-start | bytes 282632 | tf_op jit(solution)/shard_map/ppermute | solution.py:365
  25.4 1.8 %collective-permute-start.9 = (bf16[64,2880]{1,0:T(8,128)(2,1)S(1)}, bf16[64,2880]{1,0:T(8,128)(2,1)S(1)}, u32[]{:S(2)}, u32[]{:S(2)}) collective-permute-start(bf16[64,2880]{1,0:T(8,128)(2,1)S(1)} %get-tuple-element.40), channel_id=1, source_target_pairs={{0,1},{1,0},{2,3},{3,2},{4,5},{5,4},{6,7},{7,6},{8,9},{9,8},{10,11... | collective-permute-start | bytes 1105928 | tf_op jit(solution)/shard_map/ppermute | solution.py:365
  27.3 5.0 %collective-permute-start.10 = (bf16[16,2880]{1,0:T(8,128)(2,1)S(1)}, bf16[16,2880]{1,0:T(8,128)(2,1)S(1)}, u32[]{:S(2)}, u32[]{:S(2)}) collective-permute-start(bf16[16,2880]{1,0:T(8,128)(2,1)S(1)} %get-tuple-element.42), channel_id=1, source_target_pairs={{0,2},{1,3},{2,0},{3,1},{4,6},{5,7},{6,4},{7,5},{8,10},{9,11},{10,... | collective-permute-start | bytes 276488 | tf_op jit(solution)/shard_map/ppermute | solution.py:410
  28.3 7.7 %collective-permute-start.12 = (bf16[16,2880]{1,0:T(8,128)(2,1)S(1)}, bf16[16,2880]{1,0:T(8,128)(2,1)S(1)}, u32[]{:S(2)}, u32[]{:S(2)}) collective-permute-start(bf16[16,2880]{1,0:T(8,128)(2,1)S(1)} %get-tuple-element.43), channel_id=1, source_target_pairs={{6,0},{5,1},{4,2},{7,3},{2,4},{1,5},{0,6},{3,7},{14,8},{13,9},{12,... | collective-permute-start | bytes 276488 | tf_op jit(solution)/shard_map/ppermute | solution.py:412
  30.1 5.9 %collective-permute-start.13 = (bf16[16,2880]{1,0:T(8,128)(2,1)S(1)}, bf16[16,2880]{1,0:T(8,128)(2,1)S(1)}, u32[]{:S(2)}, u32[]{:S(2)}) collective-permute-start(bf16[16,2880]{1,0:T(8,128)(2,1)S(1)} %get-tuple-element.44), channel_id=1, source_target_pairs={{0,0},{3,1},{2,2},{1,3},{4,4},{7,5},{6,6},{5,7},{8,8},{11,9},{10,1... | collective-permute-start | bytes 276488 | tf_op jit(solution)/shard_map/ppermute | solution.py:412
  32.4 6.4 %collective-permute-start.11 = (bf16[16,2880]{1,0:T(8,128)(2,1)S(1)}, bf16[16,2880]{1,0:T(8,128)(2,1)S(1)}, u32[]{:S(2)}, u32[]{:S(2)}) collective-permute-start(bf16[16,2880]{1,0:T(8,128)(2,1)S(1)} %merge.1), channel_id=1, source_target_pairs={{12,0},{9,1},{14,2},{11,3},{8,4},{13,5},{10,6},{15,7},{4,8},{1,9},... | collective-permute-start | bytes 276488 | tf_op jit(solution)/shard_map/ppermute | solution.py:416
  38.8 1.6 %collective-permute-start.14 = (f32[16,2880]{1,0:T(8,128)S(1)}, f32[16,2880]{1,0:T(8,128)S(1)}, u32[]{:S(2)}, u32[]{:S(2)}) collective-permute-start(f32[16,2880]{1,0:T(8,128)S(1)} %convert_add_fusion.mine_ref), channel_id=1, source_target_pairs={{0,1},{1,0},{2,3},{3,2},{4,5},{5,4},{6,7},{7,6},{8,9},{9,8},{10,11... | collective-permute-start | bytes 552968 | tf_op jit(solution)/shard_map/ppermute | solution.py:365
